TPU v7x, 32 devices: a whole 2x2x4 slice. The times are simulated.
32 devices in a mesh: pipe: 2 (over x), dp: 4 (over y, core), tensor: 4 (over z).
Axes of the slice: x: 2, y: 2, z: 4, core: 2. Of those that a mesh axis runs over, the one named last changes fastest.
Arguments:
- x_vit: bfloat16 [8, 576, 1024], P('dp', 'tensor'), may hold values from -6 to 6
- x_conv: bfloat16 [8, 1024, 1536], P('dp', None, 'tensor'), may hold values from -12 to 12
- positions: int32 [8, 576], P('dp'), may hold values from 0 to 575, each once within a row
- valid: int32 [8, 576], P('dp'), may hold values from 0 to 1, as said below
- qkv_weight: bfloat16 [2, 1024, 3, 1024], P('pipe', None, None, 'tensor'), may hold values from -0.1875 to 0.1875
- attn_weight: bfloat16 [2, 1024, 1024], P('pipe', 'tensor'), may hold values from -1 to 1
- fc_in: bfloat16 [2, 1024, 4096], P('pipe', None, 'tensor'), may hold values from -0.1875 to 0.1875
- fc_out: bfloat16 [2, 4096, 1024], P('pipe', 'tensor'), may hold values from -0.09375 to 0.09375
- vit_gains: float32 [2, 2, 1024], P('pipe'), may hold values from 0.5 to 1.5
- vit_shifts: float32 [2, 2, 1024], P('pipe'), may hold values from -3 to 3
- pw_in: bfloat16 [2, 1536, 6144], P('pipe', None, 'tensor'), may hold values from -0.15625 to 0.15625
- pw_out: bfloat16 [2, 6144, 1536], P('pipe', 'tensor'), may hold values from -0.078125 to 0.078125
- dw_kernel: float32 [2, 49, 1536], P('pipe', None, 'tensor'), may hold values from -0.875 to 0.875
- conv_gains: float32 [2, 2, 1536], P('pipe', None, 'tensor'), may hold values from 0.5 to 1.5
- conv_shift: float32 [2, 1536], P('pipe', 'tensor'), may hold values from -3 to 3
- proj_weight: bfloat16 [2, 1536, 1024], P('pipe'), may hold values from -0.15625 to 0.15625
- taps: float32 [2, 9, 1024], P('pipe'), may hold values from -2 to 2
- gate: float32 [2, 1024], P('pipe'), may hold values from -2 to 2
- dy_vit: bfloat16 [8, 576, 1024], P('dp', 'tensor'), may hold values from -6 to 6
- dy_conv: bfloat16 [8, 1024, 1536], P('dp', None, 'tensor'), may hold values from -6 to 6
Outputs:
- out_vit: bfloat16 [2, 8, 576, 1024], P('pipe', 'dp', 'tensor')
- out_conv: bfloat16 [2, 8, 1024, 1536], P('pipe', 'dp', None, 'tensor')
- grad_vit: float32 [2, 8, 576, 1024], P('pipe', 'dp', 'tensor')
- grad_conv: float32 [2, 8, 1024, 1536], P('pipe', 'dp', None, 'tensor')
- rms_vit: float32 [2, 8, 576], P('pipe', 'dp', 'tensor')
- rms_conv: float32 [2, 8, 1024], P('pipe', 'dp')
- grad_qkv: float32 [2, 1024, 3, 1024], P('pipe', 'dp', None, 'tensor')
- grad_attn: float32 [2, 1024, 1024], P('pipe', 'tensor', 'dp')
- grad_fc_in: float32 [2, 1024, 4096], P('pipe', 'dp', 'tensor')
- grad_fc_out: float32 [2, 4096, 1024], P('pipe', 'tensor', 'dp')
- grad_vit_gains: float32 [2, 2, 1024], P('pipe')
- grad_vit_shifts: float32 [2, 2, 1024], P('pipe')
- grad_pw_in: float32 [2, 1536, 6144], P('pipe', 'dp', 'tensor')
- grad_pw_out: float32 [2, 6144, 1536], P('pipe', 'tensor', 'dp')
- grad_dw: float32 [2, 49, 1536], P('pipe', None, 'tensor')
- grad_conv_gains: float32 [2, 2, 1536], P('pipe', None, 'tensor')
- grad_conv_shift: float32 [2, 1536], P('pipe', 'tensor')
- grad_proj: float32 [2, 1536, 1024], P('pipe', 'dp', 'tensor')
- grad_taps: float32 [2, 9, 1024], P('pipe')
- grad_gate: float32 [2, 1024], P('pipe')
Inputs may be any that keep to these rules, and one draw needn't show every extreme that they name: Each row of positions names every one of the 576 grid cells once. The valid tokens of each image are a prefix of 288 tokens or more; in every draw some image has all 576 valid.
All inputs are finite; a program needn't handle non-finite values.
Results may differ from a plain program's by a relative error of at most 0.025.
Values may be sent and summed in bfloat16 or wider, within the bound.
No kernel may reach another device: no remote copies, remote signals or barrier semaphores. Data moves between devices by JAX's collectives and lax.ppermute only.
A program may use at most 320 MiB of HBM per device.

v0:
```python
import math

import jax
import jax.numpy as jnp
from jax import lax
from jax.sharding import PartitionSpec as P

HEAD_DIM = 64
MICRO = 2


def for_sending(array):
    return jax.tree.map(lambda a: a.astype(jnp.bfloat16) if a.dtype == jnp.float32 else a, array)


def shifted(array, axis, by):
    devices = lax.axis_size(axis)
    pairs = [(i, i + by) for i in range(devices) if 0 <= i + by < devices]
    return lax.ppermute(array, axis, pairs)


def gelu_exact(values):
    return jax.nn.gelu(values, approximate=False)


def gelu_slope(values):
    cumulative = 0.5 * (1.0 + lax.erf(values * (1.0 / math.sqrt(2.0))))
    density = jnp.exp(-0.5 * values * values) * (1.0 / math.sqrt(2.0 * math.pi))
    return cumulative + values * density


def pool_matrix(coarse, fine):
    row_index = jnp.arange(coarse)[:, None]
    col_index = jnp.arange(fine)[None, :]
    starts = row_index * fine // coarse
    stops = -(-(row_index + 1) * fine // coarse)
    inside = (col_index >= starts) & (col_index < stops)
    return jnp.where(inside, 1.0 / (stops - starts).astype(jnp.float32), 0.0)


def depthwise(grid, kernel, side_taps):
    half_side = side_taps // 2
    extent = grid.shape[1]
    padded = jnp.pad(grid, ((0, 0), (half_side, half_side), (half_side, half_side), (0, 0)))
    summed = jnp.zeros(grid.shape, jnp.float32)
    for row_tap in range(side_taps):
        for col_tap in range(side_taps):
            summed = (
                summed
                + padded[:, row_tap : row_tap + extent, col_tap : col_tap + extent, :]
                * kernel[row_tap * side_taps + col_tap]
            )
    return summed


def depthwise_taps(grid, upstream, side_taps):
    half_side = side_taps // 2
    extent = grid.shape[1]
    padded = jnp.pad(grid, ((0, 0), (half_side, half_side), (half_side, half_side), (0, 0)))
    rows_out = []
    for row_tap in range(side_taps):
        for col_tap in range(side_taps):
            window = padded[:, row_tap : row_tap + extent, col_tap : col_tap + extent, :]
            rows_out.append(jnp.sum(window * upstream, axis=(0, 1, 2)))
    return jnp.stack(rows_out, 0)


def norm_rows(values, epsilon):
    centred = values - jnp.mean(values, -1, keepdims=True)
    inverse = lax.rsqrt(jnp.mean(centred * centred, -1, keepdims=True) + epsilon)
    return (centred * inverse, inverse)


def norm_back(upstream, scaled, inverse, gains):
    weighted = upstream * gains
    return inverse * (
        weighted
        - jnp.mean(weighted, -1, keepdims=True)
        - scaled * jnp.mean(weighted * scaled, -1, keepdims=True)
    )


def inner(left, right):
    leading = tuple(range(left.ndim - 1))
    return lax.dot_general(
        left, right, ((leading, leading), ((), ())), preferred_element_type=jnp.float32
    )


def along(left, right):
    return lax.dot_general(
        left, right, (((left.ndim - 1,), (1,)), ((), ())), preferred_element_type=jnp.float32
    )


def own_block(values, count, axis):
    return lax.dynamic_slice_in_dim(values, lax.axis_index("tensor") * count, count, axis)


def widen(values, whole, axis):
    shape = list(values.shape)
    shape[axis] = whole
    empty = jnp.zeros(tuple(shape), jnp.float32)
    return lax.dynamic_update_slice_in_dim(
        empty, values, lax.axis_index("tensor") * values.shape[axis], axis
    )


def gather_tokens(values):
    return lax.all_gather(values, "tensor", axis=1, tiled=True)


def scatter_tokens(values):
    return lax.psum_scatter(
        values.astype(jnp.bfloat16), "tensor", scatter_dimension=1, tiled=True
    ).astype(jnp.float32)


def gather_channels(values):
    return lax.all_gather(values, "tensor", axis=1, tiled=True)


def scatter_channels(values):
    return lax.psum_scatter(
        values.astype(jnp.bfloat16), "tensor", scatter_dimension=1, tiled=True
    ).astype(jnp.float32)


def channel_total(first_part, second_part):
    return lax.psum((first_part, second_part), "tensor")


def attention_scores(query, keys_all, key_mask, score_scale):
    scores = (
        jnp.einsum("bqhd,bkhd->bhqk", query, keys_all, preferred_element_type=jnp.float32)
        * score_scale
    )
    return jnp.where(key_mask[:, None, None, :] > 0, scores, -1000000000.0)


def reduce_grads(parts):
    return (
        lax.psum_scatter(
            parts[0].astype(jnp.bfloat16), "dp", scatter_dimension=0, tiled=True
        ).astype(jnp.float32),
        lax.psum_scatter(
            parts[1].astype(jnp.bfloat16), "dp", scatter_dimension=1, tiled=True
        ).astype(jnp.float32),
        lax.psum_scatter(
            parts[2].astype(jnp.bfloat16), "dp", scatter_dimension=0, tiled=True
        ).astype(jnp.float32),
        lax.psum_scatter(
            parts[3].astype(jnp.bfloat16), "dp", scatter_dimension=1, tiled=True
        ).astype(jnp.float32),
        lax.psum_scatter(
            parts[4].astype(jnp.bfloat16), "dp", scatter_dimension=0, tiled=True
        ).astype(jnp.float32),
        lax.psum_scatter(
            parts[5].astype(jnp.bfloat16), "dp", scatter_dimension=1, tiled=True
        ).astype(jnp.float32),
        lax.psum_scatter(
            parts[6].astype(jnp.bfloat16), "dp", scatter_dimension=0, tiled=True
        ).astype(jnp.float32),
    )


def section_forward(stream, feature, places, key_mask, params):
    (
        qkv_w,
        attn_w,
        fc_in_w,
        fc_out_w,
        vit_gain,
        vit_shift,
        pw_in_w,
        pw_out_w,
        dw_w,
        conv_gain,
        conv_shift_w,
        proj_w,
        taps_w,
        gate_w,
    ) = params
    images, local_tokens, model_width = stream.shape
    conv_cells, local_channels = (feature.shape[1], feature.shape[2])
    conv_side = math.isqrt(conv_cells)
    tokens = local_tokens * lax.axis_size("tensor")
    vit_side = math.isqrt(tokens)
    channels = local_channels * lax.axis_size("tensor")
    local_width = attn_w.shape[0]
    heads_here = local_width // HEAD_DIM
    score_scale = HEAD_DIM ** (-0.5)
    feature_grid = feature.reshape(images, conv_side, conv_side, local_channels)
    mixed = depthwise(feature_grid, dw_w, 7).reshape(images * conv_cells, local_channels)
    first_sum, second_sum = channel_total(jnp.sum(mixed, -1), jnp.sum(mixed * mixed, -1))
    centre = first_sum / channels
    inverse = lax.rsqrt(second_sum / channels - centre * centre + 1e-06)
    scaled = (mixed - centre[:, None]) * inverse[:, None]
    normed_full = gather_channels((scaled * conv_gain[0] + conv_shift_w).astype(jnp.bfloat16))
    expand = jnp.dot(normed_full, pw_in_w, preferred_element_type=jnp.float32)
    hidden = gelu_exact(expand).astype(jnp.bfloat16)
    branch = scatter_channels(jnp.dot(hidden, pw_out_w, preferred_element_type=jnp.float32))
    feature_out = feature.reshape(images * conv_cells, local_channels) + conv_gain[1] * branch
    pooling = pool_matrix(vit_side, conv_side)
    pooled = jnp.einsum(
        "ai,bj,nijc->nabc",
        pooling,
        pooling,
        feature_out.reshape(images, conv_side, conv_side, local_channels),
        precision=lax.Precision.HIGHEST,
    )
    pooled_full = lax.all_gather(
        pooled.reshape(images * tokens, local_channels).astype(jnp.bfloat16),
        "tensor",
        axis=1,
        tiled=True,
    )
    proj_cols = own_block(proj_w, local_width, 1)
    taps_cols = own_block(taps_w, local_width, 1)
    gate_cols = own_block(gate_w, local_width, 0)
    adapted = jnp.dot(pooled_full, proj_cols, preferred_element_type=jnp.float32).reshape(
        images, vit_side, vit_side, local_width
    )
    spread = depthwise(adapted, taps_cols, 3).reshape(images, tokens, local_width)
    picked = jnp.tanh(gate_cols) * jnp.take_along_axis(spread, places[:, :, None], axis=1)
    moved = lax.all_to_all(
        picked.astype(jnp.bfloat16), "tensor", split_axis=1, concat_axis=2, tiled=True
    ).astype(picked.dtype)
    stream_in = stream + moved
    scaled_a, inverse_a = norm_rows(stream_in, 1e-05)
    normed_a = gather_tokens((scaled_a * vit_gain[0] + vit_shift[0]).astype(jnp.bfloat16))
    project = jnp.dot(
        normed_a, qkv_w.reshape(model_width, 3 * local_width), preferred_element_type=jnp.float32
    )
    project = project.astype(jnp.bfloat16).reshape(images, tokens, 3, heads_here, HEAD_DIM)
    query = project[:, :, 0]
    keys_all = project[:, :, 1]
    values_all = project[:, :, 2]
    scores = attention_scores(query, keys_all, key_mask, score_scale)
    highest = jnp.max(scores, -1, keepdims=True)
    raised = jnp.exp(scores - highest)
    totals = jnp.sum(raised, -1, keepdims=True)
    probs = (raised / totals).astype(jnp.bfloat16)
    log_total = highest + jnp.log(totals)
    attended = jnp.einsum("bhqk,bkhd->bqhd", probs, values_all, preferred_element_type=jnp.float32)
    attended = attended.astype(jnp.bfloat16).reshape(images, tokens, local_width)
    stream_mid = stream_in + scatter_tokens(
        jnp.dot(attended, attn_w, preferred_element_type=jnp.float32)
    )
    scaled_b, inverse_b = norm_rows(stream_mid, 1e-05)
    normed_b = gather_tokens((scaled_b * vit_gain[1] + vit_shift[1]).astype(jnp.bfloat16))
    expand_b = jnp.dot(normed_b, fc_in_w, preferred_element_type=jnp.float32)
    hidden_b = gelu_exact(expand_b).astype(jnp.bfloat16)
    stream_out = stream_mid + scatter_tokens(
        jnp.dot(hidden_b, fc_out_w, preferred_element_type=jnp.float32)
    )
    vit_measure = jnp.sqrt(jnp.mean(stream_out * stream_out, -1))
    conv_rows = feature_out.reshape(images, conv_cells, local_channels)
    conv_square = lax.psum(jnp.sum(conv_rows * conv_rows, -1), "tensor")
    conv_measure = jnp.sqrt(conv_square / channels)
    kept_values = dict(
        feature=feature_grid,
        scaled=scaled,
        inverse=inverse,
        normed_full=normed_full,
        expand=expand,
        hidden=hidden,
        branch=branch,
        pooled_full=pooled_full,
        adapted=adapted,
        spread=spread,
        places=places,
        key_mask=key_mask,
        scaled_a=scaled_a,
        inverse_a=inverse_a,
        normed_a=normed_a,
        query=query,
        keys_all=keys_all,
        values_all=values_all,
        log_total=log_total,
        attended=attended,
        scaled_b=scaled_b,
        inverse_b=inverse_b,
        normed_b=normed_b,
        expand_b=expand_b,
        hidden_b=hidden_b,
    )
    return (stream_out, conv_rows, (vit_measure, conv_measure), kept_values)


def section_backward(grad_stream, grad_feature, kept_values, params):
    (
        qkv_w,
        attn_w,
        fc_in_w,
        fc_out_w,
        vit_gain,
        vit_shift,
        pw_in_w,
        pw_out_w,
        dw_w,
        conv_gain,
        conv_shift_w,
        proj_w,
        taps_w,
        gate_w,
    ) = params
    images, local_tokens, model_width = grad_stream.shape
    conv_cells, local_channels = (grad_feature.shape[1], grad_feature.shape[2])
    conv_side = math.isqrt(conv_cells)
    tokens = local_tokens * lax.axis_size("tensor")
    vit_side = math.isqrt(tokens)
    channels = local_channels * lax.axis_size("tensor")
    local_width = attn_w.shape[0]
    heads_here = local_width // HEAD_DIM
    score_scale = HEAD_DIM ** (-0.5)
    grad_full = gather_tokens(grad_stream.astype(jnp.bfloat16))
    grad_fc_out = inner(kept_values["hidden_b"], grad_full)
    grad_expand_b = (along(grad_full, fc_out_w) * gelu_slope(kept_values["expand_b"])).astype(
        jnp.bfloat16
    )
    grad_fc_in = inner(kept_values["normed_b"], grad_expand_b)
    grad_normed_b = scatter_tokens(along(grad_expand_b, fc_in_w))
    gain_second = jnp.sum(grad_normed_b * kept_values["scaled_b"], axis=(0, 1))
    shift_second = jnp.sum(grad_normed_b, axis=(0, 1))
    grad_mid = grad_stream + norm_back(
        grad_normed_b, kept_values["scaled_b"], kept_values["inverse_b"], vit_gain[1]
    )
    grad_mid_full = gather_tokens(grad_mid.astype(jnp.bfloat16))
    grad_attn = inner(kept_values["attended"], grad_mid_full)
    grad_attended = (
        along(grad_mid_full, attn_w)
        .astype(jnp.bfloat16)
        .reshape(images, tokens, heads_here, HEAD_DIM)
    )
    query = kept_values["query"]
    keys_all = kept_values["keys_all"]
    scores = attention_scores(query, keys_all, kept_values["key_mask"], score_scale)
    exact = jnp.exp(scores - kept_values["log_total"])
    rounded = exact.astype(jnp.bfloat16)
    grad_values = jnp.einsum(
        "bhqk,bqhd->bkhd", rounded, grad_attended, preferred_element_type=jnp.float32
    )
    grad_probs = jnp.einsum(
        "bqhd,bkhd->bhqk",
        grad_attended,
        kept_values["values_all"],
        preferred_element_type=jnp.float32,
    )
    grad_scores = (exact * (grad_probs - jnp.sum(grad_probs * exact, -1, keepdims=True))).astype(
        jnp.bfloat16
    )
    grad_query = (
        jnp.einsum("bhqk,bkhd->bqhd", grad_scores, keys_all, preferred_element_type=jnp.float32)
        * score_scale
    )
    grad_keys = (
        jnp.einsum("bhqk,bqhd->bkhd", grad_scores, query, preferred_element_type=jnp.float32)
        * score_scale
    )
    grad_project = (
        jnp.stack([grad_query, grad_keys, grad_values], 2)
        .astype(jnp.bfloat16)
        .reshape(images, tokens, 3 * local_width)
    )
    grad_qkv = inner(kept_values["normed_a"], grad_project).reshape(model_width, 3, local_width)
    grad_normed_a = scatter_tokens(along(grad_project, qkv_w.reshape(model_width, 3 * local_width)))
    gain_first = jnp.sum(grad_normed_a * kept_values["scaled_a"], axis=(0, 1))
    shift_first = jnp.sum(grad_normed_a, axis=(0, 1))
    grad_in = grad_mid + norm_back(
        grad_normed_a, kept_values["scaled_a"], kept_values["inverse_a"], vit_gain[0]
    )
    grad_cols = lax.all_to_all(
        for_sending(grad_in), "tensor", split_axis=2, concat_axis=1, tiled=True
    ).astype(grad_in.dtype)
    order = jnp.argsort(kept_values["places"], axis=1)
    grad_placed = jnp.take_along_axis(grad_cols, order[:, :, None], axis=1)
    proj_cols = own_block(proj_w, local_width, 1)
    taps_cols = own_block(taps_w, local_width, 1)
    gate_value = jnp.tanh(own_block(gate_w, local_width, 0))
    grad_gate = jnp.sum(grad_placed * kept_values["spread"], axis=(0, 1)) * (
        1.0 - gate_value * gate_value
    )
    grad_spread = (grad_placed * gate_value).reshape(images, vit_side, vit_side, local_width)
    grad_taps = depthwise_taps(kept_values["adapted"], grad_spread, 3)
    grad_adapted = (
        depthwise(grad_spread, taps_cols[::-1], 3)
        .reshape(images * tokens, local_width)
        .astype(jnp.bfloat16)
    )
    grad_proj = inner(kept_values["pooled_full"], grad_adapted)
    grad_pooled = lax.psum_scatter(
        along(grad_adapted, proj_cols).astype(jnp.bfloat16),
        "tensor",
        scatter_dimension=1,
        tiled=True,
    ).astype(jnp.float32)
    grad_pooled = grad_pooled.reshape(images, vit_side, vit_side, local_channels)
    pooling = pool_matrix(vit_side, conv_side)
    unpooled = jnp.einsum(
        "ai,bj,nabc->nijc", pooling, pooling, grad_pooled, precision=lax.Precision.HIGHEST
    )
    grad_out_rows = (
        grad_feature.reshape(images, conv_side, conv_side, local_channels) + unpooled
    ).reshape(images * conv_cells, local_channels)
    grad_scale = jnp.sum(grad_out_rows * kept_values["branch"], 0)
    grad_branch = gather_channels((grad_out_rows * conv_gain[1]).astype(jnp.bfloat16))
    grad_pw_out = inner(kept_values["hidden"], grad_branch)
    grad_expand = (along(grad_branch, pw_out_w) * gelu_slope(kept_values["expand"])).astype(
        jnp.bfloat16
    )
    grad_pw_in = inner(kept_values["normed_full"], grad_expand)
    grad_normed = scatter_channels(along(grad_expand, pw_in_w))
    scaled = kept_values["scaled"]
    grad_gain = jnp.sum(grad_normed * scaled, 0)
    grad_shift = jnp.sum(grad_normed, 0)
    weighted = grad_normed * conv_gain[0]
    first_sum, second_sum = channel_total(jnp.sum(weighted, -1), jnp.sum(weighted * scaled, -1))
    grad_mixed = kept_values["inverse"][:, None] * (
        weighted - first_sum[:, None] / channels - scaled * (second_sum[:, None] / channels)
    )
    grad_grid = grad_mixed.reshape(images, conv_side, conv_side, local_channels)
    grad_dw = depthwise_taps(kept_values["feature"], grad_grid, 7)
    grad_feature_in = grad_out_rows + depthwise(grad_grid, dw_w[::-1], 7).reshape(
        images * conv_cells, local_channels
    )
    large_parts = (grad_qkv, grad_attn, grad_fc_in, grad_fc_out, grad_pw_in, grad_pw_out, grad_proj)
    small_parts = (grad_dw, jnp.stack([grad_gain, grad_scale]), grad_shift, grad_taps, grad_gate)
    norm_parts = (jnp.stack([gain_first, gain_second]), jnp.stack([shift_first, shift_second]))
    return (
        grad_in,
        grad_feature_in.reshape(images, conv_cells, local_channels),
        large_parts,
        small_parts,
        norm_parts,
    )


def body(
    x_vit,
    x_conv,
    positions,
    valid,
    qkv_weight,
    attn_weight,
    fc_in,
    fc_out,
    vit_gains,
    vit_shifts,
    pw_in,
    pw_out,
    dw_kernel,
    conv_gains,
    conv_shift,
    proj_weight,
    taps,
    gate,
    dy_vit,
    dy_conv,
):
    params = tuple(
        (
            argument[0]
            for argument in (
                qkv_weight,
                attn_weight,
                fc_in,
                fc_out,
                vit_gains,
                vit_shifts,
                pw_in,
                pw_out,
                dw_kernel,
                conv_gains,
                conv_shift,
                proj_weight,
                taps,
                gate,
            )
        )
    )
    first_section = lax.axis_index("pipe") == 0
    per_micro = x_vit.shape[0] // MICRO

    def select(former, latter):
        return jnp.where(first_section, former, latter)

    def portion(source, which_one):
        return source[which_one * per_micro : (which_one + 1) * per_micro]

    received = (
        jnp.zeros(portion(x_vit, 0).shape, jnp.bfloat16),
        jnp.zeros(portion(x_conv, 0).shape, jnp.bfloat16),
    )
    forward_out = []
    kept_list = []
    for step_index in range(MICRO + 1):
        first_index = min(step_index, MICRO - 1)
        second_index = max(step_index - 1, 0)
        stream = select(portion(x_vit, first_index), received[0]).astype(jnp.float32)
        feature = select(portion(x_conv, first_index), received[1]).astype(jnp.float32)
        places = select(portion(positions, first_index), portion(positions, second_index))
        key_mask = select(portion(valid, first_index), portion(valid, second_index))
        stream_out, feature_out, measure, kept_values = section_forward(
            stream, feature, places, key_mask, params
        )
        outgoing = (stream_out.astype(jnp.bfloat16), feature_out.astype(jnp.bfloat16))
        forward_out.append((outgoing[0], outgoing[1], measure[0], measure[1]))
        kept_list.append(kept_values)
        if step_index < MICRO:
            received = shifted((outgoing[0], outgoing[1]), "pipe", 1)
    returned = (
        jnp.zeros(portion(x_vit, 0).shape, jnp.bfloat16),
        jnp.zeros(portion(x_conv, 0).shape, jnp.bfloat16),
    )
    grads_in = []
    large_total = None
    small_total = None
    norm_total = None
    for step_index in range(MICRO + 1):
        second_index = min(step_index, MICRO - 1)
        kept_values = jax.tree.map(
            select, kept_list[max(step_index - 1, 0)], kept_list[min(step_index + 1, MICRO)]
        )
        grad_stream = select(returned[0], portion(dy_vit, second_index)).astype(jnp.float32)
        grad_feature = select(returned[1], portion(dy_conv, second_index)).astype(jnp.float32)
        grad_stream_in, grad_feature_in, large_parts, small_parts, norm_parts = section_backward(
            grad_stream, grad_feature, kept_values, params
        )
        useful = select(step_index >= 1, step_index <= MICRO - 1)
        large_parts = tuple((jnp.where(useful, member, 0.0) for member in large_parts))
        small_parts = tuple((jnp.where(useful, member, 0.0) for member in small_parts))
        norm_parts = tuple((jnp.where(useful, member, 0.0) for member in norm_parts))
        grads_in.append((grad_stream_in, grad_feature_in))
        if step_index < MICRO:
            returned = shifted(
                (grad_stream_in.astype(jnp.bfloat16), grad_feature_in.astype(jnp.bfloat16)),
                "pipe",
                -1,
            )
        large_parts = reduce_grads(large_parts)
        if large_total is None:
            large_total = large_parts
            small_total = small_parts
            norm_total = norm_parts
        else:
            large_total = tuple(
                (former + latter for former, latter in zip(large_total, large_parts))
            )
            small_total = tuple(
                (former + latter for former, latter in zip(small_total, small_parts))
            )
            norm_total = tuple((former + latter for former, latter in zip(norm_total, norm_parts)))
    local_channels = small_total[2].shape[0]
    channels = local_channels * lax.axis_size("tensor")
    model_width = norm_total[0].shape[1]
    summed = lax.psum(
        (
            widen(small_total[0], channels, 1),
            widen(small_total[1], channels, 1),
            widen(small_total[2], channels, 0),
            widen(small_total[3], model_width, 1),
            widen(small_total[4], model_width, 0),
            norm_total[0],
            norm_total[1],
        ),
        ("dp", "tensor"),
    )
    grad_dw = own_block(summed[0], local_channels, 1)
    grad_conv_gain = own_block(summed[1], local_channels, 1)
    grad_conv_shift = own_block(summed[2], local_channels, 0)
    out_vit = jnp.concatenate(
        [
            select(forward_out[micro_index][0], forward_out[micro_index + 1][0])
            for micro_index in range(MICRO)
        ],
        0,
    )[None]
    out_conv = jnp.concatenate(
        [
            select(forward_out[micro_index][1], forward_out[micro_index + 1][1])
            for micro_index in range(MICRO)
        ],
        0,
    )[None]
    rms_vit = jnp.concatenate(
        [
            select(forward_out[micro_index][2], forward_out[micro_index + 1][2])
            for micro_index in range(MICRO)
        ],
        0,
    )[None]
    rms_conv = jnp.concatenate(
        [
            select(forward_out[micro_index][3], forward_out[micro_index + 1][3])
            for micro_index in range(MICRO)
        ],
        0,
    )[None]
    grad_vit = jnp.concatenate(
        [
            select(grads_in[micro_index + 1][0], grads_in[micro_index][0])
            for micro_index in range(MICRO)
        ],
        0,
    )[None]
    grad_conv = jnp.concatenate(
        [
            select(grads_in[micro_index + 1][1], grads_in[micro_index][1])
            for micro_index in range(MICRO)
        ],
        0,
    )[None]
    return (
        out_vit,
        out_conv,
        grad_vit,
        grad_conv,
        rms_vit,
        rms_conv,
        large_total[0][None],
        large_total[1][None],
        large_total[2][None],
        large_total[3][None],
        summed[5][None],
        summed[6][None],
        large_total[4][None],
        large_total[5][None],
        grad_dw[None],
        grad_conv_gain[None],
        grad_conv_shift[None],
        large_total[6][None],
        summed[3][None],
        summed[4][None],
    )


def solution(mesh):
    return jax.shard_map(
        body,
        mesh=mesh,
        in_specs=(
            P("dp", "tensor", None),
            P("dp", None, "tensor"),
            P("dp", None),
            P("dp", None),
            P("pipe", None, None, "tensor"),
            P("pipe", "tensor", None),
            P("pipe", None, "tensor"),
            P("pipe", "tensor", None),
            P("pipe", None, None),
            P("pipe", None, None),
            P("pipe", None, "tensor"),
            P("pipe", "tensor", None),
            P("pipe", None, "tensor"),
            P("pipe", None, "tensor"),
            P("pipe", "tensor"),
            P("pipe", None, None),
            P("pipe", None, None),
            P("pipe", None),
            P("dp", "tensor", None),
            P("dp", None, "tensor"),
        ),
        out_specs=(
            P("pipe", "dp", "tensor", None),
            P("pipe", "dp", None, "tensor"),
            P("pipe", "dp", "tensor", None),
            P("pipe", "dp", None, "tensor"),
            P("pipe", "dp", "tensor"),
            P("pipe", "dp", None),
            P("pipe", "dp", None, "tensor"),
            P("pipe", "tensor", "dp"),
            P("pipe", "dp", "tensor"),
            P("pipe", "tensor", "dp"),
            P("pipe", None, None),
            P("pipe", None, None),
            P("pipe", "dp", "tensor"),
            P("pipe", "tensor", "dp"),
            P("pipe", None, "tensor"),
            P("pipe", None, "tensor"),
            P("pipe", "tensor"),
            P("pipe", "dp", "tensor"),
            P("pipe", None, None),
            P("pipe", None),
        ),
        check_vma=False,
    )
```

profile of v0, /device:TPU:0, one launch (start us, length us, event | category | flops | bytes accessed | tf_op | source)
XLA Modules:
  0.0 3415.6 jit_solution(4850756155609427240)
XLA Ops:
  45.8 61.6 %all-gather.22.cloned.1.call-done = bf16[1024,1536]{1,0:T(8,128)(2,1)} async-done(((bf16[1024,384]{1,0:T(8,128)(2,1)}), bf16[1024,1536]{1,0:T(8,128)(2,1)}) %all-gather.22.cloned.1.call-update) | async-done | bytes 3145744 | tf_op jit(solution)/shard_map/all_gather | solution.py:120
  145.5 59.0 %reduce-scatter.127.cloned.1.call-done = bf16[384,1024]{1,0:T(8,128)(2,1)} async-done(((bf16[1536,1024]{1,0:T(8,128)(2,1)}), bf16[384,1024]{1,0:T(8,128)(2,1)}) %reduce-scatter.127.cloned.1.call-update) | async-done | bytes 786448
  259.8 62.5 %all-gather.30.cloned.1.call-done = bf16[1024,1536]{1,0:T(8,128)(2,1)} async-done(((bf16[1024,384]{1,0:T(8,128)(2,1)}), bf16[1024,1536]{1,0:T(8,128)(2,1)}) %all-gather.30.cloned.1.call-update) | async-done | bytes 3145744 | tf_op jit(solution)/shard_map/all_gather | solution.py:120
  365.8 53.4 %reduce-scatter.129.cloned.1.call-done = bf16[384,1024]{1,0:T(8,128)(2,1)} async-done(((bf16[1536,1024]{1,0:T(8,128)(2,1)}), bf16[384,1024]{1,0:T(8,128)(2,1)}) %reduce-scatter.129.cloned.1.call-update) | async-done | bytes 786448
  430.7 31.1 all-gather.24.cloned.1.call-done
  464.8 38.5 %all-gather.32.cloned.1.call-done = bf16[576,1536]{1,0:T(8,128)(2,1)} async-done(((bf16[576,384]{1,0:T(8,128)(2,1)}), bf16[576,1536]{1,0:T(8,128)(2,1)}) %all-gather.32.cloned.1.call-update) | async-done | bytes 1769488 | tf_op jit(solution)/shard_map/all_gather | solution.py:212
  589.1 28.4 reduce-scatter.67.cloned.1.call-done
  620.8 29.0 all-gather.28.cloned.1.call-done
  711.2 30.8 all-gather.34.cloned.1.call-done
  886.9 30.7 reduce-scatter.73.cloned.1.call-done
  971.4 28.4 reduce-scatter.81.cloned.1.call-done
  1051.5 40.8 %reduce-scatter.133.cloned.1.call-done = bf16[384,576]{1,0:T(8,128)(2,1)} async-done(((bf16[1536,576]{1,0:T(8,128)(2,1)}), bf16[384,576]{1,0:T(8,128)(2,1)}) %reduce-scatter.133.cloned.1.call-update) | async-done | bytes 442384
  1100.8 62.5 %all-gather.58.cloned.1.call-done = bf16[1024,1536]{1,0:T(8,128)(2,1)} async-done(((bf16[1024,384]{1,0:T(8,128)(2,1)}), bf16[1024,1536]{1,0:T(8,128)(2,1)}) %all-gather.58.cloned.1.call-update) | async-done | bytes 3145744 | tf_op jit(solution)/shard_map/all_gather | solution.py:120
  1276.4 61.6 %all-gather.38.cloned.1.call-done = bf16[1024,1536]{1,0:T(8,128)(2,1)} async-done(((bf16[1024,384]{1,0:T(8,128)(2,1)}), bf16[1024,1536]{1,0:T(8,128)(2,1)}) %all-gather.38.cloned.1.call-update) | async-done | bytes 3145744 | tf_op jit(solution)/shard_map/all_gather | solution.py:120
  1376.2 58.7 %reduce-scatter.131.cloned.1.call-done = bf16[384,1024]{1,0:T(8,128)(2,1)} async-done(((bf16[1536,1024]{1,0:T(8,128)(2,1)}), bf16[384,1024]{1,0:T(8,128)(2,1)}) %reduce-scatter.131.cloned.1.call-update) | async-done | bytes 786448
  1443.5 40.7 %all-gather.40.cloned.1.call-done = bf16[576,1536]{1,0:T(8,128)(2,1)} async-done(((bf16[576,384]{1,0:T(8,128)(2,1)}), bf16[576,1536]{1,0:T(8,128)(2,1)}) %all-gather.40.cloned.1.call-update) | async-done | bytes 1769488 | tf_op jit(solution)/shard_map/all_gather | solution.py:212
  1520.3 29.2 all-gather.42.cloned.1.call-done
  1693.4 30.7 reduce-scatter.77.cloned.1.call-done
  1777.5 28.4 reduce-scatter.85.cloned.1.call-done
  2092.0 63.6 %all-gather.60.cloned.1.call-done = bf16[1024,1536]{1,0:T(8,128)(2,1)} async-done(((bf16[1024,384]{1,0:T(8,128)(2,1)}), bf16[1024,1536]{1,0:T(8,128)(2,1)}) %all-gather.60.cloned.1.call-update) | async-done | bytes 3145744 | tf_op jit(solution)/shard_map/all_gather | solution.py:120
  2195.9 44.3 %reduce-scatter.139.cloned.1.call-done = bf16[384,1024]{1,0:T(8,128)(2,1)} async-done(((bf16[1536,1024]{1,0:T(8,128)(2,1)}), bf16[384,1024]{1,0:T(8,128)(2,1)}) %reduce-scatter.139.cloned.1.call-update) | async-done | bytes 786448
  2319.2 61.3 %all-gather.62.cloned.1.call-done = bf16[1024,1536]{1,0:T(8,128)(2,1)} async-done(((bf16[1024,384]{1,0:T(8,128)(2,1)}), bf16[1024,1536]{1,0:T(8,128)(2,1)}) %all-gather.62.cloned.1.call-update) | async-done | bytes 3145744 | tf_op jit(solution)/shard_map/all_gather | solution.py:120
  2824.5 30.9 reduce-scatter.93.cloned.1.call-done
  2855.4 30.7 reduce-scatter.95.cloned.1.call-done
  2965.7 48.3 %reduce-scatter.147.cloned.1.call-done = bf16[384,1536]{1,0:T(8,128)(2,1)} async-done(((bf16[1536,1536]{1,0:T(8,128)(2,1)}), bf16[384,1536]{1,0:T(8,128)(2,1)}) %reduce-scatter.147.cloned.1.call-update) | async-done | bytes 1179664
  3017.5 44.9 %fusion.815 = f32[1,32,32,384]{3,2,1,0:T(8,128)} fusion(f32[1,32,32,384]{3,2,1,0:T(8,128)} %get-tuple-element.343, f32[1,32,32,384]{3,2,1,0:T(8,128)} %copy-done.37, f32[1,32,32,384]{3,2,1,0:T(8,128)} %bitcast.1131, f32[384]{0:T(512)S(1)} %copy-done.148, f32[384]{0:T(512)S(1)} %copy-done.152, f32[384]{0:T(512)S(1)} %copy-done.160, f32[384]{0:T(512)S(1)} %copy-done.164, ...), kind=kLoop, calls=%fused_computation.1352 | loop fusion | flops 38928384 | bytes 6366721 | tf_op jit(solution)/shard_map/jit(_where)/select_n | solution.py:486
  3065.8 41.2 %all-reduce.29.cloned.1.call-done = (f32[1,2,1024]{2,1,0:T(2,128)}, f32[1,2,1024]{2,1,0:T(2,128)}, f32[2,1536]{1,0:T(2,128)}, f32[1536]{0:T(1024)}, f32[1,9,1024]{2,0,1:T(1,128)}, /*index=5*/f32[1,1024]{1,0:T(1,128)}) async-done(((f32[1,2,1024]{2,1,0:T(2,128)}, f32[1,2,1024]{2,1,0:T(2,128)}, f32[2,1536]{1,0:T(2,128)}, f32[1536]{0:T(1024)}, f32[1,9,1024]{2,0,1:T(1,128)}, /*index=5*/f32[1,1024]{1,0:T(1,128)}), ...) | async-done | bytes 75792 | tf_op jit(solution)/shard_map/psum | solution.py:557
  3109.6 90.7 %all-reduce.27.cloned.1.call-done = f32[49,1536]{1,0:T(8,128)} async-done(((f32[49,1536]{1,0:T(8,128)}), f32[49,1536]{1,0:T(8,128)}) %all-reduce.27.cloned.1.call-update) | async-done | bytes 301072 | tf_op jit(solution)/shard_map/psum | solution.py:557
  3201.8 49.7 %reduce-scatter.149.cloned.1.call-done = bf16[384,1536]{1,0:T(8,128)(2,1)} async-done(((bf16[1536,1536]{1,0:T(8,128)(2,1)}), bf16[384,1536]{1,0:T(8,128)(2,1)}) %reduce-scatter.149.cloned.1.call-update) | async-done | bytes 1179664
  3257.7 44.1 %reduce-scatter.115.cloned.1.call-done = bf16[384,1536]{1,0:T(8,128)(2,1)} async-done(((bf16[1536,1536]{1,0:T(8,128)(2,1)}), bf16[384,1536]{1,0:T(8,128)(2,1)}) %reduce-scatter.115.cloned.1.call-update) | async-done | bytes 1179664 | tf_op jit(solution)/shard_map/reduce_scatter | solution.py:155
  3301.8 50.5 %reduce-scatter.117.cloned.1.call-done = bf16[384,1536]{1,0:T(8,128)(2,1)} async-done(((bf16[1536,1536]{1,0:T(8,128)(2,1)}), bf16[384,1536]{1,0:T(8,128)(2,1)}) %reduce-scatter.117.cloned.1.call-update) | async-done | bytes 1179664 | tf_op jit(solution)/shard_map/reduce_scatter | solution.py:155
  3352.3 50.4 %reduce-scatter.119.cloned.1.call-done = bf16[384,1536]{1,0:T(8,128)(2,1)} async-done(((bf16[1536,1536]{1,0:T(8,128)(2,1)}), bf16[384,1536]{1,0:T(8,128)(2,1)}) %reduce-scatter.119.cloned.1.call-update) | async-done | bytes 1179664 | tf_op jit(solution)/shard_map/reduce_scatter | solution.py:155
  (1730 shorter events, 1937.2 us)
Async XLA Ops:
  45.8 158.7 %reduce-scatter.127.cloned.1.call-start = ((), (), s32[]{:S(2)}) async-start(), calls=%async_computation.100 | async-start | bytes 3932160
  145.5 176.8 %all-gather.30.cloned.1.call-start = ((), (), s32[]{:S(2)}) async-start(), calls=%async_computation.54 | async-start | bytes 3932160 | tf_op jit(solution)/shard_map/all_gather | solution.py:120
  259.7 159.5 %reduce-scatter.129.cloned.1.call-start = ((), (), s32[]{:S(2)}) async-start(), calls=%async_computation.101 | async-start | bytes 3932160
  1100.5 147.0 %reduce-scatter.135.cloned.1.call-start = ((), (), s32[]{:S(2)}) async-start(), calls=%async_computation.104 | async-start | bytes 3932160
  1188.6 149.4 %all-gather.38.cloned.1.call-start = ((), (), s32[]{:S(2)}) async-start(), calls=%async_computation.60 | async-start | bytes 3932160 | tf_op jit(solution)/shard_map/all_gather | solution.py:120
  1276.1 158.9 %reduce-scatter.131.cloned.1.call-start = ((), (), s32[]{:S(2)}) async-start(), calls=%async_computation.102 | async-start | bytes 3932160
  2092.0 148.2 %reduce-scatter.139.cloned.1.call-start = ((), (), s32[]{:S(2)}) async-start(), calls=%async_computation.106 | async-start | bytes 3932160
  2195.8 184.7 %all-gather.62.cloned.1.call-start = ((), (), s32[]{:S(2)}) async-start(), calls=%async_computation.80 | async-start | bytes 3932160 | tf_op jit(solution)/shard_map/all_gather | solution.py:120
  2319.2 234.4 %reduce-scatter.143.cloned.1.call-start = ((), (), s32[]{:S(2)}) async-start(), calls=%async_computation.108 | async-start | bytes 3932160
  2405.9 285.0 %reduce-scatter.145.cloned.1.call-start = ((), (), s32[]{:S(2)}) async-start(), calls=%async_computation.109 | async-start | bytes 5898240
  2421.7 278.5 %reduce-scatter.103.cloned.1.call-start = ((), (), s32[]{:S(2)}) async-start(), calls=%async_computation.87 | async-start | bytes 2621440 | tf_op jit(solution)/shard_map/reduce_scatter | solution.py:149
  2426.7 273.6 %reduce-scatter.105.cloned.1.call-start = ((), (), s32[]{:S(2)}) async-start(), calls=%async_computation.88 | async-start | bytes 2621440 | tf_op jit(solution)/shard_map/reduce_scatter | solution.py:149
  2431.6 268.7 %reduce-scatter.107.cloned.1.call-start = ((), (), s32[]{:S(2)}) async-start(), calls=%async_computation.89 | async-start | bytes 2621440 | tf_op jit(solution)/shard_map/reduce_scatter | solution.py:149
  2437.0 265.9 %reduce-scatter.109.cloned.1.call-start = ((), (), s32[]{:S(2)}) async-start(), calls=%async_computation.90 | async-start | bytes 2621440 | tf_op jit(solution)/shard_map/reduce_scatter | solution.py:152
  2441.9 261.0 %reduce-scatter.111.cloned.1.call-start = ((), (), s32[]{:S(2)}) async-start(), calls=%async_computation.91 | async-start | bytes 2621440 | tf_op jit(solution)/shard_map/reduce_scatter | solution.py:152
  2446.8 273.8 %reduce-scatter.113.cloned.1.call-start = ((), (), s32[]{:S(2)}) async-start(), calls=%async_computation.92 | async-start | bytes 2621440 | tf_op jit(solution)/shard_map/reduce_scatter | solution.py:152
  2451.8 293.1 %reduce-scatter.97.cloned.1.call-start = ((), (), s32[]{:S(2)}) async-start(), calls=%async_computation.84 | async-start | bytes 655360 | tf_op jit(solution)/shard_map/reduce_scatter | solution.py:146
  2454.6 314.3 %reduce-scatter.99.cloned.1.call-start = ((), (), s32[]{:S(2)}) async-start(), calls=%async_computation.85 | async-start | bytes 655360 | tf_op jit(solution)/shard_map/reduce_scatter | solution.py:146
  2457.4 336.5 %reduce-scatter.101.cloned.1.call-start = ((), (), s32[]{:S(2)}) async-start(), calls=%async_computation.86 | async-start | bytes 655360 | tf_op jit(solution)/shard_map/reduce_scatter | solution.py:146
  2460.2 364.3 %reduce-scatter.91.cloned.1.call-start = ((), (), s32[]{:S(2)}) async-start(), calls=%async_computation.81 | async-start | bytes 1966080 | tf_op jit(solution)/shard_map/reduce_scatter | solution.py:143
  2464.6 390.8 %reduce-scatter.93.cloned.1.call-start = ((), (), s32[]{:S(2)}) async-start(), calls=%async_computation.82 | async-start | bytes 1966080 | tf_op jit(solution)/shard_map/reduce_scatter | solution.py:143
  2468.9 417.2 %reduce-scatter.95.cloned.1.call-start = ((), (), s32[]{:S(2)}) async-start(), calls=%async_computation.83 | async-start | bytes 1966080 | tf_op jit(solution)/shard_map/reduce_scatter | solution.py:143
  2473.5 438.6 %reduce-scatter.121.cloned.1.call-start = ((), (), s32[]{:S(2)}) async-start(), calls=%async_computation.97 | async-start | bytes 983040 | tf_op jit(solution)/shard_map/reduce_scatter | solution.py:161
  2478.2 459.7 %reduce-scatter.123.cloned.1.call-start = ((), (), s32[]{:S(2)}) async-start(), calls=%async_computation.98 | async-start | bytes 983040 | tf_op jit(solution)/shard_map/reduce_scatter | solution.py:161
  2481.8 482.0 %reduce-scatter.125.cloned.1.call-start = ((), (), s32[]{:S(2)}) async-start(), calls=%async_computation.99 | async-start | bytes 983040 | tf_op jit(solution)/shard_map/reduce_scatter | solution.py:161
  2485.2 528.9 %reduce-scatter.147.cloned.1.call-start = ((), (), s32[]{:S(2)}) async-start(), calls=%async_computation.110 | async-start | bytes 5898240
  2501.9 605.0 %all-reduce.29.cloned.1.call-start = ((), (), s32[]{:S(2)}) async-start(), calls=%async_computation.112 | async-start | bytes 155648 | tf_op jit(solution)/shard_map/psum | solution.py:557
  2624.5 575.8 %all-reduce.27.cloned.1.call-start = ((), (), s32[]{:S(2)}) async-start(), calls=%async_computation.96 | async-start | bytes 688128 | tf_op jit(solution)/shard_map/psum | solution.py:557
  2646.5 605.0 %reduce-scatter.149.cloned.1.call-start = ((), (), s32[]{:S(2)}) async-start(), calls=%async_computation.111 | async-start | bytes 5898240
  2662.7 639.1 %reduce-scatter.115.cloned.1.call-start = ((), (), s32[]{:S(2)}) async-start(), calls=%async_computation.93 | async-start | bytes 5898240 | tf_op jit(solution)/shard_map/reduce_scatter | solution.py:155
  2672.3 680.0 %reduce-scatter.117.cloned.1.call-start = ((), (), s32[]{:S(2)}) async-start(), calls=%async_computation.94 | async-start | bytes 5898240 | tf_op jit(solution)/shard_map/reduce_scatter | solution.py:155
  2681.5 721.2 %reduce-scatter.119.cloned.1.call-start = ((), (), s32[]{:S(2)}) async-start(), calls=%async_computation.95 | async-start | bytes 5898240 | tf_op jit(solution)/shard_map/reduce_scatter | solution.py:155
  (547 other events, 26845.6 us)
Sparse Core Ops, SparseCore 0:
  45.9 61.5 all-gather.21
  145.6 58.8 reduce-scatter.126
  259.8 62.4 all-gather.29
  360.4 58.8 reduce-scatter.128
  421.3 40.5 all-gather.23
  463.9 39.3 all-gather.31
  662.3 33.0 reduce-scatter.68
  1049.5 42.7 reduce-scatter.132
  1100.7 62.5 all-gather.57
  1188.7 58.8 reduce-scatter.134
  1276.2 61.7 all-gather.37
  1376.1 58.8 reduce-scatter.130
  1443.6 40.5 all-gather.39
  2025.6 42.5 reduce-scatter.136
  2092.1 63.4 all-gather.59
  2181.3 58.8 reduce-scatter.138
  2243.1 41.7 reduce-scatter.140
  2319.3 61.1 all-gather.61
  2406.0 58.8 reduce-scatter.142
  2467.3 47.8 reduce-scatter.144
  2518.4 31.4 reduce-scatter.102
  2552.9 31.4 reduce-scatter.104
  2621.3 31.4 reduce-scatter.108
  2655.3 31.3 reduce-scatter.110
  2689.1 31.4 reduce-scatter.112
  2966.2 47.8 reduce-scatter.146
  3020.1 86.8 all-reduce.28
  3110.4 89.8 all-reduce.26
  3202.9 48.5 reduce-scatter.148
  3253.9 47.8 reduce-scatter.114
  3304.4 47.8 reduce-scatter.116
  3354.8 47.8 reduce-scatter.118
  (33 shorter events, 914.0 us)
where the time goes:
time: 3430 us; the launch traced here: 3420 us
  waiting for transfers between devices  2100 us (61%)
  matrix products  454 us (13%)
  other arithmetic  412 us (12%)
  local copies, waits for them, and re-layouts  305 us (9%)
  blocking collectives  71.4 us (2%)
  starting transfers between devices  49.8 us (1%)
    unnamed x77, waiting for transfers between devices  376 us
    all_gather x6, waiting for transfers between devices, gather_channels(): return lax.all_gather(values, 'tensor', axis=1, tiled=True)  373 us
    reduce_scatter x12, waiting for transfers between devices, scatter_tokens(): lax.psum_scatter(values.astype(jnp.bfloat16), 'tensor', scatter_dimension...  314 us
    all_gather x12, waiting for transfers between devices, gather_tokens(): return lax.all_gather(values, 'tensor', axis=1, tiled=True)  305 us
    unnamed x1042, local copies, waits for them, and re-layouts  153 us
    reduce_scatter x3, waiting for transfers between devices, reduce_grads(): lax.psum_scatter(parts[4].astype(jnp.bfloat16), 'dp', scatter_dimension=0...  145 us
    psum x2, waiting for transfers between devices, body(): lax.psum((widen(small_total[0], channels, 1), widen(small_total[1], chann...  132 us
    dot_general x21, matrix products, inner(): lax.dot_general(left, right, ((leading, leading), ((), ())), preferred_el...  117 us
  transfers between devices with their start and end apart: 79, of which 65 were waited for; matrix products, arithmetic and copies ran while one was open for 18% of the time, Pallas kernels for 0%

commit v1 on v0

--- a/solution.py
+++ b/solution.py
@@ -6,36 +6,82 @@
 from jax.sharding import PartitionSpec as P
 
 HEAD_DIM = 64
-MICRO = 2
 
 
 def for_sending(array):
     return jax.tree.map(lambda a: a.astype(jnp.bfloat16) if a.dtype == jnp.float32 else a, array)
 
 
-def shifted(array, axis, by):
-    devices = lax.axis_size(axis)
-    pairs = [(i, i + by) for i in range(devices) if 0 <= i + by < devices]
-    return lax.ppermute(array, axis, pairs)
-
-
-def gelu_exact(values):
-    return jax.nn.gelu(values, approximate=False)
-
-
-def gelu_slope(values):
+def traded(array, axis, bit):
+    return lax.ppermute(array, axis, [(i, i ^ bit) for i in range(lax.axis_size(axis))])
+
+
+def bits_of(axis):
+    return [1 << k for k in range((lax.axis_size(axis) - 1).bit_length())]
+
+
+def total_over(values, axis):
+    for bit in bits_of(axis):
+        values = values + traded(values, axis, bit)
+    return values
+
+
+def layer_pair(own):
+    flat = own.reshape((2, own.shape[0] // 2) + own.shape[1:])
+    odd = lax.axis_index("dp") % 2
+    sent = lax.dynamic_index_in_dim(flat, odd, 0, keepdims=False)
+    got = traded(sent, "pipe", 1)
+    rest = traded(got, "dp", 1)
+    first_half = jnp.where(odd == 0, got, rest)
+    second_half = jnp.where(odd == 0, rest, got)
+    other = jnp.concatenate([first_half, second_half], 0)
+    first = lax.axis_index("pipe") == 0
+    return (jnp.where(first, own, other), jnp.where(first, other, own))
+
+
+def gelu_and_slope(values):
     cumulative = 0.5 * (1.0 + lax.erf(values * (1.0 / math.sqrt(2.0))))
     density = jnp.exp(-0.5 * values * values) * (1.0 / math.sqrt(2.0 * math.pi))
-    return cumulative + values * density
-
-
-def pool_matrix(coarse, fine):
-    row_index = jnp.arange(coarse)[:, None]
-    col_index = jnp.arange(fine)[None, :]
-    starts = row_index * fine // coarse
-    stops = -(-(row_index + 1) * fine // coarse)
-    inside = (col_index >= starts) & (col_index < stops)
-    return jnp.where(inside, 1.0 / (stops - starts).astype(jnp.float32), 0.0)
+    return (
+        (values * cumulative).astype(jnp.bfloat16),
+        (cumulative + values * density).astype(jnp.bfloat16),
+    )
+
+
+def windows(coarse, fine):
+    starts = [row * fine // coarse for row in range(coarse)]
+    stops = [-(-(row + 1) * fine // coarse) for row in range(coarse)]
+    return (starts, stops)
+
+
+def pool_axis(grid, axis, coarse):
+    starts, stops = windows(coarse, grid.shape[axis])
+    slabs = []
+    for start, stop in zip(starts, stops):
+        slab = lax.slice_in_dim(grid, start, stop, axis=axis)
+        slabs.append(jnp.sum(slab, axis=axis, keepdims=True) * (1.0 / (stop - start)))
+    return jnp.concatenate(slabs, axis)
+
+
+def unpool_axis(grid, axis, fine):
+    starts, stops = windows(grid.shape[axis], fine)
+    slabs = []
+    for place in range(fine):
+        parts = [
+            lax.slice_in_dim(grid, row, row + 1, axis=axis) * (1.0 / (stop - start))
+            for row, (start, stop) in enumerate(zip(starts, stops))
+            if start <= place < stop
+        ]
+        slabs.append(sum(parts[1:], parts[0]))
+    return jnp.concatenate(slabs, axis)
+
+
+def pool(grid, coarse):
+    return pool_axis(pool_axis(grid, 1, coarse), 2, coarse)
+
+
+def unpool(grid, fine):
+    return unpool_axis(unpool_axis(grid, 2, fine), 1, fine)
 
 
 def depthwise(grid, kernel, side_taps):
@@ -127,7 +173,8 @@
 
 
 def channel_total(first_part, second_part):
-    return lax.psum((first_part, second_part), "tensor")
+    both = total_over(jnp.stack([first_part, second_part]), "tensor")
+    return (both[0], both[1])
 
 
 def attention_scores(query, keys_all, key_mask, score_scale):
@@ -136,32 +183,6 @@
         * score_scale
     )
     return jnp.where(key_mask[:, None, None, :] > 0, scores, -1000000000.0)
-
-
-def reduce_grads(parts):
-    return (
-        lax.psum_scatter(
-            parts[0].astype(jnp.bfloat16), "dp", scatter_dimension=0, tiled=True
-        ).astype(jnp.float32),
-        lax.psum_scatter(
-            parts[1].astype(jnp.bfloat16), "dp", scatter_dimension=1, tiled=True
-        ).astype(jnp.float32),
-        lax.psum_scatter(
-            parts[2].astype(jnp.bfloat16), "dp", scatter_dimension=0, tiled=True
-        ).astype(jnp.float32),
-        lax.psum_scatter(
-            parts[3].astype(jnp.bfloat16), "dp", scatter_dimension=1, tiled=True
-        ).astype(jnp.float32),
-        lax.psum_scatter(
-            parts[4].astype(jnp.bfloat16), "dp", scatter_dimension=0, tiled=True
-        ).astype(jnp.float32),
-        lax.psum_scatter(
-            parts[5].astype(jnp.bfloat16), "dp", scatter_dimension=1, tiled=True
-        ).astype(jnp.float32),
-        lax.psum_scatter(
-            parts[6].astype(jnp.bfloat16), "dp", scatter_dimension=0, tiled=True
-        ).astype(jnp.float32),
-    )
 
 
 def section_forward(stream, feature, places, key_mask, params):
@@ -198,26 +219,19 @@
     scaled = (mixed - centre[:, None]) * inverse[:, None]
     normed_full = gather_channels((scaled * conv_gain[0] + conv_shift_w).astype(jnp.bfloat16))
     expand = jnp.dot(normed_full, pw_in_w, preferred_element_type=jnp.float32)
-    hidden = gelu_exact(expand).astype(jnp.bfloat16)
+    hidden, slope = gelu_and_slope(expand)
     branch = scatter_channels(jnp.dot(hidden, pw_out_w, preferred_element_type=jnp.float32))
     feature_out = feature.reshape(images * conv_cells, local_channels) + conv_gain[1] * branch
-    pooling = pool_matrix(vit_side, conv_side)
-    pooled = jnp.einsum(
-        "ai,bj,nijc->nabc",
-        pooling,
-        pooling,
-        feature_out.reshape(images, conv_side, conv_side, local_channels),
-        precision=lax.Precision.HIGHEST,
-    )
+    pooled = pool(feature_out.reshape(images, conv_side, conv_side, local_channels), vit_side)
     pooled_full = lax.all_gather(
         pooled.reshape(images * tokens, local_channels).astype(jnp.bfloat16),
         "tensor",
         axis=1,
         tiled=True,
     )
-    proj_cols = own_block(proj_w, local_width, 1)
-    taps_cols = own_block(taps_w, local_width, 1)
-    gate_cols = own_block(gate_w, local_width, 0)
+    proj_cols = proj_w
+    taps_cols = taps_w
+    gate_cols = gate_w
     adapted = jnp.dot(pooled_full, proj_cols, preferred_element_type=jnp.float32).reshape(
         images, vit_side, vit_side, local_width
     )
@@ -250,20 +264,20 @@
     scaled_b, inverse_b = norm_rows(stream_mid, 1e-05)
     normed_b = gather_tokens((scaled_b * vit_gain[1] + vit_shift[1]).astype(jnp.bfloat16))
     expand_b = jnp.dot(normed_b, fc_in_w, preferred_element_type=jnp.float32)
-    hidden_b = gelu_exact(expand_b).astype(jnp.bfloat16)
+    hidden_b, slope_b = gelu_and_slope(expand_b)
     stream_out = stream_mid + scatter_tokens(
         jnp.dot(hidden_b, fc_out_w, preferred_element_type=jnp.float32)
     )
     vit_measure = jnp.sqrt(jnp.mean(stream_out * stream_out, -1))
     conv_rows = feature_out.reshape(images, conv_cells, local_channels)
-    conv_square = lax.psum(jnp.sum(conv_rows * conv_rows, -1), "tensor")
+    conv_square = total_over(jnp.sum(conv_rows * conv_rows, -1), "tensor")
     conv_measure = jnp.sqrt(conv_square / channels)
     kept_values = dict(
         feature=feature_grid,
         scaled=scaled,
         inverse=inverse,
         normed_full=normed_full,
-        expand=expand,
+        slope=slope,
         hidden=hidden,
         branch=branch,
         pooled_full=pooled_full,
@@ -282,7 +296,7 @@
         scaled_b=scaled_b,
         inverse_b=inverse_b,
         normed_b=normed_b,
-        expand_b=expand_b,
+        slope_b=slope_b,
         hidden_b=hidden_b,
     )
     return (stream_out, conv_rows, (vit_measure, conv_measure), kept_values)
@@ -316,7 +330,7 @@
     score_scale = HEAD_DIM ** (-0.5)
     grad_full = gather_tokens(grad_stream.astype(jnp.bfloat16))
     grad_fc_out = inner(kept_values["hidden_b"], grad_full)
-    grad_expand_b = (along(grad_full, fc_out_w) * gelu_slope(kept_values["expand_b"])).astype(
+    grad_expand_b = (along(grad_full, fc_out_w) * kept_values["slope_b"].astype(jnp.float32)).astype(
         jnp.bfloat16
     )
     grad_fc_in = inner(kept_values["normed_b"], grad_expand_b)
@@ -375,9 +389,9 @@
     ).astype(grad_in.dtype)
     order = jnp.argsort(kept_values["places"], axis=1)
     grad_placed = jnp.take_along_axis(grad_cols, order[:, :, None], axis=1)
-    proj_cols = own_block(proj_w, local_width, 1)
-    taps_cols = own_block(taps_w, local_width, 1)
-    gate_value = jnp.tanh(own_block(gate_w, local_width, 0))
+    proj_cols = proj_w
+    taps_cols = taps_w
+    gate_value = jnp.tanh(gate_w)
     grad_gate = jnp.sum(grad_placed * kept_values["spread"], axis=(0, 1)) * (
         1.0 - gate_value * gate_value
     )
@@ -396,17 +410,14 @@
         tiled=True,
     ).astype(jnp.float32)
     grad_pooled = grad_pooled.reshape(images, vit_side, vit_side, local_channels)
-    pooling = pool_matrix(vit_side, conv_side)
-    unpooled = jnp.einsum(
-        "ai,bj,nabc->nijc", pooling, pooling, grad_pooled, precision=lax.Precision.HIGHEST
-    )
+    unpooled = unpool(grad_pooled, conv_side)
     grad_out_rows = (
         grad_feature.reshape(images, conv_side, conv_side, local_channels) + unpooled
     ).reshape(images * conv_cells, local_channels)
     grad_scale = jnp.sum(grad_out_rows * kept_values["branch"], 0)
     grad_branch = gather_channels((grad_out_rows * conv_gain[1]).astype(jnp.bfloat16))
     grad_pw_out = inner(kept_values["hidden"], grad_branch)
-    grad_expand = (along(grad_branch, pw_out_w) * gelu_slope(kept_values["expand"])).astype(
+    grad_expand = (along(grad_branch, pw_out_w) * kept_values["slope"].astype(jnp.float32)).astype(
         jnp.bfloat16
     )
     grad_pw_in = inner(kept_values["normed_full"], grad_expand)
@@ -425,7 +436,13 @@
         images * conv_cells, local_channels
     )
     large_parts = (grad_qkv, grad_attn, grad_fc_in, grad_fc_out, grad_pw_in, grad_pw_out, grad_proj)
-    small_parts = (grad_dw, jnp.stack([grad_gain, grad_scale]), grad_shift, grad_taps, grad_gate)
+    small_parts = (
+        grad_dw,
+        jnp.stack([grad_gain, grad_scale]),
+        grad_shift[None],
+        grad_taps,
+        grad_gate[None],
+    )
     norm_parts = (jnp.stack([gain_first, gain_second]), jnp.stack([shift_first, shift_second]))
     return (
         grad_in,
@@ -434,6 +451,24 @@
         small_parts,
         norm_parts,
     )
+
+
+def own_share(partial, axis, keep_layer):
+    count = lax.axis_size("dp")
+    index = lax.axis_index("dp")
+    shape = partial.shape
+    block = shape[axis] // count
+    blocks = partial.reshape(shape[:axis] + (count, block) + shape[axis + 1 :])
+    for bit in bits_of("dp"):
+        left = blocks.shape[axis] // 2
+        blocks = blocks.reshape(blocks.shape[:axis] + (left, 2) + blocks.shape[axis + 1 :])
+        mine = (index // bit) % 2
+        kept = lax.dynamic_index_in_dim(blocks, mine, axis + 1, keepdims=False)
+        sent = lax.dynamic_index_in_dim(blocks, 1 - mine, axis + 1, keepdims=False)
+        blocks = kept + traded(sent.astype(jnp.bfloat16), "dp", bit).astype(jnp.float32)
+    blocks = jnp.squeeze(blocks, axis)
+    arrived = lax.ppermute(blocks.astype(jnp.bfloat16), "pipe", [(1 - keep_layer, keep_layer)])
+    return blocks + arrived.astype(jnp.float32)
 
 
 def body(
@@ -458,159 +493,133 @@
     dy_vit,
     dy_conv,
 ):
-    params = tuple(
-        (
-            argument[0]
-            for argument in (
-                qkv_weight,
-                attn_weight,
-                fc_in,
-                fc_out,
-                vit_gains,
-                vit_shifts,
-                pw_in,
-                pw_out,
-                dw_kernel,
-                conv_gains,
-                conv_shift,
-                proj_weight,
-                taps,
-                gate,
+    pipe_index = lax.axis_index("pipe")
+    first_section = pipe_index == 0
+    here = x_vit.shape[0] // lax.axis_size("pipe")
+    local_width = attn_weight.shape[1]
+
+    def select(former, latter):
+        return jnp.where(first_section, former, latter)
+
+    def portion(source):
+        return lax.dynamic_slice_in_dim(source, pipe_index * here, here, 0)
+
+    weights = dict(
+        dw=dw_kernel[0],
+        gain=conv_gains[0],
+        shift=conv_shift,
+        pw_in=pw_in[0],
+        pw_out=pw_out[0],
+        proj=own_block(proj_weight[0], local_width, 1),
+        taps=own_block(taps[0], local_width, 1),
+        gate=own_block(gate, local_width, 1),
+        vit_gain=vit_gains[0],
+        vit_shift=vit_shifts[0],
+        qkv=qkv_weight[0],
+        attn=attn_weight[0],
+        fc_in=fc_in[0],
+        fc_out=fc_out[0],
+    )
+    small = ("dw", "gain", "shift", "taps", "gate", "vit_gain", "vit_shift")
+    swapped = {}
+    for name in small:
+        other = traded(weights[name], "pipe", 1)
+        swapped[name] = (select(weights[name], other), select(other, weights[name]))
+    for name in ("pw_in", "pw_out", "proj", "qkv", "attn", "fc_in", "fc_out"):
+        swapped[name] = layer_pair(weights[name])
+
+    def params_of(layer):
+        return tuple(
+            swapped[name][layer][0] if name in ("shift", "gate") else swapped[name][layer]
+            for name in (
+                "qkv",
+                "attn",
+                "fc_in",
+                "fc_out",
+                "vit_gain",
+                "vit_shift",
+                "pw_in",
+                "pw_out",
+                "dw",
+                "gain",
+                "shift",
+                "proj",
+                "taps",
+                "gate",
             )
         )
-    )
-    first_section = lax.axis_index("pipe") == 0
-    per_micro = x_vit.shape[0] // MICRO
-
-    def select(former, latter):
-        return jnp.where(first_section, former, latter)
-
-    def portion(source, which_one):
-        return source[which_one * per_micro : (which_one + 1) * per_micro]
-
-    received = (
-        jnp.zeros(portion(x_vit, 0).shape, jnp.bfloat16),
-        jnp.zeros(portion(x_conv, 0).shape, jnp.bfloat16),
-    )
-    forward_out = []
+
+    places = portion(positions)
+    key_mask = portion(valid)
+    stream = portion(x_vit)
+    feature = portion(x_conv)
+    outs = []
     kept_list = []
-    for step_index in range(MICRO + 1):
-        first_index = min(step_index, MICRO - 1)
-        second_index = max(step_index - 1, 0)
-        stream = select(portion(x_vit, first_index), received[0]).astype(jnp.float32)
-        feature = select(portion(x_conv, first_index), received[1]).astype(jnp.float32)
-        places = select(portion(positions, first_index), portion(positions, second_index))
-        key_mask = select(portion(valid, first_index), portion(valid, second_index))
+    for layer in range(2):
         stream_out, feature_out, measure, kept_values = section_forward(
-            stream, feature, places, key_mask, params
+            stream.astype(jnp.float32), feature.astype(jnp.float32), places, key_mask, params_of(layer)
         )
-        outgoing = (stream_out.astype(jnp.bfloat16), feature_out.astype(jnp.bfloat16))
-        forward_out.append((outgoing[0], outgoing[1], measure[0], measure[1]))
+        stream = stream_out.astype(jnp.bfloat16)
+        feature = feature_out.astype(jnp.bfloat16)
+        outs.append([stream, feature, measure[0], measure[1]])
         kept_list.append(kept_values)
-        if step_index < MICRO:
-            received = shifted((outgoing[0], outgoing[1]), "pipe", 1)
-    returned = (
-        jnp.zeros(portion(x_vit, 0).shape, jnp.bfloat16),
-        jnp.zeros(portion(x_conv, 0).shape, jnp.bfloat16),
-    )
-    grads_in = []
-    large_total = None
-    small_total = None
-    norm_total = None
-    for step_index in range(MICRO + 1):
-        second_index = min(step_index, MICRO - 1)
-        kept_values = jax.tree.map(
-            select, kept_list[max(step_index - 1, 0)], kept_list[min(step_index + 1, MICRO)]
+    grad_stream = portion(dy_vit)
+    grad_feature = portion(dy_conv)
+    large = [None, None]
+    small_sums = [None, None]
+    norm_sums = [None, None]
+    for layer in (1, 0):
+        grad_stream_in, grad_feature_in, large_parts, small_parts, norm_parts = section_backward(
+            grad_stream.astype(jnp.float32),
+            grad_feature.astype(jnp.float32),
+            kept_list[layer],
+            params_of(layer),
         )
-        grad_stream = select(returned[0], portion(dy_vit, second_index)).astype(jnp.float32)
-        grad_feature = select(returned[1], portion(dy_conv, second_index)).astype(jnp.float32)
-        grad_stream_in, grad_feature_in, large_parts, small_parts, norm_parts = section_backward(
-            grad_stream, grad_feature, kept_values, params
-        )
-        useful = select(step_index >= 1, step_index <= MICRO - 1)
-        large_parts = tuple((jnp.where(useful, member, 0.0) for member in large_parts))
-        small_parts = tuple((jnp.where(useful, member, 0.0) for member in small_parts))
-        norm_parts = tuple((jnp.where(useful, member, 0.0) for member in norm_parts))
-        grads_in.append((grad_stream_in, grad_feature_in))
-        if step_index < MICRO:
-            returned = shifted(
-                (grad_stream_in.astype(jnp.bfloat16), grad_feature_in.astype(jnp.bfloat16)),
-                "pipe",
-                -1,
+        grad_stream = grad_stream_in.astype(jnp.bfloat16)
+        grad_feature = grad_feature_in.astype(jnp.bfloat16)
+        outs[layer] += [grad_stream_in, grad_feature_in]
+        large[layer] = [
+            own_share(member, axis, layer)
+            for member, axis in zip(large_parts, (0, 1, 0, 1, 0, 1, 0))
+        ]
+        small_sums[layer] = small_parts
+        norm_sums[layer] = norm_parts
+
+    def over_images(pair):
+        kept = select(pair[0], pair[1])
+        sent = select(pair[1], pair[0])
+        return total_over(kept + traded(sent, "pipe", 1), "dp")
+
+    model_width = vit_gains.shape[2]
+    column_sums = over_images([jnp.concatenate([part[0], part[1], part[2]], 0) for part in small_sums])
+    token_sums = over_images(
+        [
+            jnp.concatenate(
+                [
+                    widen(part[3], model_width, 1),
+                    widen(part[4], model_width, 1),
+                    norm[0],
+                    norm[1],
+                ],
+                0,
             )
-        large_parts = reduce_grads(large_parts)
-        if large_total is None:
-            large_total = large_parts
-            small_total = small_parts
-            norm_total = norm_parts
-        else:
-            large_total = tuple(
-                (former + latter for former, latter in zip(large_total, large_parts))
-            )
-            small_total = tuple(
-                (former + latter for former, latter in zip(small_total, small_parts))
-            )
-            norm_total = tuple((former + latter for former, latter in zip(norm_total, norm_parts)))
-    local_channels = small_total[2].shape[0]
-    channels = local_channels * lax.axis_size("tensor")
-    model_width = norm_total[0].shape[1]
-    summed = lax.psum(
-        (
-            widen(small_total[0], channels, 1),
-            widen(small_total[1], channels, 1),
-            widen(small_total[2], channels, 0),
-            widen(small_total[3], model_width, 1),
-            widen(small_total[4], model_width, 0),
-            norm_total[0],
-            norm_total[1],
-        ),
-        ("dp", "tensor"),
-    )
-    grad_dw = own_block(summed[0], local_channels, 1)
-    grad_conv_gain = own_block(summed[1], local_channels, 1)
-    grad_conv_shift = own_block(summed[2], local_channels, 0)
-    out_vit = jnp.concatenate(
-        [
-            select(forward_out[micro_index][0], forward_out[micro_index + 1][0])
-            for micro_index in range(MICRO)
-        ],
-        0,
-    )[None]
-    out_conv = jnp.concatenate(
-        [
-            select(forward_out[micro_index][1], forward_out[micro_index + 1][1])
-            for micro_index in range(MICRO)
-        ],
-        0,
-    )[None]
-    rms_vit = jnp.concatenate(
-        [
-            select(forward_out[micro_index][2], forward_out[micro_index + 1][2])
-            for micro_index in range(MICRO)
-        ],
-        0,
-    )[None]
-    rms_conv = jnp.concatenate(
-        [
-            select(forward_out[micro_index][3], forward_out[micro_index + 1][3])
-            for micro_index in range(MICRO)
-        ],
-        0,
-    )[None]
-    grad_vit = jnp.concatenate(
-        [
-            select(grads_in[micro_index + 1][0], grads_in[micro_index][0])
-            for micro_index in range(MICRO)
-        ],
-        0,
-    )[None]
-    grad_conv = jnp.concatenate(
-        [
-            select(grads_in[micro_index + 1][1], grads_in[micro_index][1])
-            for micro_index in range(MICRO)
-        ],
-        0,
-    )[None]
+            for part, norm in zip(small_sums, norm_sums)
+        ]
+    )
+    token_sums = total_over(token_sums, "tensor")
+    large_own = [select(former, latter) for former, latter in zip(large[0], large[1])]
+    tap_count = dw_kernel.shape[1]
+    side = taps.shape[1]
+
+    def both_images(member):
+        mine, theirs = (select(outs[0][member], outs[1][member]), select(outs[1][member], outs[0][member]))
+        sent = theirs if member in (2, 3) else for_sending(theirs)
+        got = traded(sent, "pipe", 1).astype(mine.dtype)
+        return jnp.concatenate([select(mine, got), select(got, mine)], 0)[None]
+
+    out_vit, out_conv, rms_vit, rms_conv, grad_vit, grad_conv = (
+        both_images(member) for member in range(6)
+    )
     return (
         out_vit,
         out_conv,
@@ -618,20 +627,20 @@
         grad_conv,
         rms_vit,
         rms_conv,
-        large_total[0][None],
-        large_total[1][None],
-        large_total[2][None],
-        large_total[3][None],
-        summed[5][None],
-        summed[6][None],
-        large_total[4][None],
-        large_total[5][None],
-        grad_dw[None],
-        grad_conv_gain[None],
-        grad_conv_shift[None],
-        large_total[6][None],
-        summed[3][None],
-        summed[4][None],
+        large_own[0][None],
+        large_own[1][None],
+        large_own[2][None],
+        large_own[3][None],
+        token_sums[side + 1 : side + 3][None],
+        token_sums[side + 3 : side + 5][None],
+        large_own[4][None],
+        large_own[5][None],
+        column_sums[:tap_count][None],
+        column_sums[tap_count : tap_count + 2][None],
+        column_sums[tap_count + 2 :],
+        large_own[6][None],
+        token_sums[:side][None],
+        token_sums[side][None],
     )
 
 

time: 3430 us -> 1780 us (0.52)
  waiting for transfers between devices: 2100 us -> 730 us
  matrix products: 454 us -> 217 us
  starting transfers between devices: 49.8 us -> 123 us
  blocking collectives: 71.4 us -> 0 us
    reduce_scatter x18 -> x0, waiting for transfers between devices: 397 us -> none  [the longest x3 145 us: reduce_grads(): lax.psum_scatter(parts[4].astype(jnp.bfloat16), 'dp', scatter_dimension=0...]
    all_gather x6 -> x4, waiting for transfers between devices: 373 us -> 108 us  [gather_channels(): return lax.all_gather(values, 'tensor', axis=1, tiled=True)]
    unnamed x77 -> x34, waiting for transfers between devices: 376 us -> 115 us
    reduce_scatter x12 -> x8, waiting for transfers between devices: 314 us -> 115 us  [scatter_tokens(): lax.psum_scatter(values.astype(jnp.bfloat16), 'tensor', scatter_dimension...]
    all_gather x12 -> x8, waiting for transfers between devices: 305 us -> 131 us  [gather_tokens(): return lax.all_gather(values, 'tensor', axis=1, tiled=True)]
    psum x2 -> x0, waiting for transfers between devices: 132 us -> none  [body(): lax.psum((widen(small_total[0], channels, 1), widen(small_total[1], chann...]
    ppermute x8 -> x89, waiting for transfers between devices: 82.8 us -> 192 us  [the longest x75 174 us: traded(): lax.ppermute(array, axis, [(i, i ^ bit) for i in range(lax.axis_size(axis...]
    select_n x30 -> x17, other arithmetic: 93.5 us -> 4.65 us  [select(): return jnp.where(first_section, former, latter)]
  transfers between devices with their start and end apart: 79 -> 121, of which waited for: 65 -> 49; matrix products, arithmetic and copies ran while one was open for 18% -> 40% of each run, Pallas kernels for 0% -> 0%
where the time goes in v1:
time: 1780 us; the launch traced here: 1770 us
  waiting for transfers between devices  730 us (41%)
  other arithmetic  384 us (22%)
  local copies, waits for them, and re-layouts  289 us (16%)
  matrix products  217 us (12%)
  starting transfers between devices  123 us (7%)
  between operations  22.2 us (1%)
    ppermute x75, waiting for transfers between devices, traded(): lax.ppermute(array, axis, [(i, i ^ bit) for i in range(lax.axis_size(axis...  174 us
    all_gather x8, waiting for transfers between devices, gather_tokens(): return lax.all_gather(values, 'tensor', axis=1, tiled=True)  131 us
    unnamed x34, waiting for transfers between devices  115 us
    unnamed x819, local copies, waits for them, and re-layouts  115 us
    reduce_scatter x8, waiting for transfers between devices, scatter_tokens(): lax.psum_scatter(values.astype(jnp.bfloat16), 'tensor', scatter_dimension...  115 us
    all_gather x4, waiting for transfers between devices, gather_channels(): return lax.all_gather(values, 'tensor', axis=1, tiled=True)  108 us
    dot_general x14, matrix products, along(): lax.dot_general(left, right, (((left.ndim - 1,), (1,)), ((), ())), prefer...  70.6 us
    ppermute x75, starting transfers between devices, traded(): lax.ppermute(array, axis, [(i, i ^ bit) for i in range(lax.axis_size(axis...  66 us
  transfers between devices with their start and end apart: 121, of which 49 were waited for; matrix products, arithmetic and copies ran while one was open for 40% of the time, Pallas kernels for 0%

profile of v1, /device:TPU:0, one launch (start us, length us, event | category | flops | bytes accessed | tf_op | source)
XLA Modules:
  0.0 1765.9 jit_solution(17902588382790624264)
XLA Ops:
  24.5 45.8 %fusion.578 = (f32[32,32]{1,0:T(8,128)S(1)}, f32[32,32]{1,0:T(8,128)S(1)}, f32[1,32,32,384]{3,2,1,0:T(8,128)}) fusion(f32[384]{0:T(512)S(1)} %get-tuple-element.314, f32[384]{0:T(512)S(1)} %get-tuple-element.315, f32[384]{0:T(512)S(1)} %get-tuple-element.316, f32[384]{0:T(512)S(1)} %get-tuple-element.317, f32[384]{0:T(512)S(1)} %get-tuple-element.318, ...), kind=kLoop, calls=%fused_computation.1758 | loop fusion | flops 39319552 | bytes 3229184 | tf_op jit(solution)/shard_map/reduce_sum | solution.py:216
  83.1 36.6 %collective-permute-done.8 = bf16[768,1536]{1,0:T(8,128)(2,1)} collective-permute-done((bf16[768,1536]{1,0:T(8,128)(2,1)}, bf16[768,1536]{1,0:T(8,128)(2,1)}, u32[]{:S(2)}, u32[]{:S(2)}) %collective-permute-start.8) | collective-permute-done | bytes 2359328 | tf_op jit(solution)/shard_map/ppermute | solution.py:16
  129.5 16.8 all-gather.15.cloned.1.call-done
  146.3 10.7 multiply_convert_fusion.3
  173.7 57.8 %reduce-scatter.43.cloned.1.call-done = bf16[384,1024]{1,0:T(8,128)(2,1)} async-done(((bf16[1536,1024]{1,0:T(8,128)(2,1)}), bf16[384,1024]{1,0:T(8,128)(2,1)}) %reduce-scatter.43.cloned.1.call-update) | async-done | bytes 786448
  237.6 14.3 fusion.577
  285.9 40.0 %all-gather.23.cloned.1.call-done = bf16[1024,1536]{1,0:T(8,128)(2,1)} async-done(((bf16[1024,384]{1,0:T(8,128)(2,1)}), bf16[1024,1536]{1,0:T(8,128)(2,1)}) %all-gather.23.cloned.1.call-update) | async-done | bytes 3145744 | tf_op jit(solution)/shard_map/all_gather | solution.py:166
  325.9 10.6 multiply_convert_fusion.2
  361.7 49.2 %reduce-scatter.45.cloned.1.call-done = bf16[384,1024]{1,0:T(8,128)(2,1)} async-done(((bf16[1536,1024]{1,0:T(8,128)(2,1)}), bf16[384,1024]{1,0:T(8,128)(2,1)}) %reduce-scatter.45.cloned.1.call-update) | async-done | bytes 786448
  458.9 36.0 %all-gather.25.cloned.1.call-done = bf16[576,1536]{1,0:T(8,128)(2,1)} async-done(((bf16[576,384]{1,0:T(8,128)(2,1)}), bf16[576,1536]{1,0:T(8,128)(2,1)}) %all-gather.25.cloned.1.call-update) | async-done | bytes 1769488 | tf_op jit(solution)/shard_map/all_gather | solution.py:226
  508.4 9.2 all-to-all-done
  537.4 13.6 all-gather.19.cloned.1.call-done
  569.7 21.8 %reduce-scatter.27.cloned.1.call-done = bf16[1,144,1024]{2,1,0:T(8,128)(2,1)} async-done(((bf16[1,576,1024]{2,1,0:T(8,128)(2,1)}), bf16[1,144,1024]{2,1,0:T(8,128)(2,1)}) %reduce-scatter.27.cloned.1.call-update) | async-done | bytes 294928 | tf_op jit(solution)/shard_map/reduce_scatter | solution.py:160
  594.1 18.4 %collective-permute-done.21 = bf16[512,1024]{1,0:T(8,128)(2,1)} collective-permute-done((bf16[512,1024]{1,0:T(8,128)(2,1)}, bf16[512,1024]{1,0:T(8,128)(2,1)}, u32[]{:S(2)}, u32[]{:S(2)}) %collective-permute-start.21) | collective-permute-done | bytes 1048608 | tf_op jit(solution)/shard_map/ppermute | solution.py:16
  639.1 18.2 %all-to-all-done.1 = bf16[4,2,18432]{2,1,0:T(2,128)(2,1)S(1)} async-done(((bf16[4,2,18432]{2,1,0:T(2,128)(2,1)}), bf16[4,2,18432]{2,1,0:T(2,128)(2,1)S(1)}, u32[]{:S(2)}, u32[]{:S(2)}) %all-to-all-start.1) | async-done | bytes 294944 | tf_op jit(solution)/shard_map/all_to_all | solution.py:240
  667.7 29.7 %all-gather.27.cloned.1.call-done = bf16[1,576,1024]{2,1,0:T(8,128)(2,1)} async-done(((bf16[1,144,1024]{2,1,0:T(8,128)(2,1)}), bf16[1,576,1024]{2,1,0:T(8,128)(2,1)}) %all-gather.27.cloned.1.call-update) | async-done | bytes 1179664 | tf_op jit(solution)/shard_map/all_gather | solution.py:156
  707.8 28.4 %reduce-scatter.31.cloned.1.call-done = bf16[1,144,1024]{2,1,0:T(8,128)(2,1)} async-done(((bf16[1,576,1024]{2,1,0:T(8,128)(2,1)}), bf16[1,144,1024]{2,1,0:T(8,128)(2,1)}) %reduce-scatter.31.cloned.1.call-update) | async-done | bytes 294928 | tf_op jit(solution)/shard_map/reduce_scatter | solution.py:160
  740.2 27.5 %all-gather.29.cloned.1.call-done = bf16[1,576,1024]{2,1,0:T(8,128)(2,1)} async-done(((bf16[1,144,1024]{2,1,0:T(8,128)(2,1)}), bf16[1,576,1024]{2,1,0:T(8,128)(2,1)}) %all-gather.29.cloned.1.call-update) | async-done | bytes 1179664 | tf_op jit(solution)/shard_map/all_gather | solution.py:156
  773.0 25.8 %all-gather.31.cloned.1.call-done = bf16[1,576,1024]{2,1,0:T(8,128)(2,1)} async-done(((bf16[1,144,1024]{2,1,0:T(8,128)(2,1)}), bf16[1,576,1024]{2,1,0:T(8,128)(2,1)}) %all-gather.31.cloned.1.call-update) | async-done | bytes 1179664 | tf_op jit(solution)/shard_map/all_gather | solution.py:156
  811.8 24.4 %reduce-scatter.35.cloned.1.call-done = bf16[1,144,1024]{2,1,0:T(8,128)(2,1)} async-done(((bf16[1,576,1024]{2,1,0:T(8,128)(2,1)}), bf16[1,144,1024]{2,1,0:T(8,128)(2,1)}) %reduce-scatter.35.cloned.1.call-update) | async-done | bytes 294928 | tf_op jit(solution)/shard_map/reduce_scatter | solution.py:160
  836.2 30.1 %reduce-scatter.33.cloned.1.call-done = bf16[1,144,1024]{2,1,0:T(8,128)(2,1)} async-done(((bf16[1,576,1024]{2,1,0:T(8,128)(2,1)}), bf16[1,144,1024]{2,1,0:T(8,128)(2,1)}) %reduce-scatter.33.cloned.1.call-update) | async-done | bytes 294928 | tf_op jit(solution)/shard_map/reduce_scatter | solution.py:160
  870.7 29.2 %all-gather.33.cloned.1.call-done = bf16[1,576,1024]{2,1,0:T(8,128)(2,1)} async-done(((bf16[1,144,1024]{2,1,0:T(8,128)(2,1)}), bf16[1,576,1024]{2,1,0:T(8,128)(2,1)}) %all-gather.33.cloned.1.call-update) | async-done | bytes 1179664 | tf_op jit(solution)/shard_map/all_gather | solution.py:156
  1285.4 50.9 %all-gather.39.cloned.1.call-done = bf16[1024,1536]{1,0:T(8,128)(2,1)} async-done(((bf16[1024,384]{1,0:T(8,128)(2,1)}), bf16[1024,1536]{1,0:T(8,128)(2,1)}) %all-gather.39.cloned.1.call-update) | async-done | bytes 3145744 | tf_op jit(solution)/shard_map/all_gather | solution.py:166
  1336.3 12.0 multiply_convert_fusion.1
  1450.9 14.8 fusion.172
  1510.5 11.4 collective-permute-done.78
  1529.6 15.6 collective-permute-done.72
  1546.8 11.5 multiply_convert_fusion
  1647.0 20.2 %collective-permute-done.75 = bf16[1536,1,384]{2,0,1:T(8,128)(2,1)S(1)} collective-permute-done((bf16[1536,1,384]{2,0,1:T(8,128)(2,1)S(1)}, bf16[1536,1,384]{2,0,1:T(8,128)(2,1)S(1)}, u32[]{:S(2)}, u32[]{:S(2)}) %collective-permute-start.75) | collective-permute-done | bytes 1179680 | tf_op jit(solution)/shard_map/ppermute | solution.py:16
  1675.2 15.7 collective-permute-done.69
  1720.8 14.2 fusion.268
  1745.4 10.0 collective-permute-done.32
  (1714 shorter events, 973.4 us)
Async XLA Ops:
  7.2 139.1 %all-gather.15.cloned.1.call-start = ((), (), s32[]{:S(2)}) async-start(), calls=%async_computation.18 | async-start | bytes 3932160 | tf_op jit(solution)/shard_map/all_gather | solution.py:166
  18.3 101.4 %collective-permute-start.8 = (bf16[768,1536]{1,0:T(8,128)(2,1)}, bf16[768,1536]{1,0:T(8,128)(2,1)}, u32[]{:S(2)}, u32[]{:S(2)}) collective-permute-start(bf16[768,1536]{1,0:T(8,128)(2,1)} %dynamic-slice_bitcast_fusion), channel_id=1, source_target_pairs={{0,16},{16,0},{1,17},{17,1},{2,18},{18,2},{3,19},{19,3},{4,20},{20... | collective-permute-start | bytes 7077896 | tf_op jit(solution)/shard_map/ppermute | solution.py:16
  82.5 149.0 %reduce-scatter.43.cloned.1.call-start = ((), (), s32[]{:S(2)}) async-start(), calls=%async_computation.40 | async-start | bytes 3932160
  172.5 153.4 %all-gather.23.cloned.1.call-start = ((), (), s32[]{:S(2)}) async-start(), calls=%async_computation.24 | async-start | bytes 3932160 | tf_op jit(solution)/shard_map/all_gather | solution.py:166
  262.9 148.0 %reduce-scatter.45.cloned.1.call-start = ((), (), s32[]{:S(2)}) async-start(), calls=%async_computation.41 | async-start | bytes 3932160
  351.9 101.9 %all-gather.17.cloned.1.call-start = ((), (), s32[]{:S(2)}) async-start(), calls=%async_computation.19 | async-start | bytes 2211840 | tf_op jit(solution)/shard_map/all_gather | solution.py:226
  361.6 133.3 %all-gather.25.cloned.1.call-start = ((), (), s32[]{:S(2)}) async-start(), calls=%async_computation.25 | async-start | bytes 2211840 | tf_op jit(solution)/shard_map/all_gather | solution.py:226
  451.2 70.2 %collective-permute-start.15 = (bf16[512,3,256]{0,2,1:T(8,128)(2,1)}, bf16[512,3,256]{0,2,1:T(8,128)(2,1)}, u32[]{:S(2)}, u32[]{:S(2)}) collective-permute-start(bf16[512,3,256]{0,2,1:T(8,128)(2,1)} %bitcast.88), channel_id=1, source_target_pairs={{0,16},{16,0},{1,17},{17,1},{2,18},{18,2},{3,19},{19,3},{4,20},{20... | collective-permute-start | bytes 2359304 | tf_op jit(solution)/shard_map/ppermute | solution.py:16
  521.3 70.2 %reduce-scatter.27.cloned.1.call-start = ((), (), s32[]{:S(2)}) async-start(), calls=%async_computation.21 | async-start | bytes 1474560 | tf_op jit(solution)/shard_map/reduce_scatter | solution.py:160
  593.8 70.8 %reduce-scatter.29.cloned.1.call-start = ((), (), s32[]{:S(2)}) async-start(), calls=%async_computation.23 | async-start | bytes 1474560 | tf_op jit(solution)/shard_map/reduce_scatter | solution.py:160
  740.2 96.0 %reduce-scatter.35.cloned.1.call-start = ((), (), s32[]{:S(2)}) async-start(), calls=%async_computation.31 | async-start | bytes 1474560 | tf_op jit(solution)/shard_map/reduce_scatter | solution.py:160
  811.5 88.4 %all-gather.33.cloned.1.call-start = ((), (), s32[]{:S(2)}) async-start(), calls=%async_computation.32 | async-start | bytes 1474560 | tf_op jit(solution)/shard_map/all_gather | solution.py:156
  870.6 84.8 %reduce-scatter.37.cloned.1.call-start = ((), (), s32[]{:S(2)}) async-start(), calls=%async_computation.33 | async-start | bytes 1474560 | tf_op jit(solution)/shard_map/reduce_scatter | solution.py:160
  914.3 77.3 %all-gather.35.cloned.1.call-start = ((), (), s32[]{:S(2)}) async-start(), calls=%async_computation.34 | async-start | bytes 1474560 | tf_op jit(solution)/shard_map/all_gather | solution.py:156
  929.4 708.9 %collective-permute-start.35 = (f32[1,1024]{1,0:T(1,128)}, f32[1,1024]{1,0:T(1,128)}, u32[]{:S(2)}, u32[]{:S(2)}) collective-permute-start(f32[1,1024]{1,0:T(1,128)} %add.1821), channel_id=1, source_target_pairs={{0,2},{1,3},{2,0},{3,1},{4,6},{5,7},{6,4},{7,5},{8,10},{9,11},{10,... | collective-permute-start | bytes 12296 | tf_op jit(solution)/shard_map/ppermute | solution.py:16
  980.1 133.6 %collective-permute-start.62 = (bf16[1024,256]{1,0:T(8,128)(2,1)}, bf16[1024,256]{1,0:T(8,128)(2,1)}, u32[]{:S(2)}, u32[]{:S(2)}) collective-permute-start(bf16[1024,256]{1,0:T(8,128)(2,1)} %bitcast_convert_fusion.9), channel_id=1, source_target_pairs={{0,16},{1,17},{2,18},{3,19},{4,20},{5,21},{6,22},{7,23},{8,24},{9,... | collective-permute-start | bytes 1572872 | tf_op jit(solution)/shard_map/ppermute | solution.py:470
  985.2 135.5 %collective-permute-start.56 = (bf16[256,1024]{1,0:T(8,128)(2,1)}, bf16[256,1024]{1,0:T(8,128)(2,1)}, u32[]{:S(2)}, u32[]{:S(2)}) collective-permute-start(bf16[256,1024]{1,0:T(8,128)(2,1)} %bitcast_convert_fusion.11), channel_id=1, source_target_pairs={{0,16},{1,17},{2,18},{3,19},{4,20},{5,21},{6,22},{7,23},{8,24},{9,... | collective-permute-start | bytes 1572872 | tf_op jit(solution)/shard_map/ppermute | solution.py:470
  1000.6 84.4 %all-gather.37.cloned.1.call-start = ((), (), s32[]{:S(2)}) async-start(), calls=%async_computation.36 | async-start | bytes 1474560 | tf_op jit(solution)/shard_map/all_gather | solution.py:156
  1052.3 90.1 %reduce-scatter.41.cloned.1.call-start = ((), (), s32[]{:S(2)}) async-start(), calls=%async_computation.37 | async-start | bytes 1474560 | tf_op jit(solution)/shard_map/reduce_scatter | solution.py:160
  1106.0 86.9 %collective-permute-start.50 = (bf16[256,256]{1,0:T(8,128)(2,1)}, bf16[256,256]{1,0:T(8,128)(2,1)}, u32[]{:S(2)}, u32[]{:S(2)}) collective-permute-start(bf16[256,256]{1,0:T(8,128)(2,1)} %bitcast_convert_fusion.19), channel_id=1, source_target_pairs={{0,16},{1,17},{2,18},{3,19},{4,20},{5,21},{6,22},{7,23},{8,24},{9,... | collective-permute-start | bytes 393224 | tf_op jit(solution)/shard_map/ppermute | solution.py:470
  1113.7 85.3 %collective-permute-start.44 = (bf16[256,3,256]{2,0,1:T(8,128)(2,1)}, bf16[256,3,256]{2,0,1:T(8,128)(2,1)}, u32[]{:S(2)}, u32[]{:S(2)}) collective-permute-start(bf16[256,3,256]{2,0,1:T(8,128)(2,1)} %bitcast_convert_fusion.14), channel_id=1, source_target_pairs={{0,16},{1,17},{2,18},{3,19},{4,20},{5,21},{6,22},{7,23},{8,24},{9,... | collective-permute-start | bytes 1179656 | tf_op jit(solution)/shard_map/ppermute | solution.py:470
  1158.4 70.3 %reduce-scatter.47.cloned.1.call-start = ((), (), s32[]{:S(2)}) async-start(), calls=%async_computation.42 | async-start | bytes 2457600
  1186.8 87.5 %reduce-scatter.51.cloned.1.call-start = ((), (), s32[]{:S(2)}) async-start(), calls=%async_computation.44 | async-start | bytes 2457600
  1228.5 107.8 %all-gather.39.cloned.1.call-start = ((), (), s32[]{:S(2)}) async-start(), calls=%async_computation.38 | async-start | bytes 3932160 | tf_op jit(solution)/shard_map/all_gather | solution.py:166
  1246.8 176.1 %reduce-scatter.49.cloned.1.call-start = ((), (), s32[]{:S(2)}) async-start(), calls=%async_computation.43 | async-start | bytes 3932160
  1263.1 209.2 %collective-permute-start.86 = (bf16[2,384,256]{2,1,0:T(8,128)(2,1)}, bf16[2,384,256]{2,1,0:T(8,128)(2,1)}, u32[]{:S(2)}, u32[]{:S(2)}) collective-permute-start(bf16[2,384,256]{2,1,0:T(8,128)(2,1)} %fusion.452), channel_id=1, source_target_pairs={{0,4},{4,0},{8,12},{12,8},{1,5},{5,1},{9,13},{13,9},{2,6},{6,2},{1... | collective-permute-start | bytes 1179656 | tf_op jit(solution)/shard_map/ppermute | solution.py:16
  1272.8 203.1 %collective-permute-start.84 = (bf16[1,384,256]{2,1,0:T(8,128)(2,1)}, bf16[1,384,256]{2,1,0:T(8,128)(2,1)S(1)}, u32[]{:S(2)}, u32[]{:S(2)}) collective-permute-start(bf16[1,384,256]{2,1,0:T(8,128)(2,1)} %dynamic-slice_convert_fusion.17), channel_id=1, source_target_pairs={{0,8},{4,12},{8,0},{12,4},{1,9},{5,13},{9,1},{13,5},{2,10},{6,14},... | collective-permute-start | bytes 589832 | tf_op jit(solution)/shard_map/ppermute | solution.py:16
  1363.9 182.9 %all-gather.41.cloned.1.call-start = ((), (), s32[]{:S(2)}) async-start(), calls=%async_computation.39 | async-start | bytes 3932160 | tf_op jit(solution)/shard_map/all_gather | solution.py:166
  1415.1 74.2 %collective-permute-start.77 = (bf16[1536,2,384]{2,0,1:T(8,128)(2,1)}, bf16[1536,2,384]{2,0,1:T(8,128)(2,1)}, u32[]{:S(2)}, u32[]{:S(2)}) collective-permute-start(bf16[1536,2,384]{2,0,1:T(8,128)(2,1)} %bitcast.1345), channel_id=1, source_target_pairs={{0,4},{4,0},{8,12},{12,8},{1,5},{5,1},{9,13},{13,9},{2,6},{6,2},{1... | collective-permute-start | bytes 7077896 | tf_op jit(solution)/shard_map/ppermute | solution.py:16
  1472.2 199.6 %reduce-scatter.53.cloned.1.call-start = ((), (), s32[]{:S(2)}) async-start(), calls=%async_computation.45 | async-start | bytes 3932160
  1523.3 173.3 %collective-permute-start.79 = (bf16[1536,384]{1,0:T(8,128)(2,1)}, bf16[1536,384]{1,0:T(8,128)(2,1)}, u32[]{:S(2)}, u32[]{:S(2)}) collective-permute-start(bf16[1536,384]{1,0:T(8,128)(2,1)} %bitcast_convert_fusion.2), channel_id=1, source_target_pairs={{0,16},{1,17},{2,18},{3,19},{4,20},{5,21},{6,22},{7,23},{8,24},{9,... | collective-permute-start | bytes 3538952 | tf_op jit(solution)/shard_map/ppermute | solution.py:470
  1616.8 121.0 %collective-permute-start.73 = (bf16[384,1536]{1,0:T(8,128)(2,1)}, bf16[384,1536]{1,0:T(8,128)(2,1)}, u32[]{:S(2)}, u32[]{:S(2)}) collective-permute-start(bf16[384,1536]{1,0:T(8,128)(2,1)} %bitcast_convert_fusion.4), channel_id=1, source_target_pairs={{0,16},{1,17},{2,18},{3,19},{4,20},{5,21},{6,22},{7,23},{8,24},{9,... | collective-permute-start | bytes 3538952 | tf_op jit(solution)/shard_map/ppermute | solution.py:470
  (485 other events, 11751.2 us)
Sparse Core Ops, SparseCore 0:
  82.6 63.6 all-gather.14
  172.6 58.8 reduce-scatter.42
  263.0 62.8 all-gather.22
  352.0 58.8 reduce-scatter.44
  412.9 40.5 all-gather.16
  455.5 39.3 all-gather.24
  521.5 29.4 all-gather.18
  563.2 28.2 reduce-scatter.26
  593.9 29.1 all-gather.20
  632.0 32.4 reduce-scatter.28
  667.6 29.7 all-gather.26
  707.8 28.2 reduce-scatter.30
  738.5 29.1 all-gather.28
  769.1 29.5 all-gather.30
  807.3 28.9 reduce-scatter.34
  838.4 27.8 reduce-scatter.32
  870.7 29.1 all-gather.32
  914.4 28.4 reduce-scatter.36
  959.7 28.5 all-gather.34
  1000.7 28.2 reduce-scatter.38
  1033.3 35.3 all-gather.36
  1106.1 29.0 reduce-scatter.40
  1186.9 38.6 reduce-scatter.46
  1228.6 42.8 reduce-scatter.50
  1273.7 62.5 all-gather.38
  1364.0 58.8 reduce-scatter.48
  1472.3 63.2 all-gather.40
  1573.9 61.0 reduce-scatter.52

commit v2 on v1

v2 whole, which is shorter than its diff:
```python
import functools
import math

import jax
import jax.numpy as jnp
from jax import lax
from jax.experimental import pallas as pl
from jax.experimental.pallas import tpu as pltpu
from jax.sharding import PartitionSpec as P

HEAD_DIM = 64
LANES = 128
MARGIN = 8
BAND = 4
F32 = jnp.float32
BF16 = jnp.bfloat16


def product(left, right, left_axis, right_axis):
    return lax.dot_general(
        left, right, (((left_axis,), (right_axis,)), ((), ())), preferred_element_type=F32
    )


def settings(mebibytes):
    return pltpu.CompilerParams(vmem_limit_bytes=mebibytes << 20)


def fill_padded(padded, values):
    extent = values.shape[0]
    half = (padded.shape[0] - extent) // 2
    padded[...] = jnp.zeros_like(padded)
    padded[half : half + extent, MARGIN : MARGIN + extent, :] = values.astype(F32)


def windows_of(padded, first, side, extent):
    for col in range(side):
        start = MARGIN - side // 2 + col
        yield col, padded[pl.ds(first, BAND + side - 1), pl.ds(start, extent), :]


def mix_kernel(side, reverse, with_base, *refs):
    x_ref, kernel_ref = refs[:2]
    out_ref, padded = refs[-2:]
    extent = x_ref.shape[1]
    fill_padded(padded, x_ref[0])

    def band(step, carry):
        first = step * BAND
        if with_base:
            total = refs[2][0, pl.ds(first, BAND)]
        else:
            total = jnp.zeros((BAND, extent, x_ref.shape[3]), F32)
        for col, window in windows_of(padded, first, side, extent):
            for row in range(side):
                tap = row * side + col
                weight = kernel_ref[side * side - 1 - tap if reverse else tap]
                total = total + window[row : row + BAND] * weight
        out_ref[0, pl.ds(first, BAND)] = total.astype(out_ref.dtype)
        return carry

    lax.fori_loop(0, extent // BAND, band, 0)


def depthwise(grid, kernel, side, base=None, reverse=False, dtype=F32):
    images, extent, _, channels = grid.shape
    block = pl.BlockSpec((1, extent, extent, LANES), lambda n, c: (n, 0, 0, c))
    taps = pl.BlockSpec((side * side, LANES), lambda n, c: (0, c))
    extra = () if base is None else (base,)
    return pl.pallas_call(
        functools.partial(mix_kernel, side, reverse, base is not None),
        grid=(images, channels // LANES),
        in_specs=[block, taps] + [block] * len(extra),
        out_specs=block,
        out_shape=jax.ShapeDtypeStruct(grid.shape, dtype),
        scratch_shapes=[pltpu.VMEM((extent + side - 1, extent + 2 * MARGIN, LANES), F32)],
        compiler_params=settings(32),
    )(grid, kernel, *extra)


def taps_kernel(side, x_ref, upstream_ref, out_ref, padded, sums):
    extent = x_ref.shape[1]
    fill_padded(padded, x_ref[0])
    sums[...] = jnp.zeros_like(sums)

    def band(step, carry):
        first = step * BAND
        upstream = upstream_ref[0, pl.ds(first, BAND)]
        for col, window in windows_of(padded, first, side, extent):
            for row in range(side):
                part = window[row : row + BAND] * upstream
                sums[row * side + col] += jnp.sum(part.reshape(-1, 8, LANES), 0)
        return carry

    lax.fori_loop(0, extent // BAND, band, 0)
    out_ref[0] = jnp.sum(sums[...], 1)


def depthwise_taps(grid, upstream, side):
    images, extent, _, channels = grid.shape
    block = pl.BlockSpec((1, extent, extent, LANES), lambda n, c: (n, 0, 0, c))
    sums = pl.pallas_call(
        functools.partial(taps_kernel, side),
        grid=(images, channels // LANES),
        in_specs=[block, block],
        out_specs=pl.BlockSpec((1, side * side, LANES), lambda n, c: (n, 0, c)),
        out_shape=jax.ShapeDtypeStruct((images, side * side, channels), F32),
        scratch_shapes=[
            pltpu.VMEM((extent + side - 1, extent + 2 * MARGIN, LANES), F32),
            pltpu.VMEM((side * side, 8, LANES), F32),
        ],
        compiler_params=settings(32),
    )(grid, upstream)
    return jnp.sum(sums, 0)


def gelu_and_slope(values):
    cumulative = 0.5 * (1.0 + lax.erf(values * (1.0 / math.sqrt(2.0))))
    density = jnp.exp(-0.5 * values * values) * (1.0 / math.sqrt(2.0 * math.pi))
    return ((values * cumulative).astype(BF16), (cumulative + values * density).astype(BF16))


def store_parts(out_ref, total):
    if len(out_ref.shape) == 2:
        out_ref[...] = total.astype(BF16)
        return
    width = out_ref.shape[2]
    for part in range(out_ref.shape[0]):
        out_ref[part] = total[:, part * width : (part + 1) * width].astype(BF16)


def mlp_kernel(step, x_ref, first_ref, second_ref, hidden_ref, slope_ref, out_ref):
    x = x_ref[...]
    total = None
    for at in range(0, first_ref.shape[1], step):
        units = slice(at, at + step)
        hidden, slope = gelu_and_slope(product(x, first_ref[:, units], 1, 0))
        hidden_ref[:, units] = hidden
        slope_ref[:, units] = slope
        part = product(hidden, second_ref[units, :], 1, 0)
        total = part if total is None else total + part
    store_parts(out_ref, total)


def mlp_back_kernel(step, upstream_ref, slope_ref, first_ref, second_ref, grad_ref, out_ref):
    upstream = upstream_ref[...]
    total = None
    for at in range(0, first_ref.shape[1], step):
        units = slice(at, at + step)
        grad = product(upstream, second_ref[units, :], 1, 1) * slope_ref[:, units].astype(F32)
        grad = grad.astype(BF16)
        grad_ref[:, units] = grad
        part = product(grad, first_ref[:, units], 1, 1)
        total = part if total is None else total + part
    store_parts(out_ref, total)


def parts_spec(count, rows, width, tile):
    if count is None:
        return (
            pl.BlockSpec((tile, width), lambda i: (i, 0)),
            jax.ShapeDtypeStruct((rows, width), BF16),
        )
    return (
        pl.BlockSpec((count, tile, width // count), lambda i: (0, i, 0)),
        jax.ShapeDtypeStruct((count, rows, width // count), BF16),
    )


def largest_step(units):
    return 512 if units % 512 == 0 else units


def mlp(x, first, second, tile, count=None):
    rows, units = (x.shape[0], first.shape[1])
    whole = [pl.BlockSpec(w.shape, lambda i: (0, 0)) for w in (first, second)]
    out_spec, out_shape = parts_spec(count, rows, second.shape[1], tile)
    inside = pl.BlockSpec((tile, units), lambda i: (i, 0))
    return pl.pallas_call(
        functools.partial(mlp_kernel, largest_step(units)),
        grid=(rows // tile,),
        in_specs=[pl.BlockSpec((tile, x.shape[1]), lambda i: (i, 0))] + whole,
        out_specs=[inside, inside, out_spec],
        out_shape=[jax.ShapeDtypeStruct((rows, units), BF16)] * 2 + [out_shape],
        compiler_params=settings(56),
    )(x, first, second)


def mlp_back(upstream, slope, first, second, tile, count=None):
    rows, units = slope.shape
    whole = [pl.BlockSpec(w.shape, lambda i: (0, 0)) for w in (first, second)]
    out_spec, out_shape = parts_spec(count, rows, first.shape[0], tile)
    inside = pl.BlockSpec((tile, units), lambda i: (i, 0))
    return pl.pallas_call(
        functools.partial(mlp_back_kernel, largest_step(units)),
        grid=(rows // tile,),
        in_specs=[pl.BlockSpec((tile, upstream.shape[1]), lambda i: (i, 0)), inside] + whole,
        out_specs=[inside, out_spec],
        out_shape=[jax.ShapeDtypeStruct((rows, units), BF16), out_shape],
        compiler_params=settings(56),
    )(upstream, slope, first, second)


def head_probs(query, keys, mask):
    scores = product(query, keys, 1, 1) * (HEAD_DIM**-0.5)
    scores = jnp.where(mask > 0, scores, -1000000000.0)
    raised = jnp.exp(scores - jnp.max(scores, -1, keepdims=True))
    return raised * (1.0 / jnp.sum(raised, -1, keepdims=True))


def lane_pairs(width):
    for pair in range(width // LANES):
        yield [slice(at + pair * LANES, at + (pair + 1) * LANES) for at in (0, width, 2 * width)]


def heads_of(pair):
    return [pair[:, at : at + HEAD_DIM] for at in range(0, LANES, HEAD_DIM)]


def attend_kernel(project_ref, mask_ref, out_ref):
    mask = mask_ref[0]
    for places in lane_pairs(out_ref.shape[2]):
        query, keys, values = (heads_of(project_ref[0, :, at]) for at in places)
        parts = [
            product(head_probs(q, k, mask).astype(BF16), u, 1, 0).astype(BF16)
            for q, k, u in zip(query, keys, values)
        ]
        out_ref[0, :, places[0]] = jnp.concatenate(parts, 1)


def attend(project, mask):
    images, tokens, wide = project.shape
    width = wide // 3
    return pl.pallas_call(
        attend_kernel,
        grid=(images,),
        in_specs=[
            pl.BlockSpec((1, tokens, wide), lambda i: (i, 0, 0)),
            pl.BlockSpec((1, 1, tokens), lambda i: (i, 0, 0)),
        ],
        out_specs=pl.BlockSpec((1, tokens, width), lambda i: (i, 0, 0)),
        out_shape=jax.ShapeDtypeStruct((images, tokens, width), BF16),
        compiler_params=settings(48),
    )(project, mask[:, None, :])


def attend_back_kernel(project_ref, mask_ref, upstream_ref, out_ref):
    mask = mask_ref[0]
    scale = HEAD_DIM**-0.5
    for places in lane_pairs(upstream_ref.shape[2]):
        query, keys, values = (heads_of(project_ref[0, :, at]) for at in places)
        upstream = heads_of(upstream_ref[0, :, places[0]])
        grads = ([], [], [])
        for q, k, u, d in zip(query, keys, values, upstream):
            exact = head_probs(q, k, mask)
            grad_probs = product(d, u, 1, 1)
            held = jnp.sum(grad_probs * exact, -1, keepdims=True)
            grad_scores = (exact * (grad_probs - held)).astype(BF16)
            grads[0].append((product(grad_scores, k, 1, 0) * scale).astype(BF16))
            grads[1].append((product(grad_scores, q, 0, 0) * scale).astype(BF16))
            grads[2].append(product(exact.astype(BF16), d, 0, 0).astype(BF16))
        for at, parts in zip(places, grads):
            out_ref[0, :, at] = jnp.concatenate(parts, 1)


def attend_back(project, mask, upstream):
    images, tokens, wide = project.shape
    width = wide // 3
    whole = pl.BlockSpec((1, tokens, wide), lambda i: (i, 0, 0))
    return pl.pallas_call(
        attend_back_kernel,
        grid=(images,),
        in_specs=[
            whole,
            pl.BlockSpec((1, 1, tokens), lambda i: (i, 0, 0)),
            pl.BlockSpec((1, tokens, width), lambda i: (i, 0, 0)),
        ],
        out_specs=whole,
        out_shape=jax.ShapeDtypeStruct(project.shape, BF16),
        compiler_params=settings(48),
    )(project, mask[:, None, :], upstream)


def traded(array, axis, bit):
    return lax.ppermute(array, axis, [(i, i ^ bit) for i in range(lax.axis_size(axis))])


def bits_of(axis):
    return [1 << k for k in range((lax.axis_size(axis) - 1).bit_length())]


def total_over(values, axis):
    for bit in bits_of(axis):
        values = values + traded(values, axis, bit)
    return values


def first_section():
    return lax.axis_index("pipe") == 0


def select(former, latter):
    return jnp.where(first_section(), former, latter)


def layer_pair(own):
    flat = own.reshape((2, own.shape[0] // 2) + own.shape[1:])
    odd = lax.axis_index("dp") % 2
    sent = lax.dynamic_index_in_dim(flat, odd, 0, keepdims=False)
    got = traded(sent, "pipe", 1)
    rest = traded(got, "dp", 1)
    first_half = jnp.where(odd == 0, got, rest)
    second_half = jnp.where(odd == 0, rest, got)
    other = jnp.concatenate([first_half, second_half], 0)
    return (select(own, other), select(other, own))


def small_pair(own):
    other = traded(own, "pipe", 1)
    return (select(own, other), select(other, own))


def own_block(values, count, axis):
    return lax.dynamic_slice_in_dim(values, lax.axis_index("tensor") * count, count, axis)


def widen(values, whole, axis):
    shape = list(values.shape)
    shape[axis] = whole
    empty = jnp.zeros(tuple(shape), F32)
    return lax.dynamic_update_slice_in_dim(
        empty, values, lax.axis_index("tensor") * values.shape[axis], axis
    )


def gather(values):
    return lax.all_gather(values, "tensor", axis=1, tiled=True)


def scatter_tokens(values):
    return lax.psum_scatter(values, "tensor", scatter_dimension=1, tiled=True).astype(F32)


def scatter_parts(parts):
    return lax.psum_scatter(parts, "tensor", scatter_dimension=0, tiled=False).astype(F32)


def relative_order(count):
    width = (count - 1).bit_length()
    return sorted(range(count), key=lambda r: format(r, f"0{width}b")[::-1])


def by_relative(values):
    count = lax.axis_size("dp")
    index = lax.axis_index("dp")
    block = values.shape[1] // count
    return jnp.concatenate(
        [
            lax.dynamic_slice_in_dim(values, (index ^ r) * block, block, 1)
            for r in relative_order(count)
        ],
        1,
    )


def inner(left, right, axis):
    if axis == 0:
        left = by_relative(left)
    else:
        right = by_relative(right)
    return product(left, right, 0, 0).astype(BF16)


def halved(partial, axis):
    for bit in bits_of("dp"):
        kept, sent = jnp.split(partial, 2, axis)
        partial = kept.astype(F32) + traded(sent, "dp", bit).astype(F32)
        if bit != bits_of("dp")[-1]:
            partial = partial.astype(BF16)
    return partial


def share_of(partial, axis, layer):
    block = halved(partial, axis)
    arrived = lax.ppermute(block.astype(BF16), "pipe", [(1 - layer, layer)])
    return (block, arrived)


def windows(coarse, fine):
    starts = [row * fine // coarse for row in range(coarse)]
    stops = [-(-(row + 1) * fine // coarse) for row in range(coarse)]
    return (starts, stops)


def pool_axis(grid, axis, coarse):
    starts, stops = windows(coarse, grid.shape[axis])
    slabs = []
    for start, stop in zip(starts, stops):
        slab = lax.slice_in_dim(grid, start, stop, axis=axis)
        slabs.append(jnp.sum(slab, axis=axis, keepdims=True) * (1.0 / (stop - start)))
    return jnp.concatenate(slabs, axis)


def unpool_axis(grid, axis, fine):
    starts, stops = windows(grid.shape[axis], fine)
    slabs = []
    for place in range(fine):
        parts = [
            lax.slice_in_dim(grid, row, row + 1, axis=axis) * (1.0 / (stop - start))
            for row, (start, stop) in enumerate(zip(starts, stops))
            if start <= place < stop
        ]
        slabs.append(sum(parts[1:], parts[0]))
    return jnp.concatenate(slabs, axis)


def norm_rows(values, epsilon):
    centred = values - jnp.mean(values, -1, keepdims=True)
    inverse = lax.rsqrt(jnp.mean(centred * centred, -1, keepdims=True) + epsilon)
    return (centred * inverse, inverse)


def norm_back(upstream, scaled, inverse, gains):
    weighted = upstream * gains
    return inverse * (
        weighted
        - jnp.mean(weighted, -1, keepdims=True)
        - scaled * jnp.mean(weighted * scaled, -1, keepdims=True)
    )


def flat(values):
    return values.reshape(-1, values.shape[-1])


def placing(places):
    cells = jnp.arange(places.shape[1])
    return (places[:, :, None] == cells[None, None, :]).astype(BF16)


def conv_forward(feature, w):
    images, cells, own = feature.shape
    side = math.isqrt(cells)
    count = lax.axis_size("tensor")
    channels = own * count
    grid = feature.reshape(images, side, side, own)
    mixed = flat(depthwise(grid, w["dw"], 7))
    sums = total_over(jnp.stack([jnp.sum(mixed, -1), jnp.sum(mixed * mixed, -1)]), "tensor")
    centre = sums[0] / channels
    inverse = lax.rsqrt(sums[1] / channels - centre * centre + 1e-06)
    scaled = (mixed - centre[:, None]) * inverse[:, None]
    normed = gather((scaled * w["gain"][0] + w["shift"]).astype(BF16))
    hidden, slope, parts = mlp(normed, w["pw_in"], w["pw_out"], cells // 2, count)
    branch = scatter_parts(parts)
    out = flat(feature).astype(F32) + w["gain"][1] * branch
    square = total_over(jnp.sum(out * out, -1), "tensor")
    measure = jnp.sqrt(square / channels).reshape(images, cells)
    kept = dict(
        grid=grid,
        scaled=scaled,
        inverse=inverse,
        normed=normed,
        hidden=hidden,
        slope=slope,
        branch=branch,
    )
    return (out.reshape(images, cells, own), measure, kept)


def vit_forward(stream, feature_out, places, key_mask, w):
    images, own_tokens, width = stream.shape
    count = lax.axis_size("tensor")
    tokens = own_tokens * count
    side = math.isqrt(tokens)
    cells, own = feature_out.shape[1:]
    fine = math.isqrt(cells)
    own_width = w["attn"].shape[0]
    pooled = pool_axis(feature_out.reshape(images, fine, fine, own), 1, side)
    pooled = pool_axis(pooled, 2, side)
    pooled = gather(pooled.reshape(images * tokens, own).astype(BF16))
    adapted = product(pooled, w["proj_cols"], 1, 0).reshape(images, side, side, own_width)
    spread = depthwise(adapted, w["taps"], 3).reshape(images, tokens, own_width)
    gated = (jnp.tanh(w["gate"]) * spread).astype(BF16)
    picked = jnp.einsum("ntc,ncw->ntw", places, gated, preferred_element_type=F32).astype(BF16)
    moved = lax.all_to_all(picked, "tensor", split_axis=1, concat_axis=2, tiled=True)
    stream_in = stream + moved.astype(F32)
    scaled_a, inverse_a = norm_rows(stream_in, 1e-05)
    normed_a = gather((scaled_a * w["vit_gain"][0] + w["vit_shift"][0]).astype(BF16))
    project = product(flat(normed_a), w["qkv"], 1, 0).astype(BF16)
    project = project.reshape(images, tokens, 3 * own_width)
    attended = attend(project, key_mask)
    partial = product(flat(attended), w["attn"], 1, 0).astype(BF16)
    stream_mid = stream_in + scatter_tokens(partial.reshape(images, tokens, width))
    scaled_b, inverse_b = norm_rows(stream_mid, 1e-05)
    normed_b = gather((scaled_b * w["vit_gain"][1] + w["vit_shift"][1]).astype(BF16))
    hidden, slope, partial = mlp(flat(normed_b), w["fc_in"], w["fc_out"], tokens)
    stream_out = stream_mid + scatter_tokens(partial.reshape(images, tokens, width))
    measure = jnp.sqrt(jnp.mean(stream_out * stream_out, -1))
    kept = dict(
        pooled=pooled,
        adapted=adapted,
        spread=spread,
        places=places,
        key_mask=key_mask,
        scaled_a=scaled_a,
        inverse_a=inverse_a,
        normed_a=normed_a,
        project=project,
        attended=attended,
        scaled_b=scaled_b,
        inverse_b=inverse_b,
        normed_b=normed_b,
        hidden=hidden,
        slope=slope,
    )
    return (stream_out, measure, kept)


def vit_backward(grad_stream, cells, kept, w):
    images, own_tokens, width = grad_stream.shape
    count = lax.axis_size("tensor")
    tokens = own_tokens * count
    side = math.isqrt(tokens)
    own_width = w["attn"].shape[0]
    grad_full = flat(gather(grad_stream.astype(BF16)))
    grad_hidden, partial = mlp_back(grad_full, kept["slope"], w["fc_in"], w["fc_out"], tokens)
    fc_out = inner(kept["hidden"], grad_full, 1)
    fc_in = inner(flat(kept["normed_b"]), grad_hidden, 0)
    grad_normed_b = scatter_tokens(partial.reshape(images, tokens, width))
    gain_second = jnp.sum(grad_normed_b * kept["scaled_b"], (0, 1))
    shift_second = jnp.sum(grad_normed_b, (0, 1))
    grad_mid = grad_stream.astype(F32) + norm_back(
        grad_normed_b, kept["scaled_b"], kept["inverse_b"], w["vit_gain"][1]
    )
    grad_mid_full = flat(gather(grad_mid.astype(BF16)))
    grad_attended = product(grad_mid_full, w["attn"], 1, 1).astype(BF16)
    grad_project = flat(
        attend_back(
            kept["project"], kept["key_mask"], grad_attended.reshape(images, tokens, own_width)
        )
    )
    partial = product(grad_project, w["qkv"], 1, 1).astype(BF16)
    attn = inner(flat(kept["attended"]), grad_mid_full, 1)
    qkv = inner(flat(kept["normed_a"]), grad_project, 0)
    grad_normed_a = scatter_tokens(partial.reshape(images, tokens, width))
    gain_first = jnp.sum(grad_normed_a * kept["scaled_a"], (0, 1))
    shift_first = jnp.sum(grad_normed_a, (0, 1))
    grad_in = grad_mid + norm_back(
        grad_normed_a, kept["scaled_a"], kept["inverse_a"], w["vit_gain"][0]
    )
    grad_cols = lax.all_to_all(
        grad_in.astype(BF16), "tensor", split_axis=2, concat_axis=1, tiled=True
    )
    grad_placed = jnp.einsum(
        "ntc,ntw->ncw", kept["places"], grad_cols, preferred_element_type=F32
    )
    gate_value = jnp.tanh(w["gate"])
    gate = jnp.sum(grad_placed * kept["spread"], (0, 1)) * (1.0 - gate_value * gate_value)
    grad_spread = (grad_placed * gate_value).reshape(images, side, side, own_width)
    grad_adapted = flat(depthwise(grad_spread, w["taps"], 3, reverse=True, dtype=BF16))
    taps = depthwise_taps(kept["adapted"], grad_spread, 3)
    grad_pooled = product(gather(grad_adapted), w["proj_rows"], 1, 1)
    proj = inner(kept["pooled"], grad_adapted, 0)
    grads = dict(qkv=qkv, attn=attn, fc_in=fc_in, fc_out=fc_out, proj=proj)
    model_width = w["vit_gain"].shape[1]
    sums = jnp.concatenate(
        [
            widen(taps, model_width, 1),
            widen(gate[None], model_width, 1),
            jnp.stack([gain_first, gain_second, shift_first, shift_second]),
        ],
        0,
    )
    return (grad_in, grad_pooled, grads, sums)


def conv_backward(grad_feature, grad_pooled, kept, w):
    images, cells, own = grad_feature.shape
    count = lax.axis_size("tensor")
    channels = own * count
    side = math.isqrt(cells)
    coarse = math.isqrt(grad_pooled.shape[0] // images)
    unpooled = unpool_axis(grad_pooled.reshape(images, coarse, coarse, own), 2, side)
    unpooled = unpool_axis(unpooled, 1, side)
    grad_rows = flat(grad_feature).astype(F32) + flat(unpooled)
    grad_branch = gather((grad_rows * w["gain"][1]).astype(BF16))
    grad_hidden, parts = mlp_back(
        grad_branch, kept["slope"], w["pw_in"], w["pw_out"], cells // 2, count
    )
    scale = jnp.sum(grad_rows * kept["branch"], 0)
    pw_out = inner(kept["hidden"], grad_branch, 1)
    pw_in = inner(kept["normed"], grad_hidden, 0)
    grad_normed = scatter_parts(parts)
    scaled = kept["scaled"]
    gain = jnp.sum(grad_normed * scaled, 0)
    shift = jnp.sum(grad_normed, 0)
    weighted = grad_normed * w["gain"][0]
    sums = total_over(jnp.stack([jnp.sum(weighted, -1), jnp.sum(weighted * scaled, -1)]), "tensor")
    grad_mixed = kept["inverse"][:, None] * (
        weighted - sums[0][:, None] / channels - scaled * (sums[1][:, None] / channels)
    )
    grad_grid = grad_mixed.reshape(images, side, side, own)
    grad_in = depthwise(
        grad_grid, w["dw"], 7, base=grad_rows.reshape(images, side, side, own), reverse=True
    )
    taps = depthwise_taps(kept["grid"], grad_grid, 7)
    sums = jnp.concatenate([taps, jnp.stack([gain, scale, shift])], 0)
    return (grad_in.reshape(images, cells, own), dict(pw_in=pw_in, pw_out=pw_out), sums)


SPLIT_AXIS = dict(qkv=0, attn=1, fc_in=0, fc_out=1, pw_in=0, pw_out=1, proj=0)


def body(
    x_vit,
    x_conv,
    positions,
    valid,
    qkv_weight,
    attn_weight,
    fc_in,
    fc_out,
    vit_gains,
    vit_shifts,
    pw_in,
    pw_out,
    dw_kernel,
    conv_gains,
    conv_shift,
    proj_weight,
    taps,
    gate,
    dy_vit,
    dy_conv,
):
    sections = lax.axis_size("pipe")
    here = x_vit.shape[0] // sections
    own_width = attn_weight.shape[1]
    own_channels = pw_out.shape[2] // lax.axis_size("tensor")
    model_width = vit_gains.shape[2]
    tap_count = dw_kernel.shape[1]
    side = taps.shape[1]

    def portion(source):
        return lax.dynamic_slice_in_dim(source, lax.axis_index("pipe") * here, here, 0)

    conv_small = small_pair(jnp.concatenate([dw_kernel[0], conv_gains[0], conv_shift], 0))
    pairs = dict(pw_in=layer_pair(pw_in[0]), pw_out=layer_pair(pw_out[0]))
    vit_small = small_pair(jnp.concatenate([taps[0], gate, vit_gains[0], vit_shifts[0]], 0))
    pairs.update(
        proj_cols=layer_pair(own_block(proj_weight[0], own_width, 1)),
        qkv=layer_pair(qkv_weight[0].reshape(model_width, -1)),
        attn=layer_pair(attn_weight[0]),
        fc_in=layer_pair(fc_in[0]),
        fc_out=layer_pair(fc_out[0]),
        proj_rows=layer_pair(own_block(proj_weight[0], own_channels, 0)),
    )

    def weights_of(layer):
        w = {name: pair[layer] for name, pair in pairs.items()}
        conv, vit = (conv_small[layer], vit_small[layer])
        w.update(
            dw=conv[:tap_count],
            gain=conv[tap_count : tap_count + 2],
            shift=conv[tap_count + 2],
            taps=own_block(vit[:side], own_width, 1),
            gate=own_block(vit[side], own_width, 0),
            vit_gain=vit[side + 1 : side + 3],
            vit_shift=vit[side + 3 :],
        )
        return w

    weights = [weights_of(0), weights_of(1)]
    places = placing(portion(positions))
    key_mask = portion(valid)
    stream, feature = (portion(x_vit), portion(x_conv))
    outs = [{}, {}]
    conv_kept, vit_kept = ([None, None], [None, None])
    features = [None, None]
    for layer in range(2):
        features[layer], measure, conv_kept[layer] = conv_forward(feature, weights[layer])
        feature = features[layer].astype(BF16)
        outs[layer].update(conv=feature, rms_conv=measure)
    for layer in range(2):
        stream_out, measure, vit_kept[layer] = vit_forward(
            stream.astype(F32), features[layer], places, key_mask, weights[layer]
        )
        stream = stream_out.astype(BF16)
        outs[layer].update(vit=stream, rms_vit=measure)
    grad_stream, grad_feature = (portion(dy_vit), portion(dy_conv))
    shares = [{}, {}]
    vit_sums, conv_sums = ([None, None], [None, None])
    pooled_grads = [None, None]
    for layer in (1, 0):
        grad_stream, pooled_grads[layer], grads, vit_sums[layer] = vit_backward(
            grad_stream, feature.shape[1], vit_kept[layer], weights[layer]
        )
        outs[layer]["grad_vit"] = grad_stream
        grad_stream = grad_stream.astype(BF16)
        for name, partial in grads.items():
            shares[layer][name] = share_of(partial, SPLIT_AXIS[name], layer)
    for layer in (1, 0):
        grad_feature, grads, conv_sums[layer] = conv_backward(
            grad_feature, pooled_grads[layer], conv_kept[layer], weights[layer]
        )
        outs[layer]["grad_conv"] = grad_feature
        grad_feature = grad_feature.astype(BF16)
        for name, partial in grads.items():
            shares[layer][name] = share_of(partial, SPLIT_AXIS[name], layer)

    def over_images(pair):
        return total_over(select(*pair) + traded(select(*pair[::-1]), "pipe", 1), "dp")

    token_sums = total_over(over_images(vit_sums), "tensor")
    column_sums = over_images(conv_sums)

    def large(name):
        (block, arrived), (other_block, other_arrived) = (shares[0][name], shares[1][name])
        total = select(block, other_block) + arrived.astype(F32) + other_arrived.astype(F32)
        return total.reshape((1,) + total.shape)

    def both_images(name):
        mine, theirs = (
            select(outs[0][name], outs[1][name]),
            select(outs[1][name], outs[0][name]),
        )
        sent = theirs.astype(BF16) if name.startswith("grad") else theirs
        got = traded(sent, "pipe", 1).astype(mine.dtype)
        return jnp.concatenate([select(mine, got), select(got, mine)], 0)[None]

    grad_qkv = large("qkv")
    return (
        both_images("vit"),
        both_images("conv"),
        both_images("grad_vit"),
        both_images("grad_conv"),
        both_images("rms_vit"),
        both_images("rms_conv"),
        grad_qkv.reshape(grad_qkv.shape[:2] + (3, own_width)),
        large("attn"),
        large("fc_in"),
        large("fc_out"),
        token_sums[side + 1 : side + 3][None],
        token_sums[side + 3 :][None],
        large("pw_in"),
        large("pw_out"),
        column_sums[:tap_count][None],
        column_sums[tap_count : tap_count + 2][None],
        column_sums[tap_count + 2 :],
        large("proj"),
        token_sums[:side][None],
        token_sums[side][None],
    )


def solution(mesh):
    return jax.shard_map(
        body,
        mesh=mesh,
        in_specs=(
            P("dp", "tensor", None),
            P("dp", None, "tensor"),
            P("dp", None),
            P("dp", None),
            P("pipe", None, None, "tensor"),
            P("pipe", "tensor", None),
            P("pipe", None, "tensor"),
            P("pipe", "tensor", None),
            P("pipe", None, None),
            P("pipe", None, None),
            P("pipe", None, "tensor"),
            P("pipe", "tensor", None),
            P("pipe", None, "tensor"),
            P("pipe", None, "tensor"),
            P("pipe", "tensor"),
            P("pipe", None, None),
            P("pipe", None, None),
            P("pipe", None),
            P("dp", "tensor", None),
            P("dp", None, "tensor"),
        ),
        out_specs=(
            P("pipe", "dp", "tensor", None),
            P("pipe", "dp", None, "tensor"),
            P("pipe", "dp", "tensor", None),
            P("pipe", "dp", None, "tensor"),
            P("pipe", "dp", "tensor"),
            P("pipe", "dp", None),
            P("pipe", "dp", None, "tensor"),
            P("pipe", "tensor", "dp"),
            P("pipe", "dp", "tensor"),
            P("pipe", "tensor", "dp"),
            P("pipe", None, None),
            P("pipe", None, None),
            P("pipe", "dp", "tensor"),
            P("pipe", "tensor", "dp"),
            P("pipe", None, "tensor"),
            P("pipe", None, "tensor"),
            P("pipe", "tensor"),
            P("pipe", "dp", "tensor"),
            P("pipe", None, None),
            P("pipe", None),
        ),
        check_vma=False,
    )
```

time: 1780 us -> 1600 us (0.90)
  Pallas kernels: 0 us -> 158 us
  other arithmetic: 384 us -> 239 us
  matrix products: 217 us -> 75.4 us
  local copies, waits for them, and re-layouts: 289 us -> 174 us
  waiting for transfers between devices: 730 us -> 768 us
  blocking collectives: 0 us -> 35.8 us
    pallas_call x0 -> x24, Pallas kernels: none -> 158 us  [the longest x4 47.2 us: mlp(): pl.pallas_call(functools.partial(mlp_kernel, largest_step(units)), grid=(...]
    dot_general x54 -> x30, matrix products: 217 us -> 75.4 us  [the longest x26 72.5 us: product(): lax.dot_general(left, right, (((left_axis,), (right_axis,)), ((), ())), p...]
    reduce_scatter x8 -> x12, waiting for transfers between devices: 115 us -> 231 us  [the longest x4 148 us: scatter_parts(): lax.psum_scatter(parts, 'tensor', scatter_dimension=0, tiled=False)]
    unnamed x34 -> x28, waiting for transfers between devices: 115 us -> 0.96 us
    ppermute x75 -> x72, waiting for transfers between devices: 174 us -> 275 us  [traded(): lax.ppermute(array, axis, [(i, i ^ bit) for i in range(lax.axis_size(axis...]
    reduce_sum x23 -> x14, other arithmetic: 116 us -> 21.8 us  [the longest x2 4.89 us: conv_backward(): gain = jnp.sum(grad_normed * scaled, 0)]
    unnamed x819 -> x479, local copies, waits for them, and re-layouts: 115 us -> 52.9 us
    add x23 -> x6, other arithmetic: 61.4 us -> 8.57 us  [the longest x2 3.22 us: conv_forward(): out = flat(feature).astype(F32) + w['gain'][1] * branch]
  transfers between devices with their start and end apart: 121 -> 116, of which waited for: 49 -> 57; matrix products, arithmetic and copies ran while one was open for 40% -> 26% of each run, Pallas kernels for 0% -> 8%
where the time goes in v2:
time: 1600 us; the launch traced here: 1590 us
  waiting for transfers between devices  768 us (48%)
  other arithmetic  239 us (15%)
  local copies, waits for them, and re-layouts  174 us (11%)
  Pallas kernels  158 us (10%)
  starting transfers between devices  118 us (7%)
  matrix products  75.4 us (5%)
  blocking collectives  35.8 us (2%)
  between operations  18.6 us (1%)
    ppermute x72, waiting for transfers between devices, traded(): lax.ppermute(array, axis, [(i, i ^ bit) for i in range(lax.axis_size(axis...  275 us
    all_gather x16, waiting for transfers between devices, gather(): return lax.all_gather(values, 'tensor', axis=1, tiled=True)  227 us
    reduce_scatter x4, waiting for transfers between devices, scatter_parts(): lax.psum_scatter(parts, 'tensor', scatter_dimension=0, tiled=False)  148 us
    reduce_scatter x8, waiting for transfers between devices, scatter_tokens(): lax.psum_scatter(values, 'tensor', scatter_dimension=1, tiled=True)  83.3 us
    dot_general x26, matrix products, product(): lax.dot_general(left, right, (((left_axis,), (right_axis,)), ((), ())), p...  72.5 us
    ppermute x72, starting transfers between devices, traded(): lax.ppermute(array, axis, [(i, i ^ bit) for i in range(lax.axis_size(axis...  66 us
    unnamed x139, other arithmetic  62 us
    unnamed x479, local copies, waits for them, and re-layouts  52.9 us
  transfers between devices with their start and end apart: 116, of which 57 were waited for; matrix products, arithmetic and copies ran while one was open for 26% of the time, Pallas kernels for 8%

profile of v2, /device:TPU:0, one launch (start us, length us, event | category | flops | bytes accessed | tf_op | source)
XLA Modules:
  0.0 1587.1 jit_solution(25147334943621686)
XLA Ops:
  15.0 49.5 %collective-permute-done.6 = bf16[768,1536]{1,0:T(8,128)(2,1)} collective-permute-done((bf16[768,1536]{1,0:T(8,128)(2,1)S(1)}, bf16[768,1536]{1,0:T(8,128)(2,1)}, u32[]{:S(2)}, u32[]{:S(2)}) %collective-permute-start.6) | collective-permute-done | bytes 2359328 | tf_op jit(solution)/shard_map/ppermute | solution.py:285
  67.9 48.1 %collective-permute-done.1 = f32[52,384]{1,0:T(8,128)S(1)} collective-permute-done((f32[52,384]{1,0:T(8,128)S(1)}, f32[52,384]{1,0:T(8,128)S(1)}, u32[]{:S(2)}, u32[]{:S(2)}) %collective-permute-start.1) | collective-permute-done | bytes 79904 | tf_op jit(solution)/shard_map/ppermute | solution.py:285
  152.4 49.6 %all-gather.17.cloned.1.call-done.x_ref = bf16[1024,1536]{1,0:T(8,128)(2,1)} async-done(((bf16[1024,384]{1,0:T(8,128)(2,1)}), bf16[1024,1536]{1,0:T(8,128)(2,1)}) %all-gather.17.cloned.1.call-update) | async-done | bytes 3145744 | tf_op jit(solution)/shard_map/all_gather | solution.py:337
  202.0 17.0 %shard_map.348 = (bf16[1024,1536]{1,0:T(8,128)(2,1)}, bf16[1024,1536]{1,0:T(8,128)(2,1)}, bf16[4,1024,384]{2,1,0:T(8,128)(2,1)}) custom-call(bf16[1024,1536]{1,0:T(8,128)(2,1)} %all-gather.17.cloned.1.call-done.x_ref, bf16[1536,1536]{1,0:T(8,128)(2,1)} %get-tuple-element.362.first_ref, bf16[1536,1536]{1,0:T(8,128)(2,1)} %get-tuple-element.360.second_ref), custom_call_target="tpu_custom_call" | custom-call | tf_op jit(solution)/shard_map/pallas_call | solution.py:179
  219.3 58.8 %reduce-scatter.13.cloned.1.call-done = bf16[1,1024,384]{2,1,0:T(8,128)(2,1)} async-done(((bf16[4,1024,384]{2,1,0:T(8,128)(2,1)}), bf16[1,1024,384]{2,1,0:T(8,128)(2,1)}) %reduce-scatter.13.cloned.1.call-update) | async-done | bytes 786448 | tf_op jit(solution)/shard_map/reduce_scatter | solution.py:345
  286.3 9.9 collective-permute-done
  298.9 25.5 %all-gather.19.cloned.1.call-done = bf16[576,1536]{1,0:T(8,128)(2,1)} async-done(((bf16[576,384]{1,0:T(8,128)(2,1)}), bf16[576,1536]{1,0:T(8,128)(2,1)}) %all-gather.19.cloned.1.call-update) | async-done | bytes 1769488 | tf_op jit(solution)/shard_map/all_gather | solution.py:337
  335.8 13.4 all_to_all.48
  399.0 13.9 collective-permute-done.10
  452.9 17.0 %shard_map.353 = (bf16[1024,1536]{1,0:T(8,128)(2,1)}, bf16[1024,1536]{1,0:T(8,128)(2,1)}, bf16[4,1024,384]{2,1,0:T(8,128)(2,1)}) custom-call(bf16[1024,1536]{1,0:T(8,128)(2,1)} %all-gather.25.cloned.1.call-done.x_ref, bf16[1536,1536]{1,0:T(8,128)(2,1)} %get-tuple-element.361.first_ref, bf16[1536,1536]{1,0:T(8,128)(2,1)} %get-tuple-element.359.second_ref), custom_call_target="tpu_custom_call" | custom-call | tf_op jit(solution)/shard_map/pallas_call | solution.py:179
  486.5 58.2 %reduce-scatter.19.cloned.1.call-done = bf16[1,1024,384]{2,1,0:T(8,128)(2,1)} async-done(((bf16[4,1024,384]{2,1,0:T(8,128)(2,1)}), bf16[1,1024,384]{2,1,0:T(8,128)(2,1)}) %reduce-scatter.19.cloned.1.call-update) | async-done | bytes 786448 | tf_op jit(solution)/shard_map/reduce_scatter | solution.py:345
  593.4 25.8 %all-gather.27.cloned.1.call-done = bf16[576,1536]{1,0:T(8,128)(2,1)} async-done(((bf16[576,384]{1,0:T(8,128)(2,1)}), bf16[576,1536]{1,0:T(8,128)(2,1)}) %all-gather.27.cloned.1.call-update) | async-done | bytes 1769488 | tf_op jit(solution)/shard_map/all_gather | solution.py:337
  629.8 22.3 %all_to_all.49 = bf16[4,2,18432]{2,1,0:T(2,128)(2,1)} all-to-all(bf16[4,2,18432]{2,1,0:T(2,128)(2,1)} %reshape.2932), channel_id=1, replica_groups=mesh['pipe'=2,'dp'=4,'tensor'=4] {'tensor'}, dimensions={0} | all-to-all | bytes 589824 | tf_op jit(solution)/shard_map/all_to_all | solution.py:485
  662.6 30.3 %all-gather.29.cloned.1.call-done = bf16[1,576,1024]{2,1,0:T(8,128)(2,1)} async-done(((bf16[1,144,1024]{2,1,0:T(8,128)(2,1)}), bf16[1,576,1024]{2,1,0:T(8,128)(2,1)}) %all-gather.29.cloned.1.call-update) | async-done | bytes 1179664 | tf_op jit(solution)/shard_map/all_gather | solution.py:337
  702.6 28.4 %reduce-scatter.21.cloned.1.call-done = bf16[1,144,1024]{2,1,0:T(8,128)(2,1)} async-done(((bf16[1,576,1024]{2,1,0:T(8,128)(2,1)}), bf16[1,144,1024]{2,1,0:T(8,128)(2,1)}) %reduce-scatter.21.cloned.1.call-update) | async-done | bytes 294928 | tf_op jit(solution)/shard_map/reduce_scatter | solution.py:341
  735.9 27.5 %all-gather.31.cloned.1.call-done = bf16[1,576,1024]{2,1,0:T(8,128)(2,1)} async-done(((bf16[1,144,1024]{2,1,0:T(8,128)(2,1)}), bf16[1,576,1024]{2,1,0:T(8,128)(2,1)}) %all-gather.31.cloned.1.call-update) | async-done | bytes 1179664 | tf_op jit(solution)/shard_map/all_gather | solution.py:337
  769.8 25.1 %all-gather.33.cloned.1.call-done = bf16[1,576,1024]{2,1,0:T(8,128)(2,1)} async-done(((bf16[1,144,1024]{2,1,0:T(8,128)(2,1)}), bf16[1,576,1024]{2,1,0:T(8,128)(2,1)}) %all-gather.33.cloned.1.call-update) | async-done | bytes 1179664 | tf_op jit(solution)/shard_map/all_gather | solution.py:337
  804.8 8.8 collective-permute-done.23
  830.1 30.1 %reduce-scatter.23.cloned.1.call-done = bf16[1,144,1024]{2,1,0:T(8,128)(2,1)} async-done(((bf16[1,576,1024]{2,1,0:T(8,128)(2,1)}), bf16[1,144,1024]{2,1,0:T(8,128)(2,1)}) %reduce-scatter.23.cloned.1.call-update) | async-done | bytes 294928 | tf_op jit(solution)/shard_map/reduce_scatter | solution.py:341
  884.9 8.9 all-gather.35.cloned.1.call-done
  916.3 9.3 collective-permute-done.57
  1046.0 8.8 reduce-scatter.29.cloned.1.call-done
  1064.1 24.2 %all-gather.39.cloned.1.call-done = bf16[1,576,1024]{2,1,0:T(8,128)(2,1)} async-done(((bf16[1,144,1024]{2,1,0:T(8,128)(2,1)}), bf16[1,576,1024]{2,1,0:T(8,128)(2,1)}) %all-gather.39.cloned.1.call-update) | async-done | bytes 1179664 | tf_op jit(solution)/shard_map/all_gather | solution.py:337
  1187.2 9.8 all-to-all-done.3
  1219.4 16.0 %shard_map.362 = (bf16[1024,1536]{1,0:T(8,128)(2,1)}, bf16[4,1024,384]{2,1,0:T(8,128)(2,1)}) custom-call(bf16[1024,1536]{1,0:T(8,128)(2,1)} %all-gather.43.cloned.1.call-done.upstream_ref, bf16[1024,1536]{1,0:T(8,128)(2,1)} %get-tuple-element.48.slope_ref, bf16[1536,1536]{1,0:T(8,128)(2,1)} %get-tuple-element.361.first_ref, ...), custom_call_target="tpu_custom_call" | custom-call | tf_op jit(solution)/shard_map/pallas_call | solution.py:194
  1262.4 30.8 %reduce-scatter.33.cloned.1.call-done = bf16[1,1024,384]{2,1,0:T(8,128)(2,1)} async-done(((bf16[4,1024,384]{2,1,0:T(8,128)(2,1)}), bf16[1,1024,384]{2,1,0:T(8,128)(2,1)}) %reduce-scatter.33.cloned.1.call-update) | async-done | bytes 786448 | tf_op jit(solution)/shard_map/reduce_scatter | solution.py:345
  1369.9 9.2 collective-permute-done.64
  1393.4 16.0 %shard_map.365 = (bf16[1024,1536]{1,0:T(8,128)(2,1)}, bf16[4,1024,384]{2,1,0:T(8,128)(2,1)}) custom-call(bf16[1024,1536]{1,0:T(8,128)(2,1)} %all-gather.47.cloned.1.call-done.upstream_ref, bf16[1024,1536]{1,0:T(8,128)(2,1)} %get-tuple-element.50.slope_ref, bf16[1536,1536]{1,0:T(8,128)(2,1)} %get-tuple-element.362.first_ref, ...), custom_call_target="tpu_custom_call" | custom-call | tf_op jit(solution)/shard_map/pallas_call | solution.py:194
  1445.6 13.8 collective-permute-done.68
  1479.5 8.7 collective-permute-done.72
  1490.9 12.1 collective-permute-done.35
  1564.3 12.5 collective-permute-done.29
  (1238 shorter events, 829.1 us)
Async XLA Ops:
  7.2 194.8 %all-gather.17.cloned.1.call-start = ((), (), s32[]{:S(2)}) async-start(), calls=%async_computation.16 | async-start | bytes 3932160 | tf_op jit(solution)/shard_map/all_gather | solution.py:337
  13.9 109.2 %collective-permute-start.4 = (bf16[768,1536]{1,0:T(8,128)(2,1)}, bf16[768,1536]{1,0:T(8,128)(2,1)}, u32[]{:S(2)}, u32[]{:S(2)}) collective-permute-start(bf16[768,1536]{1,0:T(8,128)(2,1)} %dynamic-slice_bitcast_fusion.1), channel_id=1, source_target_pairs={{0,16},{16,0},{1,17},{17,1},{2,18},{18,2},{3,19},{19,3},{4,20},{20... | collective-permute-start | bytes 7077896 | tf_op jit(solution)/shard_map/ppermute | solution.py:285
  137.1 141.0 %reduce-scatter.13.cloned.1.call-start = ((), (), s32[]{:S(2)}) async-start(), calls=%async_computation.17 | async-start | bytes 3932160 | tf_op jit(solution)/shard_map/reduce_scatter | solution.py:345
  219.1 105.4 %all-gather.19.cloned.1.call-start = ((), (), s32[]{:S(2)}) async-start(), calls=%async_computation.18 | async-start | bytes 2211840 | tf_op jit(solution)/shard_map/all_gather | solution.py:337
  283.8 151.5 %all-gather.21.cloned.1.call-start = ((), (), s32[]{:S(2)}) async-start(), calls=%async_computation.19 | async-start | bytes 1474560 | tf_op jit(solution)/shard_map/all_gather | solution.py:337
  358.6 94.2 %all-gather.25.cloned.1.call-start = ((), (), s32[]{:S(2)}) async-start(), calls=%async_computation.23 | async-start | bytes 3932160 | tf_op jit(solution)/shard_map/all_gather | solution.py:337
  382.0 101.4 %reduce-scatter.15.cloned.1.call-start = ((), (), s32[]{:S(2)}) async-start(), calls=%async_computation.20 | async-start | bytes 1474560 | tf_op jit(solution)/shard_map/reduce_scatter | solution.py:341
  444.3 100.3 %reduce-scatter.19.cloned.1.call-start = ((), (), s32[]{:S(2)}) async-start(), calls=%async_computation.24 | async-start | bytes 3932160 | tf_op jit(solution)/shard_map/reduce_scatter | solution.py:345
  469.9 115.3 %all-gather.23.cloned.1.call-start = ((), (), s32[]{:S(2)}) async-start(), calls=%async_computation.21 | async-start | bytes 1474560 | tf_op jit(solution)/shard_map/all_gather | solution.py:337
  472.3 100.1 %collective-permute-start.16 = (bf16[512,1024]{1,0:T(8,128)(2,1)}, bf16[512,1024]{1,0:T(8,128)(2,1)}, u32[]{:S(2)}, u32[]{:S(2)}) collective-permute-start(bf16[512,1024]{1,0:T(8,128)(2,1)} %dynamic-slice_bitcast_fusion.2), channel_id=1, source_target_pairs={{0,16},{16,0},{1,17},{17,1},{2,18},{18,2},{3,19},{19,3},{4,20},{20... | collective-permute-start | bytes 3145736 | tf_op jit(solution)/shard_map/ppermute | solution.py:285
  474.9 97.6 %collective-permute-start.14 = (bf16[512,1024]{1,0:T(8,128)(2,1)}, bf16[512,1024]{1,0:T(8,128)(2,1)}, u32[]{:S(2)}, u32[]{:S(2)}) collective-permute-start(bf16[512,1024]{1,0:T(8,128)(2,1)} %dynamic-slice_bitcast_fusion.3), channel_id=1, source_target_pairs={{0,16},{16,0},{1,17},{17,1},{2,18},{18,2},{3,19},{19,3},{4,20},{20... | collective-permute-start | bytes 3145736 | tf_op jit(solution)/shard_map/ppermute | solution.py:285
  486.4 132.8 %all-gather.27.cloned.1.call-start = ((), (), s32[]{:S(2)}) async-start(), calls=%async_computation.25 | async-start | bytes 2211840 | tf_op jit(solution)/shard_map/all_gather | solution.py:337
  572.2 86.3 %reduce-scatter.17.cloned.1.call-start = ((), (), s32[]{:S(2)}) async-start(), calls=%async_computation.22 | async-start | bytes 1474560 | tf_op jit(solution)/shard_map/reduce_scatter | solution.py:341
  591.9 100.9 %all-gather.29.cloned.1.call-start = ((), (), s32[]{:S(2)}) async-start(), calls=%async_computation.26 | async-start | bytes 1474560 | tf_op jit(solution)/shard_map/all_gather | solution.py:337
  735.8 94.2 %reduce-scatter.25.cloned.1.call-start = ((), (), s32[]{:S(2)}) async-start(), calls=%async_computation.31 | async-start | bytes 1474560 | tf_op jit(solution)/shard_map/reduce_scatter | solution.py:341
  802.2 91.6 %all-gather.35.cloned.1.call-start = ((), (), s32[]{:S(2)}) async-start(), calls=%async_computation.32 | async-start | bytes 1474560 | tf_op jit(solution)/shard_map/all_gather | solution.py:337
  904.1 99.4 %all-gather.37.cloned.1.call-start = ((), (), s32[]{:S(2)}) async-start(), calls=%async_computation.34 | async-start | bytes 1474560 | tf_op jit(solution)/shard_map/all_gather | solution.py:337
  926.6 221.2 %collective-permute-start.59 = (bf16[1024,256]{1,0:T(8,128)(2,1)}, bf16[1024,256]{1,0:T(8,128)(2,1)}, u32[]{:S(2)}, u32[]{:S(2)}) collective-permute-start(bf16[1024,256]{1,0:T(8,128)(2,1)} %fusion.163), channel_id=1, source_target_pairs={{0,16},{1,17},{2,18},{3,19},{4,20},{5,21},{6,22},{7,23},{8,24},{9,... | collective-permute-start | bytes 1572872 | tf_op jit(solution)/shard_map/ppermute | solution.py:385
  936.9 217.7 %collective-permute-start.53 = (bf16[256,1024]{1,0:T(8,128)(2,1)}, bf16[256,1024]{1,0:T(8,128)(2,1)}, u32[]{:S(2)}, u32[]{:S(2)}) collective-permute-start(bf16[256,1024]{1,0:T(8,128)(2,1)} %fusion.161), channel_id=1, source_target_pairs={{0,16},{1,17},{2,18},{3,19},{4,20},{5,21},{6,22},{7,23},{8,24},{9,... | collective-permute-start | bytes 1572872 | tf_op jit(solution)/shard_map/ppermute | solution.py:385
  1002.0 129.8 %collective-permute-start.83 = (bf16[384,256]{1,0:T(8,128)(2,1)}, bf16[384,256]{1,0:T(8,128)(2,1)}, u32[]{:S(2)}, u32[]{:S(2)}) collective-permute-start(bf16[384,256]{1,0:T(8,128)(2,1)} %split.279), channel_id=1, source_target_pairs={{0,8},{4,12},{8,0},{12,4},{1,9},{5,13},{9,1},{13,5},{2,10},{6,14},... | collective-permute-start | bytes 589832 | tf_op jit(solution)/shard_map/ppermute | solution.py:285
  1009.7 100.7 %collective-permute-start.54 = (bf16[1024,512]{1,0:T(8,128)(2,1)}, bf16[1024,512]{1,0:T(8,128)(2,1)}, u32[]{:S(2)}, u32[]{:S(2)}) collective-permute-start(bf16[1024,512]{1,0:T(8,128)(2,1)} %split.249), channel_id=1, source_target_pairs={{0,4},{4,0},{8,12},{12,8},{1,5},{5,1},{9,13},{13,9},{2,6},{6,2},{1... | collective-permute-start | bytes 3145736 | tf_op jit(solution)/shard_map/ppermute | solution.py:285
  1022.1 96.4 %collective-permute-start.48 = (bf16[512,1024]{1,0:T(8,128)(2,1)}, bf16[512,1024]{1,0:T(8,128)(2,1)}, u32[]{:S(2)}, u32[]{:S(2)}) collective-permute-start(bf16[512,1024]{1,0:T(8,128)(2,1)} %split.241), channel_id=1, source_target_pairs={{0,4},{4,0},{8,12},{12,8},{1,5},{5,1},{9,13},{13,9},{2,6},{6,2},{1... | collective-permute-start | bytes 3145736 | tf_op jit(solution)/shard_map/ppermute | solution.py:285
  1059.0 108.0 %reduce-scatter.31.cloned.1.call-start = ((), (), s32[]{:S(2)}) async-start(), calls=%async_computation.37 | async-start | bytes 1474560 | tf_op jit(solution)/shard_map/reduce_scatter | solution.py:341
  1098.6 109.1 %all-gather.43.cloned.1.call-start = ((), (), s32[]{:S(2)}) async-start(), calls=%async_computation.39 | async-start | bytes 3932160 | tf_op jit(solution)/shard_map/all_gather | solution.py:337
  1145.5 188.6 %collective-permute-start.41 = (bf16[256,768]{0,1:T(8,128)(2,1)}, bf16[256,768]{0,1:T(8,128)(2,1)}, u32[]{:S(2)}, u32[]{:S(2)}) collective-permute-start(bf16[256,768]{0,1:T(8,128)(2,1)} %fusion.193), channel_id=1, source_target_pairs={{0,16},{1,17},{2,18},{3,19},{4,20},{5,21},{6,22},{7,23},{8,24},{9,... | collective-permute-start | bytes 1179656 | tf_op jit(solution)/shard_map/ppermute | solution.py:385
  1147.8 282.6 %collective-permute-start.85 = (bf16[384,256]{1,0:T(8,128)(2,1)}, bf16[384,256]{1,0:T(8,128)(2,1)}, u32[]{:S(2)}, u32[]{:S(2)}) collective-permute-start(bf16[384,256]{1,0:T(8,128)(2,1)} %fusion.227), channel_id=1, source_target_pairs={{0,16},{1,17},{2,18},{3,19},{4,20},{5,21},{6,22},{7,23},{8,24},{9,... | collective-permute-start | bytes 589832 | tf_op jit(solution)/shard_map/ppermute | solution.py:385
  1202.2 91.0 %reduce-scatter.33.cloned.1.call-start = ((), (), s32[]{:S(2)}) async-start(), calls=%async_computation.40 | async-start | bytes 3932160 | tf_op jit(solution)/shard_map/reduce_scatter | solution.py:345
  1206.6 123.6 %collective-permute-start.37 = (bf16[256,768]{0,1:T(8,128)(2,1)}, bf16[256,768]{0,1:T(8,128)(2,1)S(1)}, u32[]{:S(2)}, u32[]{:S(2)}) collective-permute-start(bf16[256,768]{0,1:T(8,128)(2,1)} %split.227), channel_id=1, source_target_pairs={{0,8},{4,12},{8,0},{12,4},{1,9},{5,13},{9,1},{13,5},{2,10},{6,14},... | collective-permute-start | bytes 1179656 | tf_op jit(solution)/shard_map/ppermute | solution.py:285
  1219.4 168.8 %collective-permute-start.73 = (bf16[1536,768]{1,0:T(8,128)(2,1)}, bf16[1536,768]{1,0:T(8,128)(2,1)}, u32[]{:S(2)}, u32[]{:S(2)}) collective-permute-start(bf16[1536,768]{1,0:T(8,128)(2,1)} %split.269), channel_id=1, source_target_pairs={{0,4},{4,0},{8,12},{12,8},{1,5},{5,1},{9,13},{13,9},{2,6},{6,2},{1... | collective-permute-start | bytes 7077896 | tf_op jit(solution)/shard_map/ppermute | solution.py:285
  1235.5 157.9 %all-gather.47.cloned.1.call-start = ((), (), s32[]{:S(2)}) async-start(), calls=%async_computation.42 | async-start | bytes 3932160 | tf_op jit(solution)/shard_map/all_gather | solution.py:337
  1318.8 196.2 %reduce-scatter.35.cloned.1.call-start = ((), (), s32[]{:S(2)}) async-start(), calls=%async_computation.43 | async-start | bytes 3932160 | tf_op jit(solution)/shard_map/reduce_scatter | solution.py:345
  1330.1 97.8 %collective-permute-start.67 = (bf16[768,1536]{1,0:T(8,128)(2,1)}, bf16[768,1536]{1,0:T(8,128)(2,1)}, u32[]{:S(2)}, u32[]{:S(2)}) collective-permute-start(bf16[768,1536]{1,0:T(8,128)(2,1)} %split.261), channel_id=1, source_target_pairs={{0,4},{4,0},{8,12},{12,8},{1,5},{5,1},{9,13},{13,9},{2,6},{6,2},{1... | collective-permute-start | bytes 7077896 | tf_op jit(solution)/shard_map/ppermute | solution.py:285
  (316 other events, 5554.9 us)
Sparse Core Ops, SparseCore 0:
  137.2 64.8 all-gather.16
  219.2 58.8 reduce-scatter.12
  283.9 40.5 all-gather.18
  358.7 29.5 all-gather.20
  390.4 62.4 all-gather.24
  455.6 27.7 reduce-scatter.14
  485.7 58.9 reduce-scatter.18
  546.8 30.4 all-gather.22
  579.5 39.6 all-gather.26
  621.4 32.7 reduce-scatter.16
  662.4 30.3 all-gather.28
  702.7 28.2 reduce-scatter.20
  734.2 29.1 all-gather.30
  765.4 29.5 all-gather.32
  801.7 28.2 reduce-scatter.24
  832.2 27.8 reduce-scatter.22
  864.6 29.1 all-gather.34
  904.2 28.2 reduce-scatter.26
  950.5 31.7 all-gather.36
  994.2 30.6 all-gather.40
  1027.2 27.4 reduce-scatter.28
  1059.1 29.1 all-gather.38
  1098.8 28.1 reduce-scatter.30
  1128.9 68.2 all-gather.42
  1202.3 29.3 all-gather.44
  1235.6 57.5 reduce-scatter.32
  1319.0 66.0 all-gather.46
  1409.6 60.8 reduce-scatter.34

commit v3 on v2

v3 whole, which is shorter than its diff:
```python
import functools
import math

import jax
import jax.numpy as jnp
from jax import lax
from jax.experimental import pallas as pl
from jax.experimental.pallas import tpu as pltpu
from jax.sharding import PartitionSpec as P

PIPE, DP, TENSOR = ("pipe", "dp", "tensor")
HEAD_DIM = 64
LANES = 128
MARGIN = 8
BAND = 4
F32 = jnp.float32
BF16 = jnp.bfloat16


def product(left, right, left_axis, right_axis):
    return lax.dot_general(
        left, right, (((left_axis,), (right_axis,)), ((), ())), preferred_element_type=F32
    )


ANYWHERE = pl.BlockSpec(memory_space=pl.ANY)


def settings(mebibytes):
    return pltpu.CompilerParams(vmem_limit_bytes=mebibytes << 20)


def run(kernel, args, in_specs, mebibytes, later_than=(), **rest):
    count, extra = (len(args), len(later_than))

    def without_extra(*refs):
        kernel(*refs[:count], *refs[count + extra :])

    return pl.pallas_call(
        without_extra,
        in_specs=list(in_specs) + [ANYWHERE] * extra,
        compiler_params=settings(mebibytes),
        **rest,
    )(*args, *later_than)


def after(array, *earlier):
    def nothing(*refs):
        return None

    return pl.pallas_call(
        nothing,
        in_specs=[ANYWHERE] * (1 + len(earlier)),
        out_specs=ANYWHERE,
        out_shape=jax.ShapeDtypeStruct(array.shape, array.dtype),
        input_output_aliases={0: 0},
    )(array, *earlier)


def fill_padded(padded, values):
    extent = values.shape[0]
    half = (padded.shape[0] - extent) // 2
    padded[...] = jnp.zeros_like(padded)
    padded[half : half + extent, MARGIN : MARGIN + extent, :] = values.astype(F32)


def windows_of(padded, first, side, extent):
    for col in range(side):
        start = MARGIN - side // 2 + col
        yield col, padded[pl.ds(first, BAND + side - 1), pl.ds(start, extent), :]


def mix_kernel(side, reverse, with_base, *refs):
    x_ref, kernel_ref = refs[:2]
    out_ref, padded = refs[-2:]
    extent = x_ref.shape[1]
    fill_padded(padded, x_ref[0])

    def band(step, carry):
        first = step * BAND
        if with_base:
            total = refs[2][0, pl.ds(first, BAND)]
        else:
            total = jnp.zeros((BAND, extent, x_ref.shape[3]), F32)
        for col, window in windows_of(padded, first, side, extent):
            for row in range(side):
                tap = row * side + col
                weight = kernel_ref[side * side - 1 - tap if reverse else tap]
                total = total + window[row : row + BAND] * weight
        out_ref[0, pl.ds(first, BAND)] = total.astype(out_ref.dtype)
        return carry

    lax.fori_loop(0, extent // BAND, band, 0)


def depthwise(grid, kernel, side, base=None, reverse=False, dtype=F32, later_than=()):
    images, extent, _, channels = grid.shape
    block = pl.BlockSpec((1, extent, extent, LANES), lambda n, c: (n, 0, 0, c))
    taps = pl.BlockSpec((side * side, LANES), lambda n, c: (0, c))
    extra = () if base is None else (base,)
    return run(
        functools.partial(mix_kernel, side, reverse, base is not None),
        (grid, kernel) + extra,
        [block, taps] + [block] * len(extra),
        32,
        later_than,
        grid=(images, channels // LANES),
        out_specs=block,
        out_shape=jax.ShapeDtypeStruct(grid.shape, dtype),
        scratch_shapes=[pltpu.VMEM((extent + side - 1, extent + 2 * MARGIN, LANES), F32)],
    )


def taps_kernel(side, x_ref, upstream_ref, out_ref, padded, sums):
    extent = x_ref.shape[1]
    fill_padded(padded, x_ref[0])
    sums[...] = jnp.zeros_like(sums)

    def band(step, carry):
        first = step * BAND
        upstream = upstream_ref[0, pl.ds(first, BAND)]
        for col, window in windows_of(padded, first, side, extent):
            for row in range(side):
                part = window[row : row + BAND] * upstream
                sums[row * side + col] += jnp.sum(part.reshape(-1, 8, LANES), 0)
        return carry

    lax.fori_loop(0, extent // BAND, band, 0)
    out_ref[0] = jnp.sum(sums[...], 1)


def depthwise_taps(grid, upstream, side, later_than=()):
    images, extent, _, channels = grid.shape
    block = pl.BlockSpec((1, extent, extent, LANES), lambda n, c: (n, 0, 0, c))
    sums = run(
        functools.partial(taps_kernel, side),
        (grid, upstream),
        [block, block],
        32,
        later_than,
        grid=(images, channels // LANES),
        out_specs=pl.BlockSpec((1, side * side, LANES), lambda n, c: (n, 0, c)),
        out_shape=jax.ShapeDtypeStruct((images, side * side, channels), F32),
        scratch_shapes=[
            pltpu.VMEM((extent + side - 1, extent + 2 * MARGIN, LANES), F32),
            pltpu.VMEM((side * side, 8, LANES), F32),
        ],
    )
    return jnp.sum(sums, 0)


def gelu_and_slope(values):
    cumulative = 0.5 * (1.0 + lax.erf(values * (1.0 / math.sqrt(2.0))))
    density = jnp.exp(-0.5 * values * values) * (1.0 / math.sqrt(2.0 * math.pi))
    return ((values * cumulative).astype(BF16), (cumulative + values * density).astype(BF16))


def mlp_kernel(step, x_ref, first_ref, second_ref, hidden_ref, slope_ref, out_ref):
    x = x_ref[...]
    total = None
    for at in range(0, first_ref.shape[1], step):
        units = slice(at, at + step)
        hidden, slope = gelu_and_slope(product(x, first_ref[:, units], 1, 0))
        hidden_ref[:, units] = hidden
        slope_ref[:, units] = slope
        part = product(hidden, second_ref[units, :], 1, 0)
        total = part if total is None else total + part
    out_ref[...] = total.astype(BF16)


def mlp_back_kernel(step, upstream_ref, slope_ref, first_ref, second_ref, grad_ref, out_ref):
    upstream = upstream_ref[...]
    total = None
    for at in range(0, first_ref.shape[1], step):
        units = slice(at, at + step)
        grad = product(upstream, second_ref[units, :], 1, 1) * slope_ref[:, units].astype(F32)
        grad = grad.astype(BF16)
        grad_ref[:, units] = grad
        part = product(grad, first_ref[:, units], 1, 1)
        total = part if total is None else total + part
    out_ref[...] = total.astype(BF16)


QUARTERS = 4


def load_weight(meta_ref, sources, held_ref, semaphores):
    own, got, pair, rest = sources
    size = held_ref.shape[0] // QUARTERS
    rows = [pl.ds(k * size, size) for k in range(QUARTERS)]
    traded_quarters = [(got, 0, 0), (pair, 0, 2), (rest, 0, 1), (rest, 1, 3)]

    @pl.when(meta_ref[0] == 1)
    def _():
        for k in range(QUARTERS):
            pltpu.make_async_copy(
                own.at[rows[k]], held_ref.at[rows[k]], semaphores.at[k]
            ).start()

    @pl.when(meta_ref[0] != 1)
    def _():
        for k, (source, at, relative) in enumerate(traded_quarters):
            start = pl.multiple_of(lax.bitwise_xor(meta_ref[1], relative) * size, 16)
            pltpu.make_async_copy(
                source.at[rows[at]], held_ref.at[pl.ds(start, size)], semaphores.at[k]
            ).start()

    return [
        pltpu.make_async_copy(own.at[rows[k]], held_ref.at[rows[k]], semaphores.at[k])
        for k in range(QUARTERS)
    ]


def store_parts(out_ref, total):
    width = out_ref.shape[2]
    for part in range(out_ref.shape[0]):
        out_ref[part] = total[:, part * width : (part + 1) * width].astype(BF16)


def wide_mlp_kernel(back, step, meta_ref, *refs):
    inputs, refs = (refs[: 2 if back else 1], refs[2 if back else 1 :])
    sources, refs = ((refs[:4], refs[4:8]), refs[8:])
    inside, (out_ref, first_ref, second_ref, sems) = (refs[:-4], refs[-4:])

    @pl.when(pl.program_id(0) == 0)
    def _():
        copies = load_weight(meta_ref, sources[0], first_ref, sems.at[0])
        copies += load_weight(meta_ref, sources[1], second_ref, sems.at[1])
        for copy in copies:
            copy.wait()

    x = inputs[0][...]
    total = None
    for at in range(0, first_ref.shape[1], step):
        units = slice(at, at + step)
        if back:
            value = product(x, second_ref[units, :], 1, 1) * inputs[1][:, units].astype(F32)
            value = value.astype(BF16)
            part = product(value, first_ref[:, units], 1, 1)
        else:
            value, slope = gelu_and_slope(product(x, first_ref[:, units], 1, 0))
            inside[1][:, units] = slope
            part = product(value, second_ref[units, :], 1, 0)
        inside[0][:, units] = value
        total = part if total is None else total + part
    store_parts(out_ref, total)


def wide_mlp(layer, x, first, second, tile, slope=None, later_than=()):
    rows, units = (x.shape[0], first[0].shape[1])
    count = lax.axis_size(TENSOR)
    back = slope is not None
    meta = jnp.stack(
        [(lax.axis_index(PIPE) == layer).astype(jnp.int32), lax.axis_index(DP) % QUARTERS]
    )
    x_spec = pl.BlockSpec((tile, x.shape[1]), lambda i, s: (i, 0))
    units_spec = pl.BlockSpec((tile, units), lambda i, s: (i, 0))
    width = first[0].shape[0] // count
    inside = 1 if back else 2
    args = [x] + ([slope] if back else []) + list(first) + list(second)
    taken, extra = (len(args), len(later_than))
    kernel = functools.partial(wide_mlp_kernel, back, largest_step(units))

    def without_extra(meta_ref, *refs):
        kernel(meta_ref, *refs[:taken], *refs[taken + extra :])

    out = pl.pallas_call(
        without_extra,
        grid_spec=pltpu.PrefetchScalarGridSpec(
            num_scalar_prefetch=1,
            grid=(rows // tile,),
            in_specs=[x_spec] + [units_spec] * back + [ANYWHERE] * (8 + extra),
            out_specs=[units_spec] * inside
            + [pl.BlockSpec((count, tile, width), lambda i, s: (0, i, 0))],
            scratch_shapes=[
                pltpu.VMEM(first[0].shape, BF16),
                pltpu.VMEM(second[0].shape, BF16),
                pltpu.SemaphoreType.DMA((2, QUARTERS)),
            ],
        ),
        out_shape=[jax.ShapeDtypeStruct((rows, units), BF16)] * inside
        + [jax.ShapeDtypeStruct((count, rows, width), BF16)],
        compiler_params=settings(56),
    )(meta, *args, *later_than)
    return (out[:-1], out[-1])


def largest_step(units):
    return 512 if units % 512 == 0 else units


def mlp(x, first, second, later_than=()):
    rows, units = (x.shape[0], first.shape[1])
    args = (x, first, second)
    shapes = [(rows, units), (rows, units), (rows, second.shape[1])]
    return run(
        functools.partial(mlp_kernel, largest_step(units)),
        args,
        [pl.BlockSpec(arg.shape, lambda: (0, 0)) for arg in args],
        56,
        later_than,
        out_specs=[pl.BlockSpec(shape, lambda: (0, 0)) for shape in shapes],
        out_shape=[jax.ShapeDtypeStruct(shape, BF16) for shape in shapes],
    )


def mlp_back(upstream, slope, first, second, later_than=()):
    args = (upstream, slope, first, second)
    shapes = [slope.shape, (slope.shape[0], first.shape[0])]
    return run(
        functools.partial(mlp_back_kernel, largest_step(slope.shape[1])),
        args,
        [pl.BlockSpec(arg.shape, lambda: (0, 0)) for arg in args],
        56,
        later_than,
        out_specs=[pl.BlockSpec(shape, lambda: (0, 0)) for shape in shapes],
        out_shape=[jax.ShapeDtypeStruct(shape, BF16) for shape in shapes],
    )


def head_probs(query, keys, mask):
    scores = product(query, keys, 1, 1) * (HEAD_DIM**-0.5)
    scores = jnp.where(mask > 0, scores, -1000000000.0)
    raised = jnp.exp(scores - jnp.max(scores, -1, keepdims=True))
    return raised * (1.0 / jnp.sum(raised, -1, keepdims=True))


def lane_pairs(width):
    for pair in range(width // LANES):
        yield [slice(at + pair * LANES, at + (pair + 1) * LANES) for at in (0, width, 2 * width)]


def heads_of(pair):
    return [pair[:, at : at + HEAD_DIM] for at in range(0, LANES, HEAD_DIM)]


def attend_kernel(project_ref, mask_ref, out_ref):
    mask = mask_ref[0]
    for places in lane_pairs(out_ref.shape[2]):
        query, keys, values = (heads_of(project_ref[0, :, at]) for at in places)
        parts = [
            product(head_probs(q, k, mask).astype(BF16), u, 1, 0).astype(BF16)
            for q, k, u in zip(query, keys, values)
        ]
        out_ref[0, :, places[0]] = jnp.concatenate(parts, 1)


def attend(project, mask, later_than=()):
    images, tokens, wide = project.shape
    width = wide // 3
    return run(
        attend_kernel,
        (project, mask[:, None, :]),
        [
            pl.BlockSpec((1, tokens, wide), lambda i: (i, 0, 0)),
            pl.BlockSpec((1, 1, tokens), lambda i: (i, 0, 0)),
        ],
        48,
        later_than,
        grid=(images,),
        out_specs=pl.BlockSpec((1, tokens, width), lambda i: (i, 0, 0)),
        out_shape=jax.ShapeDtypeStruct((images, tokens, width), BF16),
    )


def attend_back_kernel(project_ref, mask_ref, upstream_ref, out_ref):
    mask = mask_ref[0]
    scale = HEAD_DIM**-0.5
    for places in lane_pairs(upstream_ref.shape[2]):
        query, keys, values = (heads_of(project_ref[0, :, at]) for at in places)
        upstream = heads_of(upstream_ref[0, :, places[0]])
        grads = ([], [], [])
        for q, k, u, d in zip(query, keys, values, upstream):
            exact = head_probs(q, k, mask)
            grad_probs = product(d, u, 1, 1)
            held = jnp.sum(grad_probs * exact, -1, keepdims=True)
            grad_scores = (exact * (grad_probs - held)).astype(BF16)
            grads[0].append((product(grad_scores, k, 1, 0) * scale).astype(BF16))
            grads[1].append((product(grad_scores, q, 0, 0) * scale).astype(BF16))
            grads[2].append(product(exact.astype(BF16), d, 0, 0).astype(BF16))
        for at, parts in zip(places, grads):
            out_ref[0, :, at] = jnp.concatenate(parts, 1)


def attend_back(project, mask, upstream, later_than=()):
    images, tokens, wide = project.shape
    width = wide // 3
    whole = pl.BlockSpec((1, tokens, wide), lambda i: (i, 0, 0))
    return run(
        attend_back_kernel,
        (project, mask[:, None, :], upstream),
        [
            whole,
            pl.BlockSpec((1, 1, tokens), lambda i: (i, 0, 0)),
            pl.BlockSpec((1, tokens, width), lambda i: (i, 0, 0)),
        ],
        48,
        later_than,
        grid=(images,),
        out_specs=whole,
        out_shape=jax.ShapeDtypeStruct(project.shape, BF16),
    )


def residual_kernel(feature_ref, branch_ref, gain_ref, out_ref, pooled_ref, rows):
    total = feature_ref[0].astype(F32) + gain_ref[0] * branch_ref[0].astype(F32)
    out_ref[0] = total.astype(BF16)
    groups = total.shape[0] // 4
    for group in range(groups):
        for part in range(3):
            fine = 4 * group + part
            rows[3 * group + part] = 0.5 * (total[fine] + total[fine + 1])
    columns = [rows[:, pl.ds(part, groups, stride=4), :] for part in range(4)]
    for part in range(3):
        pooled_ref[0, :, pl.ds(part, groups, stride=3), :] = 0.5 * (columns[part] + columns[part + 1])


def residual_and_pool(feature, branch, gain, later_than=()):
    images, fine, _, channels = feature.shape
    coarse = fine // 4 * 3
    block = pl.BlockSpec((1, fine, fine, LANES), lambda n, c: (n, 0, 0, c))
    out, pooled = run(
        residual_kernel,
        (feature, branch, gain[None]),
        [block, block, pl.BlockSpec((1, LANES), lambda n, c: (0, c))],
        32,
        later_than,
        grid=(images, channels // LANES),
        out_specs=[block, pl.BlockSpec((1, coarse, coarse, LANES), lambda n, c: (n, 0, 0, c))],
        out_shape=[
            jax.ShapeDtypeStruct(feature.shape, BF16),
            jax.ShapeDtypeStruct((images, coarse, coarse, channels), F32),
        ],
        scratch_shapes=[pltpu.VMEM((coarse, fine, LANES), F32)],
    )
    return (out, pooled.astype(BF16))


def spread_back_kernel(pooled_ref, upstream_ref, gain_ref, out_ref, scaled_ref, rows):
    groups = upstream_ref.shape[1] // 4
    columns = [pooled_ref[0, :, pl.ds(part, groups, stride=3), :] for part in range(3)]
    for part in range(4):
        near = [columns[at] for at in (part - 1, part) if 0 <= at < 3]
        rows[:, pl.ds(part, groups, stride=4), :] = 0.5 * sum(near[1:], near[0])
    for group in range(groups):
        for part in range(4):
            near = [rows[3 * group + at] for at in (part - 1, part) if 0 <= at < 3]
            total = upstream_ref[0, 4 * group + part].astype(F32) + 0.5 * sum(near[1:], near[0])
            out_ref[0, 4 * group + part] = total
            scaled_ref[0, 4 * group + part] = (gain_ref[0] * total).astype(BF16)


def spread_back(pooled, upstream, gain, later_than=()):
    images, fine, _, channels = upstream.shape
    coarse = pooled.shape[1]
    block = pl.BlockSpec((1, fine, fine, LANES), lambda n, c: (n, 0, 0, c))
    return run(
        spread_back_kernel,
        (pooled, upstream, gain[None]),
        [
            pl.BlockSpec((1, coarse, coarse, LANES), lambda n, c: (n, 0, 0, c)),
            block,
            pl.BlockSpec((1, LANES), lambda n, c: (0, c)),
        ],
        32,
        later_than,
        grid=(images, channels // LANES),
        out_specs=[block, block],
        out_shape=[
            jax.ShapeDtypeStruct(upstream.shape, F32),
            jax.ShapeDtypeStruct(upstream.shape, BF16),
        ],
        scratch_shapes=[pltpu.VMEM((coarse, fine, LANES), F32)],
    )


def add_kernel(kept_ref, got_ref, out_ref):
    out_ref[...] = (kept_ref[...].astype(F32) + got_ref[...].astype(F32)).astype(BF16)


def add_to_first_half(partial, got, later_than=()):
    rows, width = got.shape
    tile = math.gcd(rows, 256)
    if tile % 16:
        return (partial[:rows].astype(F32) + got.astype(F32)).astype(BF16)
    block = pl.BlockSpec((tile, width), lambda i: (i, 0))
    return run(
        add_kernel,
        (partial, got),
        [block, block],
        32,
        later_than,
        grid=(rows // tile,),
        out_specs=block,
        out_shape=jax.ShapeDtypeStruct(got.shape, BF16),
    )


class Held:
    def __init__(self, **arrays):
        self.add(**arrays)

    def add(self, **arrays):
        vars(self).update(arrays)


def traded(array, axis, bit):
    return lax.ppermute(array, axis, [(i, i ^ bit) for i in range(lax.axis_size(axis))])


def bits_of(axis):
    return [1 << k for k in range((lax.axis_size(axis) - 1).bit_length())]


def total_over(values, axis):
    for bit in bits_of(axis):
        values = values + traded(values, axis, bit)
    return values


def first_section():
    return lax.axis_index(PIPE) == 0


def select(former, latter):
    return jnp.where(first_section(), former, latter)


def halves_of(own, axis):
    half = own.shape[axis] // 2
    odd = lax.axis_index(DP) % 2
    return lax.dynamic_slice_in_dim(own, odd * half, half, axis)


def joined(mine, theirs, axis):
    even = lax.axis_index(DP) % 2 == 0
    return jnp.concatenate([jnp.where(even, mine, theirs), jnp.where(even, theirs, mine)], axis)


class Trade:
    def __init__(self, own, *earlier):
        self.own = own
        self.got = traded(after(halves_of(own, 0), *earlier), PIPE, 1)

    def share(self, *earlier):
        self.got = after(self.got, *earlier)
        self.rest = traded(self.got, DP, 1)

    def layers(self, *earlier):
        rest = after(self.rest, *earlier) if earlier else self.rest
        other = joined(self.got, rest, 0)
        return (select(self.own, other), select(other, self.own))


class QuarterTrade:
    def __init__(self, own, *earlier):
        size = own.shape[0] // QUARTERS
        sent = lax.dynamic_slice_in_dim(own, lax.axis_index(DP) % QUARTERS * size, size, 0)
        self.own = own
        self.got = traded(after(sent, *earlier), PIPE, 1)

    def share(self, *earlier):
        self.got = after(self.got, *earlier)
        self.pair = traded(self.got, DP, 2)

    def share_again(self, *earlier):
        self.pair = after(self.pair, *earlier)
        self.rest = traded(jnp.concatenate([self.got, self.pair], 0), DP, 1)

    def pieces(self):
        return (self.own, self.got, self.pair, self.rest)


def small_pair(own):
    other = traded(own, PIPE, 1)
    return (select(own, other), select(other, own))


def own_block(values, count, axis):
    return lax.dynamic_slice_in_dim(values, lax.axis_index(TENSOR) * count, count, axis)


def widen(values, whole, axis):
    shape = list(values.shape)
    shape[axis] = whole
    empty = jnp.zeros(tuple(shape), F32)
    return lax.dynamic_update_slice_in_dim(
        empty, values, lax.axis_index(TENSOR) * values.shape[axis], axis
    )


def gather(values):
    return lax.all_gather(values, TENSOR, axis=1, tiled=True)


def turned(values, by):
    count = lax.axis_size(TENSOR)
    return lax.ppermute(values, TENSOR, [(i, (i + by) % count) for i in range(count)])


def ring_total(values):
    count = lax.axis_size(TENSOR)
    return sum([turned(values, k) for k in range(1, count)], values)


def in_order(blocks, axis):
    count = len(blocks)
    size = blocks[0].shape[axis]
    start = (count - 1 - lax.axis_index(TENSOR)) * size
    joined = jnp.concatenate(blocks[::-1] + blocks[:0:-1], axis)
    return lax.dynamic_slice_in_dim(joined, start, count * size, axis)


def exchanged(values, split_axis, concat_axis):
    count = lax.axis_size(TENSOR)
    index = lax.axis_index(TENSOR)
    size = values.shape[split_axis] // count
    blocks = []
    for k in range(count):
        start = (index + k) % count * size
        block = lax.dynamic_slice_in_dim(values, start, size, split_axis)
        blocks.append(turned(block, k) if k else block)
    return in_order(blocks, concat_axis)


def ring_gather(values):
    blocks = [turned(values, k) if k else values for k in range(lax.axis_size(TENSOR))]
    return in_order(blocks, 1)


def tokens_to_holders(values):
    return exchanged(values, 1, 2)


def features_to_holders(values):
    return exchanged(values, 2, 1)


def scatter_tokens(values):
    return lax.psum_scatter(values, TENSOR, scatter_dimension=1, tiled=True).astype(F32)


def scatter_parts(parts):
    return lax.psum_scatter(parts, TENSOR, scatter_dimension=0, tiled=False).astype(F32)


def relative_order(count):
    width = (count - 1).bit_length()
    return sorted(range(count), key=lambda r: format(r, f"0{width}b")[::-1])


def by_relative(values, axis=DP):
    count = lax.axis_size(axis)
    index = lax.axis_index(axis)
    block = values.shape[1] // count
    return jnp.concatenate(
        [
            lax.dynamic_slice_in_dim(values, (index ^ r) * block, block, 1)
            for r in relative_order(count)
        ],
        1,
    )


def inner(left, right, *earlier):
    left = by_relative(left)
    if earlier:
        left = after(left, *earlier)
    return product(left, right, 0, 0).astype(BF16)


class Reduction:
    def __init__(self, partial, also_tensor=False):
        self.partial = partial
        self.steps_left = 4 if also_tensor else 2
        self.moves = [(DP, bit, 0) for bit in bits_of(DP)]
        if also_tensor:
            self.moves += [(TENSOR, bit, 1) for bit in bits_of(TENSOR)]
        self.send()

    def send(self):
        name, bit, axis = self.moves.pop(0)
        size = self.partial.shape[axis] // 2
        self.got = traded(lax.slice_in_dim(self.partial, size, 2 * size, axis=axis), name, bit)

    def step(self, *earlier):
        halvings = -(-(len(self.moves) + 1) // self.steps_left)
        self.steps_left -= 1
        for _ in range(halvings):
            self.partial = add_to_first_half(self.partial, self.got, earlier)
            if self.moves:
                self.send()
        return self.partial


def over_sections(former, latter):
    kept, sent = (select(former, latter), select(latter, former))
    return kept.astype(F32) + traded(sent, PIPE, 1).astype(F32)


def norm_rows(values, epsilon):
    centred = values - jnp.mean(values, -1, keepdims=True)
    inverse = lax.rsqrt(jnp.mean(centred * centred, -1, keepdims=True) + epsilon)
    return (centred * inverse, inverse)


def norm_back(upstream, scaled, inverse, gains):
    weighted = upstream * gains
    return inverse * (
        weighted
        - jnp.mean(weighted, -1, keepdims=True)
        - scaled * jnp.mean(weighted * scaled, -1, keepdims=True)
    )


def flat(values):
    return values.reshape(-1, values.shape[-1])


def placing(places):
    cells = jnp.arange(places.shape[1])
    return (places[:, :, None] == cells[None, None, :]).astype(BF16)


def conv_norm(grid, w, later_than=()):
    own = grid.shape[-1]
    channels = own * lax.axis_size(TENSOR)
    mixed = flat(depthwise(grid, w.dw, 7, later_than=later_than))
    sums = ring_total(jnp.stack([jnp.sum(mixed, -1), jnp.sum(mixed * mixed, -1)]))
    centre = sums[0] / channels
    inverse = lax.rsqrt(sums[1] / channels - centre * centre + 1e-06)
    scaled = (mixed - centre[:, None]) * inverse[:, None]
    normed = (scaled * w.gain[0] + w.shift).astype(BF16)
    return (normed, Held(grid=grid, scaled=scaled, inverse=inverse))


def conv_residual(grid, branch, w, *earlier):
    own = grid.shape[-1]
    channels = own * lax.axis_size(TENSOR)
    out, pooled = residual_and_pool(grid, branch.reshape(grid.shape), w.gain[1], earlier)
    exact = grid.astype(F32) + w.gain[1] * branch.reshape(grid.shape).astype(F32)
    square = jnp.sum(exact * exact, -1).reshape(grid.shape[0], -1)
    return (out, flat(pooled), square / channels)


def adapter_forward(stream, pooled, places, w, *earlier):
    images, tokens, _ = places.shape
    side = math.isqrt(tokens)
    pooled_rows = tokens_to_holders(pooled.reshape(images, tokens, -1))
    adapted_rows = product(flat(pooled_rows), w.proj, 1, 0).astype(BF16)
    adapted = features_to_holders(adapted_rows.reshape(pooled_rows.shape[:2] + (-1,)))
    adapted = adapted.reshape(images, side, side, -1)
    spread = depthwise(adapted, w.taps, 3, later_than=earlier).reshape(images, tokens, -1)
    gated = (jnp.tanh(w.gate) * spread).astype(BF16)
    picked = jnp.einsum("ntc,ncw->ntw", places, gated, preferred_element_type=F32).astype(BF16)
    stream_in = stream + tokens_to_holders(picked).astype(F32)
    return (stream_in, Held(pooled=flat(pooled_rows), adapted=adapted, spread=spread))


def vit_norm(stream, w, which):
    scaled, inverse = norm_rows(stream, 1e-05)
    normed = (scaled * w.vit_gain[which] + w.vit_shift[which]).astype(BF16)
    return (normed, scaled, inverse)


def vit_attention(normed, key_mask, w, *earlier):
    images, tokens, width = normed.shape
    project = product(flat(normed), w.qkv, 1, 0).astype(BF16).reshape(images, tokens, -1)
    attended = attend(project, key_mask, earlier)
    held = tokens_to_holders(attended)
    return (project, flat(held), product(flat(held), w.attn, 1, 0).reshape(held.shape))


def vit_attention_back(grad_own, kept, key_mask, w, *earlier):
    images, _, width = grad_own.shape
    grad_attended = product(flat(grad_own), w.attn, 1, 1).astype(BF16)
    grad_attended = features_to_holders(grad_attended.reshape(grad_own.shape))
    grad_project = flat(attend_back(kept.project, key_mask, grad_attended, earlier))
    partial = product(grad_project, w.qkv, 1, 1).astype(BF16)
    return (grad_project, partial.reshape(images, -1, width))


def adapter_backward(grad_cols, kept, places, w, later_than=()):
    images, tokens, _ = places.shape
    side = math.isqrt(tokens)
    grad_placed = jnp.einsum("ntc,ntw->ncw", places, grad_cols, preferred_element_type=F32)
    gate_value = jnp.tanh(w.gate)
    gate = jnp.sum(grad_placed * kept.spread, (0, 1)) * (1.0 - gate_value * gate_value)
    grad_spread = (grad_placed * gate_value).reshape(images, side, side, -1)
    grad_adapted = flat(
        depthwise(
            grad_spread, w.taps, 3, reverse=True, dtype=BF16, later_than=later_than
        )
    )
    grad_rows = tokens_to_holders(grad_adapted.reshape(images, tokens, -1))
    grad_pooled = product(flat(grad_rows), w.proj, 1, 1).astype(BF16)
    grad_pooled = features_to_holders(grad_pooled.reshape(grad_rows.shape[:2] + (-1,)))
    taps = depthwise_taps(kept.adapted, grad_spread, 3, later_than=(grad_adapted,))
    grad_pooled = grad_pooled.astype(F32).reshape(images, side, side, -1)
    return (flat(grad_rows), grad_pooled, taps, gate)


def conv_norm_back(grad_normed, kept, w):
    grid = kept.grid
    channels = grid.shape[-1] * lax.axis_size(TENSOR)
    scaled = kept.scaled
    weighted = grad_normed * w.gain[0]
    sums = ring_total(jnp.stack([jnp.sum(weighted, -1), jnp.sum(weighted * scaled, -1)]))
    grad_mixed = kept.inverse[:, None] * (
        weighted - sums[0][:, None] / channels - scaled * (sums[1][:, None] / channels)
    )
    gain = jnp.sum(grad_normed * scaled, 0)
    shift = jnp.sum(grad_normed, 0)
    return (grad_mixed.reshape(grid.shape), gain, shift)


def body(
    x_vit,
    x_conv,
    positions,
    valid,
    qkv_weight,
    attn_weight,
    fc_in,
    fc_out,
    vit_gains,
    vit_shifts,
    pw_in,
    pw_out,
    dw_kernel,
    conv_gains,
    conv_shift,
    proj_weight,
    taps,
    gate,
    dy_vit,
    dy_conv,
):
    here = x_vit.shape[0] // lax.axis_size(PIPE)
    count = lax.axis_size(TENSOR)
    cells = x_conv.shape[1]
    own_channels = x_conv.shape[2]
    conv_side = math.isqrt(cells)
    own_width = attn_weight.shape[1]
    own_units = fc_out.shape[1]
    conv_units = pw_out.shape[1]
    channels = pw_out.shape[2]
    model_width = vit_gains.shape[2]
    tap_count = dw_kernel.shape[1]
    side = taps.shape[1]
    tile = cells // 2

    def portion(source):
        return lax.dynamic_slice_in_dim(source, lax.axis_index(PIPE) * here, here, 0)

    conv_small = small_pair(jnp.concatenate([dw_kernel[0], conv_gains[0], conv_shift], 0))
    trade_in = QuarterTrade(pw_in[0], conv_small[0])
    vit_small = small_pair(
        after(jnp.concatenate([taps[0], gate, vit_gains[0], vit_shifts[0]], 0), conv_small[0])
    )
    weights = [Held(), Held()]
    for layer in range(2):
        conv, vit = (conv_small[layer], vit_small[layer])
        weights[layer].add(
            dw=conv[:tap_count],
            gain=conv[tap_count : tap_count + 2],
            shift=conv[tap_count + 2],
            taps=own_block(vit[:side], own_width, 1),
            gate=own_block(vit[side], own_width, 0),
            vit_gain=vit[side + 1 : side + 3],
            vit_shift=vit[side + 3 :],
        )
    w0, w1 = weights

    def take(**pairs):
        for name, pair in pairs.items():
            for w, weight in zip(weights, pair):
                w.add(**{name: weight})

    def both_images(former, latter, *earlier):
        mine, theirs = (select(former, latter), select(latter, former))
        sent = theirs.astype(BF16) if theirs.ndim > 3 else theirs
        if earlier:
            sent = after(sent, *earlier)
        got = traded(sent, PIPE, 1).astype(mine.dtype)
        return jnp.concatenate([select(mine, got), select(got, mine)], 0)

    stream = portion(x_vit)
    grid0 = portion(x_conv).reshape(here, conv_side, conv_side, own_channels)
    grad_top = portion(dy_vit)
    grad_top_full = gather(grad_top)
    attn_half = lax.all_gather(halves_of(attn_weight[0], 1), TENSOR, axis=0, tiled=True)
    places = placing(portion(positions))
    key_mask = portion(valid)

    normed0, conv0 = conv_norm(grid0, w0)
    conv0.normed = gather(after(normed0, grad_top_full, attn_half))
    trade_in.share(normed0)
    trade_out = QuarterTrade(pw_out[0], trade_in.got)
    trade_in.share_again()
    first = trade_in.pieces()
    trade_out.share(trade_in.pair)
    trade_proj = Trade(proj_weight[0], trade_out.got)
    trade_out.share_again(trade_proj.got)
    second = trade_out.pieces()
    (conv0.hidden, conv0.slope), parts = wide_mlp(0, conv0.normed, first, second, tile)
    branch = scatter_parts(parts)
    conv0.branch = branch
    trade_proj.share(parts)
    trade_qkv = Trade(qkv_weight[0].reshape(model_width, -1), parts)
    trade_fc_in = Trade(fc_in[0], parts)
    grid1, pooled0, square0 = conv_residual(
        grid0, branch, w0, trade_qkv.got, trade_fc_in.got
    )
    trade_fc_out = Trade(fc_out[0], pooled0)
    take(proj=trade_proj.layers())
    trade_qkv.share(pooled0)

    normed1, conv1 = conv_norm(grid1, w1, (pooled0,))
    conv1.normed = gather(normed1)
    take(qkv=trade_qkv.layers(normed1))
    stream_in0, vit0 = adapter_forward(stream.astype(F32), pooled0, places, w0, normed1, w0.qkv)
    normed_a0, vit0.scaled_a, vit0.inverse_a = vit_norm(stream_in0, w0, 0)
    vit0.normed_a = gather(normed_a0)
    trade_fc_in.share(normed_a0)
    trade_fc_out.share(normed_a0)
    (conv1.hidden, conv1.slope), parts = wide_mlp(
        1, conv1.normed, first, second, tile, None, (normed_a0, trade_fc_out.got)
    )
    branch = scatter_parts(parts)
    conv1.branch = branch
    attn_got = traded(after(attn_half, parts), PIPE, 1)
    attn_halves = jnp.stack([attn_half, attn_got])
    attn_rest = traded(attn_halves, DP, 1)
    attn_full = [joined(mine, theirs, 1) for mine, theirs in zip(attn_halves, attn_rest)]
    take(attn=(select(*attn_full), select(*attn_full[::-1])))
    take(fc_in=trade_fc_in.layers(parts))
    take(fc_out=trade_fc_out.layers(parts))
    vit0.project, vit0.attended, moved = vit_attention(
        vit0.normed_a, key_mask, w0, parts
    )
    stream_mid0 = stream_in0 + moved
    normed_b0, vit0.scaled_b, vit0.inverse_b = vit_norm(stream_mid0, w0, 1)
    vit0.normed_b = gather(normed_b0)
    grid2, pooled1, square1 = conv_residual(grid1, branch, w1)
    vit0.hidden, vit0.slope, partial = mlp(
        flat(vit0.normed_b), w0.fc_in, w0.fc_out, (pooled1,)
    )
    stream_out0 = stream_mid0 + scatter_tokens(partial.reshape(stream_shape(vit0)))
    stream1 = stream_out0.astype(BF16)

    stream_in1, vit1 = adapter_forward(stream1.astype(F32), pooled1, places, w1, partial)
    normed_a1, vit1.scaled_a, vit1.inverse_a = vit_norm(stream_in1, w1, 0)
    vit1.normed_a = gather(normed_a1)
    vit1.project, vit1.attended, moved = vit_attention(vit1.normed_a, key_mask, w1)
    stream_mid1 = stream_in1 + moved
    normed_b1, vit1.scaled_b, vit1.inverse_b = vit_norm(stream_mid1, w1, 1)
    vit1.normed_b = gather(normed_b1)
    vit1.hidden, vit1.slope, top_partial = mlp(
        flat(vit1.normed_b), w1.fc_in, w1.fc_out
    )

    norm_sums = [None, None]
    tap_sums = [None, None]

    def back_to_middle(grad_out, grad_full, kept, w, beside, *earlier):
        grad_hidden, partial = mlp_back(
            flat(grad_full), kept.slope, w.fc_in, w.fc_out, earlier
        )
        grad_normed = scatter_tokens(partial.reshape(stream_shape(kept)))
        packed = jnp.concatenate(
            [
                inner(flat(kept.normed_b), grad_hidden, partial),
                inner(flat(grad_full), kept.hidden, partial),
            ],
            1,
        )
        grad_normed = after(grad_normed, packed, *beside(partial))
        sums = [jnp.sum(grad_normed * kept.scaled_b, (0, 1)), jnp.sum(grad_normed, (0, 1))]
        grad_mid = grad_out.astype(F32) + norm_back(
            grad_normed, kept.scaled_b, kept.inverse_b, w.vit_gain[1]
        )
        return (grad_mid, Reduction(packed), sums)

    def back_to_start(grad_mid, grad_own, kept, w, beside, *earlier):
        grad_project, partial = vit_attention_back(grad_own, kept, key_mask, w, *earlier)
        grad_normed = scatter_tokens(partial)
        qkv = inner(flat(kept.normed_a), grad_project, partial)
        grad_normed = after(grad_normed, qkv, *beside(partial))
        sums = [jnp.sum(grad_normed * kept.scaled_a, (0, 1)), jnp.sum(grad_normed, (0, 1))]
        grad_in = grad_mid + norm_back(
            grad_normed, kept.scaled_a, kept.inverse_a, w.vit_gain[0]
        )
        return (grad_in, qkv, sums)

    def row_grads(kept, grad_rows, grad_own, *earlier):
        sides = lax.axis_size(DP)
        pairs = [
            product(by_relative(left), by_relative(after(right, *earlier), TENSOR), 0, 0)
            for left, right in ((kept.pooled, grad_rows), (flat(grad_own), kept.attended))
        ]
        blocks = [pair.astype(BF16).reshape(sides, -1, model_width) for pair in pairs]
        return jnp.concatenate(blocks, 1).reshape(-1, model_width)

    def step_all(reductions, *earlier):
        return [reduction.step(*earlier) for reduction in reductions]

    grad_mid1, mlp1, sums_b1 = back_to_middle(
        grad_top, grad_top_full, vit1, w1, lambda partial: (), top_partial
    )
    grad_mid1_own = grad_mid1.astype(BF16)

    def beside_start1(partial):
        mlp1.step(partial)
        return [mlp1.step(partial)]

    grad_in1, qkv1, sums_a1 = back_to_start(grad_mid1, grad_mid1_own, vit1, w1, beside_start1)
    norm_sums[1] = jnp.stack([sums_a1[0], sums_b1[0], sums_a1[1], sums_b1[1]])
    grad_stream = grad_in1.astype(BF16)
    grad_stream_full = gather(grad_stream)
    grad_rows1, grad_pooled1, tap_sum, gate_sum = adapter_backward(
        features_to_holders(grad_stream), vit1, places, w1
    )
    tap_sums[1] = jnp.concatenate([tap_sum, gate_sum[None]], 0)

    grad_map1, scaled1 = spread_back(
        grad_pooled1, portion(dy_conv).reshape(grid0.shape), w1.gain[1]
    )
    grad_branch1 = gather(flat(scaled1))
    grad_mid0, mlp0, sums_b0 = back_to_middle(
        grad_stream, grad_stream_full, vit0, w0, lambda partial: (), scaled1
    )
    rows1 = Reduction(row_grads(vit1, grad_rows1, grad_mid1_own, scaled1), True)
    grad_mid0_own = grad_mid0.astype(BF16)
    rows1.step(grad_mid0_own)
    grad_in0, qkv0, sums_a0 = back_to_start(
        grad_mid0, grad_mid0_own, vit0, w0, lambda partial: ()
    )
    (grad_hidden1,), parts = wide_mlp(
        1, grad_branch1, first, second, tile, conv1.slope, (grad_mid0_own, rows1.partial)
    )
    grad_normed1 = scatter_parts(parts)
    conv_in1 = Reduction(inner(conv1.normed, grad_hidden1, parts))
    conv_out1 = Reduction(inner(grad_branch1, conv1.hidden, parts))
    norm_sums[0] = jnp.stack([sums_a0[0], sums_b0[0], sums_a0[1], sums_b0[1]])
    grad_last = grad_in0.astype(BF16)
    qkv = Reduction(jnp.concatenate([qkv0, qkv1], 1))
    grad_mixed1, gain1, shift1 = conv_norm_back(grad_normed1, conv1, w1)
    mlp0.step(grad_last)
    rows1.step(grad_last)
    qkv.step(grad_last)
    grad_rows0, grad_pooled0, tap_sum, gate_sum = adapter_backward(
        features_to_holders(grad_last), vit0, places, w0, (conv_in1.partial, conv_out1.partial)
    )
    tap_sums[0] = jnp.concatenate([tap_sum, gate_sum[None]], 0)
    grad_grid1 = depthwise(grad_mixed1, w1.dw, 7, grad_map1, True)
    grad_next = grad_grid1.astype(BF16)

    ready = step_all([mlp0, qkv], grad_grid1)
    grad_map0, scaled0 = spread_back(grad_pooled0, grad_next, w0.gain[1], ready)
    grad_branch0 = gather(flat(scaled0))
    step_all([conv_out1, conv_in1], scaled0)
    grad_fc = over_sections(after(mlp0.partial, scaled0), mlp1.partial)
    half = qkv.partial.shape[1] // 2
    grad_qkv = over_sections(after(qkv.partial[:, :half], scaled0), qkv.partial[:, half:])
    rows0 = Reduction(row_grads(vit0, grad_rows0, grad_mid0_own), True)
    taps1 = depthwise_taps(conv1.grid, grad_mixed1, 7, later_than=(scaled0,))
    ready = step_all([conv_out1, conv_in1], taps1)
    rows0.step(*ready)
    (grad_hidden0,), parts = wide_mlp(
        0,
        grad_branch0,
        first,
        second,
        tile,
        conv0.slope,
        ready + [rows0.partial, grad_fc, grad_qkv],
    )
    grad_normed0 = scatter_parts(parts)
    rows0.step(parts)
    conv_out0 = Reduction(inner(grad_branch0, conv0.hidden, rows0.partial))
    conv_in0 = Reduction(inner(conv0.normed, grad_hidden0, conv_out0.partial))
    conv_out0.step(conv_in0.partial)
    conv_in0.step(conv_out0.partial)
    conv_out0.step(conv_in0.partial)
    rows1.step(conv_in0.partial)
    grad_normed0 = after(grad_normed0, conv_in0.partial, conv_out0.partial)
    grad_mixed0, gain0, shift0 = conv_norm_back(grad_normed0, conv0, w0)
    grad_grid0 = depthwise(grad_mixed0, w0.dw, 7, grad_map0, True)
    grad_conv_out = over_sections(conv_out0.partial, conv_out1.partial)
    grad_conv = both_images(grad_grid0, grad_grid1)
    taps0 = depthwise_taps(conv0.grid, grad_mixed0, 7, later_than=(grad_grid0,))
    conv_in0.step(grad_grid0)
    grad_conv_in = over_sections(conv_in0.partial, conv_in1.partial)
    step_all([rows0, rows1], grad_grid0)
    stream_out1 = stream_mid1 + scatter_tokens(
        after(top_partial, grad_normed0).reshape(stream_shape(vit1))
    )
    rows0.step(taps0)
    grad_proj_attn = over_sections(rows0.partial, rows1.partial)
    proj_rows = channels // lax.axis_size(DP)
    scale1 = jnp.sum(flat(grad_map1) * conv1.branch, 0)
    scale0 = jnp.sum(flat(grad_map0) * conv0.branch, 0)

    def over_images(pair):
        return total_over(select(*pair) + traded(select(*pair[::-1]), PIPE, 1), DP)

    token_terms = [
        jnp.concatenate([widen(tap_sums[layer], model_width, 1), norm_sums[layer]], 0)
        for layer in range(2)
    ]
    token_sums = total_over(over_images(token_terms), TENSOR)
    column_sums = over_images(
        [
            jnp.concatenate([taps0, jnp.stack([gain0, scale0, shift0])], 0),
            jnp.concatenate([taps1, jnp.stack([gain1, scale1, shift1])], 0),
        ]
    )

    out_conv = both_images(grid1, grid2, grad_mid1_own).reshape(1, -1, cells, own_channels)
    out_vit = both_images(stream1, stream_out1.astype(BF16))[None]
    squares = total_over(both_images(square0, square1, grad_mid1_own), TENSOR)
    rms_conv = jnp.sqrt(squares)[None]
    mean_squares = [jnp.mean(out * out, -1) for out in (stream_out0, stream_out1)]
    rms_vit = jnp.sqrt(both_images(*mean_squares))[None]
    grad_vit = both_images(grad_in0[None], grad_in1[None], grad_last)
    grad_vit = grad_vit.reshape((1, -1) + grad_in0.shape[1:])
    return (
        out_vit,
        out_conv,
        grad_vit,
        grad_conv.reshape(1, -1, cells, own_channels),
        rms_vit,
        rms_conv,
        grad_qkv.reshape(1, -1, 3, own_width),
        grad_proj_attn[proj_rows:].T[None],
        grad_fc[:, :own_units][None],
        grad_fc[:, own_units:].T[None],
        token_sums[side + 1 : side + 3][None],
        token_sums[side + 3 :][None],
        grad_conv_in[None],
        grad_conv_out.T[None],
        column_sums[:tap_count][None],
        column_sums[tap_count : tap_count + 2][None],
        column_sums[tap_count + 2 :],
        grad_proj_attn[:proj_rows][None],
        token_sums[:side][None],
        token_sums[side][None],
    )


def stream_shape(kept):
    return kept.normed_b.shape


def solution(mesh):
    return jax.shard_map(
        body,
        mesh=mesh,
        in_specs=(
            P(DP, TENSOR, None),
            P(DP, None, TENSOR),
            P(DP, None),
            P(DP, None),
            P(PIPE, None, None, TENSOR),
            P(PIPE, TENSOR, None),
            P(PIPE, None, TENSOR),
            P(PIPE, TENSOR, None),
            P(PIPE, None, None),
            P(PIPE, None, None),
            P(PIPE, None, TENSOR),
            P(PIPE, TENSOR, None),
            P(PIPE, None, TENSOR),
            P(PIPE, None, TENSOR),
            P(PIPE, TENSOR),
            P(PIPE, None, None),
            P(PIPE, None, None),
            P(PIPE, None),
            P(DP, TENSOR, None),
            P(DP, None, TENSOR),
        ),
        out_specs=(
            P(PIPE, DP, TENSOR, None),
            P(PIPE, DP, None, TENSOR),
            P(PIPE, DP, TENSOR, None),
            P(PIPE, DP, None, TENSOR),
            P(PIPE, DP, TENSOR),
            P(PIPE, DP, None),
            P(PIPE, DP, None, TENSOR),
            P(PIPE, TENSOR, DP),
            P(PIPE, DP, TENSOR),
            P(PIPE, TENSOR, DP),
            P(PIPE, None, None),
            P(PIPE, None, None),
            P(PIPE, DP, TENSOR),
            P(PIPE, TENSOR, DP),
            P(PIPE, None, TENSOR),
            P(PIPE, None, TENSOR),
            P(PIPE, TENSOR),
            P(PIPE, DP, TENSOR),
            P(PIPE, None, None),
            P(PIPE, None),
        ),
        check_vma=False,
    )
```

time: 1600 us -> 1350 us (0.84)
  waiting for transfers between devices: 768 us -> 546 us
  other arithmetic: 239 us -> 157 us
  Pallas kernels: 158 us -> 219 us
  blocking collectives: 35.8 us -> 0 us
    reduce_scatter x12 -> x10, waiting for transfers between devices: 231 us -> 75.6 us  [the longest x4 47.3 us: scatter_parts(): lax.psum_scatter(parts, TENSOR, scatter_dimension=0, tiled=False)]
    ppermute x14 -> x60, waiting for transfers between devices: 16.5 us -> 162 us  [turned(): lax.ppermute(values, TENSOR, [(i, (i + by) % count) for i in range(count)])]
    all_gather x16 -> x11, waiting for transfers between devices: 227 us -> 101 us  [the longest x10 101 us: gather(): return lax.all_gather(values, TENSOR, axis=1, tiled=True)]
    ppermute x72 -> x61, waiting for transfers between devices: 275 us -> 207 us  [traded(): lax.ppermute(array, axis, [(i, i ^ bit) for i in range(lax.axis_size(axis...]
    unnamed x139 -> x2, other arithmetic: 62 us -> 0.01 us
    pallas_call x24 -> x95, Pallas kernels: 158 us -> 219 us  [the longest x46 146 us: run(): pl.pallas_call(without_extra, in_specs=list(in_specs) + [ANYWHERE] * extr...]
    concatenate x8 -> x27, other arithmetic: 4.77 us -> 46.9 us  [the longest x10 14.5 us: by_relative(): jnp.concatenate([lax.dynamic_slice_in_dim(values, (index ^ r) * block, bl...]
    ppermute x14 -> x60, starting transfers between devices: 39.5 us -> 75.9 us  [turned(): lax.ppermute(values, TENSOR, [(i, (i + by) % count) for i in range(count)])]
  transfers between devices with their start and end apart: 116 -> 142, of which waited for: 57 -> 65; matrix products, arithmetic and copies ran while one was open for 26% -> 24% of each run, Pallas kernels for 8% -> 12%
where the time goes in v3:
time: 1350 us; the launch traced here: 1340 us
  waiting for transfers between devices  546 us (40%)
  Pallas kernels  219 us (16%)
  local copies, waits for them, and re-layouts  176 us (13%)
  other arithmetic  157 us (12%)
  starting transfers between devices  129 us (10%)
  matrix products  89.7 us (7%)
  between operations  20.3 us (2%)
    ppermute x61, waiting for transfers between devices, traded(): lax.ppermute(array, axis, [(i, i ^ bit) for i in range(lax.axis_size(axis...  207 us
    ppermute x60, waiting for transfers between devices, turned(): lax.ppermute(values, TENSOR, [(i, (i + by) % count) for i in range(count)])  162 us
    pallas_call x46, Pallas kernels, run(): pl.pallas_call(without_extra, in_specs=list(in_specs) + [ANYWHERE] * extr...  146 us
    all_gather x10, waiting for transfers between devices, gather(): return lax.all_gather(values, TENSOR, axis=1, tiled=True)  101 us
    unnamed x762, local copies, waits for them, and re-layouts  88.1 us
    dot_general x26, matrix products, product(): lax.dot_general(left, right, (((left_axis,), (right_axis,)), ((), ())), p...  86.1 us
    ppermute x60, starting transfers between devices, turned(): lax.ppermute(values, TENSOR, [(i, (i + by) % count) for i in range(count)])  75.9 us
    pallas_call x4, Pallas kernels, wide_mlp(): pl.pallas_call(without_extra, grid_spec=pltpu.PrefetchScalarGridSpec(num_...  73.7 us
  transfers between devices with their start and end apart: 142, of which 65 were waited for; matrix products, arithmetic and copies ran while one was open for 24% of the time, Pallas kernels for 12%

profile of v3, /device:TPU:0, one launch (start us, length us, event | category | flops | bytes accessed | tf_op | source)
XLA Modules:
  0.0 1338.6 jit_solution(5310453502839060739)
XLA Ops:
  38.8 21.0 %collective-permute-done.5.refs_0_ = bf16[384,1536]{1,0:T(8,128)(2,1)} collective-permute-done((bf16[384,1536]{1,0:T(8,128)(2,1)}, bf16[384,1536]{1,0:T(8,128)(2,1)}, u32[]{:S(2)}, u32[]{:S(2)}) %collective-permute-start.5) | collective-permute-done | bytes 1179680 | tf_op jit(solution)/shard_map/ppermute | solution.py:508
  61.9 11.7 all-gather.13.cloned.1.call-done.refs_1_
  76.4 9.4 collective-permute-done.6.refs_0_
  91.7 20.5 %collective-permute-done.9.refs_0_ = bf16[384,1536]{1,0:T(8,128)(2,1)} collective-permute-done((bf16[384,1536]{1,0:T(8,128)(2,1)}, bf16[384,1536]{1,0:T(8,128)(2,1)}, u32[]{:S(2)}, u32[]{:S(2)}) %collective-permute-start.9) | collective-permute-done | bytes 1179680 | tf_op jit(solution)/shard_map/ppermute | solution.py:508
  112.3 8.5 collective-permute-done.10.refs_1_.refs_0_
  128.9 9.4 all-gather.15.cloned.1.call-done.refs_0_
  138.2 18.8 %shard_map.357 = (bf16[1024,1536]{1,0:T(8,128)(2,1)}, bf16[1024,1536]{1,0:T(8,128)(2,1)}, bf16[4,1024,384]{2,1,0:T(8,128)(2,1)}) custom-call(s32[2]{0:T(128)} %pad_add_fusion.meta_ref, bf16[1024,1536]{1,0:T(8,128)(2,1)} %all-gather.15.cloned.1.call-done.refs_0_, bf16[1536,1536]{1,0:T(8,128)(2,1)} %bitcast.548, ...), custom_call_target="tpu_custom_call" | custom-call | tf_op jit(solution)/shard_map/pallas_call | solution.py:267
  177.6 38.5 %reduce-scatter.11.cloned.1.call-done = bf16[1,1024,384]{2,1,0:T(8,128)(2,1)} async-done(((bf16[4,1024,384]{2,1,0:T(8,128)(2,1)}), bf16[1,1024,384]{2,1,0:T(8,128)(2,1)}) %reduce-scatter.11.cloned.1.call-update) | async-done | bytes 786448 | tf_op jit(solution)/shard_map/reduce_scatter | solution.py:644
  257.9 9.1 collective-permute-done.19
  294.5 23.4 %collective-permute-done.28.refs_0_ = bf16[512,1024]{1,0:T(8,128)(2,1)S(1)} collective-permute-done((bf16[512,1024]{1,0:T(8,128)(2,1)}, bf16[512,1024]{1,0:T(8,128)(2,1)S(1)}, u32[]{:S(2)}, u32[]{:S(2)}) %collective-permute-start.28) | collective-permute-done | bytes 1048608 | tf_op jit(solution)/shard_map/ppermute | solution.py:508
  318.9 19.0 %shard_map.368 = (bf16[1024,1536]{1,0:T(8,128)(2,1)}, bf16[1024,1536]{1,0:T(8,128)(2,1)}, bf16[4,1024,384]{2,1,0:T(8,128)(2,1)}) custom-call(s32[2]{0:T(128)} %pad_add_fusion.1.meta_ref, bf16[1024,1536]{1,0:T(8,128)(2,1)} %all-gather.19.cloned.1.call-done.refs_0_, bf16[1536,1536]{1,0:T(8,128)(2,1)} %bitcast.549, ...), custom_call_target="tpu_custom_call" | custom-call | tf_op jit(solution)/shard_map/pallas_call | solution.py:267
  352.3 12.0 collective-permute-done.32
  403.7 8.9 reduce-scatter.13.cloned.1.call-done
  422.7 8.5 collective-permute-done.37
  439.3 12.7 all-gather.21.cloned.1.call-done
  477.8 10.2 collective-permute-done.43
  496.4 30.2 %all-gather.23.cloned.1.call-done = bf16[1,576,1024]{2,1,0:T(8,128)(2,1)} async-done(((bf16[1,144,1024]{2,1,0:T(8,128)(2,1)}), bf16[1,576,1024]{2,1,0:T(8,128)(2,1)}) %all-gather.23.cloned.1.call-update) | async-done | bytes 1179664 | tf_op jit(solution)/shard_map/all_gather | solution.py:593
  546.0 29.7 %all-gather.25.cloned.1.call-done = bf16[1,576,1024]{2,1,0:T(8,128)(2,1)} async-done(((bf16[1,144,1024]{2,1,0:T(8,128)(2,1)}), bf16[1,576,1024]{2,1,0:T(8,128)(2,1)}) %all-gather.25.cloned.1.call-update) | async-done | bytes 1179664 | tf_op jit(solution)/shard_map/all_gather | solution.py:593
  603.2 14.1 %reduce-scatter.17.cloned.1.call-done = bf16[1,144,1024]{2,1,0:T(8,128)(2,1)} async-done(((bf16[1,576,1024]{2,1,0:T(8,128)(2,1)}), bf16[1,144,1024]{2,1,0:T(8,128)(2,1)}) %reduce-scatter.17.cloned.1.call-update) | async-done | bytes 294928 | tf_op jit(solution)/shard_map/reduce_scatter | solution.py:640
  660.7 18.0 %collective-permute-done.52.refs_1_ = bf16[256,2048]{1,0:T(8,128)(2,1)} collective-permute-done((bf16[256,2048]{1,0:T(8,128)(2,1)}, bf16[256,2048]{1,0:T(8,128)(2,1)}, u32[]{:S(2)}, u32[]{:S(2)}) %collective-permute-start.52) | collective-permute-done | bytes 1048608 | tf_op jit(solution)/shard_map/ppermute | solution.py:508
  721.5 14.0 %collective-permute-done.60 = bf16[1,144,384]{2,1,0:T(8,128)(2,1)S(1)} collective-permute-done((bf16[1,144,384]{2,1,0:T(8,128)(2,1)S(1)}, bf16[1,144,384]{2,1,0:T(8,128)(2,1)S(1)}, u32[]{:S(2)}, u32[]{:S(2)}) %collective-permute-start.60) | collective-permute-done | bytes 110624 | tf_op jit(solution)/shard_map/ppermute | solution.py:598
  766.4 9.2 reduce-scatter.21.cloned.1.call-done
  792.0 9.5 collective-permute-done.63
  844.4 17.9 %shard_map.400 = (bf16[1024,1536]{1,0:T(8,128)(2,1)}, bf16[4,1024,384]{2,1,0:T(8,128)(2,1)}) custom-call(s32[2]{0:T(128)} %pad_add_fusion.1.meta_ref, bf16[1024,1536]{1,0:T(8,128)(2,1)} %all-gather.29.cloned.1.call-done.refs_0_, bf16[1024,1536]{1,0:T(8,128)(2,1)} %get-tuple-element.64.refs_1_, bf16[1536,1536]{1,0:T(8,128)(2,1)} %bitcast.550, ...), custom_call_target="tpu_custom_call" | custom-call | tf_op jit(solution)/shard_map/pallas_call | solution.py:267
  862.3 9.4 convolution_convert_fusion.3.refs_2_.refs_0_
  893.8 11.6 collective-permute-done.66
  915.6 11.5 collective-permute-done.70
  940.7 12.5 collective-permute-done.73
  1052.1 21.8 %collective-permute-done.85.refs_1_ = bf16[384,1536]{1,0:T(8,128)(2,1)S(1)} collective-permute-done((bf16[384,1536]{1,0:T(8,128)(2,1)}, bf16[384,1536]{1,0:T(8,128)(2,1)S(1)}, u32[]{:S(2)}, u32[]{:S(2)}) %collective-permute-start.85) | collective-permute-done | bytes 1179680 | tf_op jit(solution)/shard_map/ppermute | solution.py:508
  1088.5 18.0 %shard_map.420 = (bf16[1024,1536]{1,0:T(8,128)(2,1)}, bf16[4,1024,384]{2,1,0:T(8,128)(2,1)}) custom-call(s32[2]{0:T(128)} %pad_add_fusion.meta_ref, bf16[1024,1536]{1,0:T(8,128)(2,1)} %all-gather.31.cloned.1.call-done.refs_0_, bf16[1024,1536]{1,0:T(8,128)(2,1)} %get-tuple-element.70.refs_1_, bf16[1536,1536]{1,0:T(8,128)(2,1)} %bitcast.551, ...), custom_call_target="tpu_custom_call" | custom-call | tf_op jit(solution)/shard_map/pallas_call | solution.py:267
  1268.4 23.8 %collective-permute-done.105.refs_1_ = bf16[640,256]{1,0:T(8,128)(2,1)S(1)} collective-permute-done((bf16[640,256]{1,0:T(8,128)(2,1)S(1)}, bf16[640,256]{1,0:T(8,128)(2,1)S(1)}, u32[]{:S(2)}, u32[]{:S(2)}) %collective-permute-start.105) | collective-permute-done | bytes 327712 | tf_op jit(solution)/shard_map/ppermute | solution.py:508
  1295.4 11.9 collective-permute-done.109
  (1450 shorter events, 813.7 us)
Async XLA Ops:
  7.2 54.7 %all-gather.33.cloned.1.call-start = ((), (), s32[]{:S(2)}) async-start(), calls=%async_computation.30 | async-start | bytes 1310720 | tf_op jit(solution)/shard_map/all_gather | solution.py:892
  9.1 64.5 %all-gather.13.cloned.1.call-start = ((), (), s32[]{:S(2)}) async-start(), calls=%async_computation.10 | async-start | bytes 1474560 | tf_op jit(solution)/shard_map/all_gather | solution.py:593
  59.8 78.5 %all-gather.15.cloned.1.call-start = ((), (), s32[]{:S(2)}) async-start(), calls=%async_computation.11 | async-start | bytes 3932160 | tf_op jit(solution)/shard_map/all_gather | solution.py:593
  73.6 142.4 %reduce-scatter.11.cloned.1.call-start = ((), (), s32[]{:S(2)}) async-start(), calls=%async_computation.12 | async-start | bytes 3932160 | tf_op jit(solution)/shard_map/reduce_scatter | solution.py:644
  157.0 161.9 %all-gather.19.cloned.1.call-start = ((), (), s32[]{:S(2)}) async-start(), calls=%async_computation.14 | async-start | bytes 3932160 | tf_op jit(solution)/shard_map/all_gather | solution.py:593
  168.6 48.8 %collective-permute-start.13 = (bf16[512,1024]{1,0:T(8,128)(2,1)}, bf16[512,1024]{1,0:T(8,128)(2,1)S(1)}, u32[]{:S(2)}, u32[]{:S(2)}) collective-permute-start(bf16[512,1024]{1,0:T(8,128)(2,1)} %shard_map.359), channel_id=1, source_target_pairs={{0,16},{16,0},{1,17},{17,1},{2,18},{18,2},{3,19},{19,3},{4,20},{20... | collective-permute-start | bytes 3145736 | tf_op jit(solution)/shard_map/ppermute | solution.py:508
  237.6 129.5 %all-gather.17.cloned.1.call-start = ((), (), s32[]{:S(2)}) async-start(), calls=%async_computation.13 | async-start | bytes 1474560 | tf_op jit(solution)/shard_map/all_gather | solution.py:593
  291.1 121.5 %reduce-scatter.13.cloned.1.call-start = ((), (), s32[]{:S(2)}) async-start(), calls=%async_computation.16 | async-start | bytes 3932160 | tf_op jit(solution)/shard_map/reduce_scatter | solution.py:644
  338.0 114.0 %all-gather.21.cloned.1.call-start = ((), (), s32[]{:S(2)}) async-start(), calls=%async_computation.15 | async-start | bytes 1474560 | tf_op jit(solution)/shard_map/all_gather | solution.py:593
  419.9 72.3 %reduce-scatter.15.cloned.1.call-start = ((), (), s32[]{:S(2)}) async-start(), calls=%async_computation.17 | async-start | bytes 1474560 | tf_op jit(solution)/shard_map/reduce_scatter | solution.py:640
  458.4 68.2 %all-gather.23.cloned.1.call-start = ((), (), s32[]{:S(2)}) async-start(), calls=%async_computation.18 | async-start | bytes 1474560 | tf_op jit(solution)/shard_map/all_gather | solution.py:593
  496.4 79.4 %all-gather.25.cloned.1.call-start = ((), (), s32[]{:S(2)}) async-start(), calls=%async_computation.19 | async-start | bytes 1474560 | tf_op jit(solution)/shard_map/all_gather | solution.py:593
  545.8 71.5 %reduce-scatter.17.cloned.1.call-start = ((), (), s32[]{:S(2)}) async-start(), calls=%async_computation.20 | async-start | bytes 1474560 | tf_op jit(solution)/shard_map/reduce_scatter | solution.py:640
  588.8 92.3 %reduce-scatter.19.cloned.1.call-start = ((), (), s32[]{:S(2)}) async-start(), calls=%async_computation.21 | async-start | bytes 1474560 | tf_op jit(solution)/shard_map/reduce_scatter | solution.py:640
  647.1 93.6 %all-gather.27.cloned.1.call-start = ((), (), s32[]{:S(2)}) async-start(), calls=%async_computation.22 | async-start | bytes 1474560 | tf_op jit(solution)/shard_map/all_gather | solution.py:593
  701.8 73.7 %reduce-scatter.21.cloned.1.call-start = ((), (), s32[]{:S(2)}) async-start(), calls=%async_computation.23 | async-start | bytes 1474560 | tf_op jit(solution)/shard_map/reduce_scatter | solution.py:640
  747.3 97.1 %all-gather.29.cloned.1.call-start = ((), (), s32[]{:S(2)}) async-start(), calls=%async_computation.25 | async-start | bytes 3932160 | tf_op jit(solution)/shard_map/all_gather | solution.py:593
  750.0 125.8 %reduce-scatter.23.cloned.1.call-start = ((), (), s32[]{:S(2)}) async-start(), calls=%async_computation.24 | async-start | bytes 1474560 | tf_op jit(solution)/shard_map/reduce_scatter | solution.py:640
  810.1 147.1 %reduce-scatter.25.cloned.1.call-start = ((), (), s32[]{:S(2)}) async-start(), calls=%async_computation.26 | async-start | bytes 3932160 | tf_op jit(solution)/shard_map/reduce_scatter | solution.py:644
  829.4 99.5 %collective-permute-start.78 = (bf16[512,2048]{1,0:T(8,128)(2,1)}, bf16[512,2048]{1,0:T(8,128)(2,1)}, u32[]{:S(2)}, u32[]{:S(2)}) collective-permute-start(bf16[512,2048]{1,0:T(8,128)(2,1)} %fusion.16), channel_id=1, source_target_pairs={{0,4},{4,0},{8,12},{12,8},{1,5},{5,1},{9,13},{13,9},{2,6},{6,2},{1... | collective-permute-start | bytes 6291464 | tf_op jit(solution)/shard_map/ppermute | solution.py:508
  862.3 226.2 %all-gather.31.cloned.1.call-start = ((), (), s32[]{:S(2)}) async-start(), calls=%async_computation.27 | async-start | bytes 3932160 | tf_op jit(solution)/shard_map/all_gather | solution.py:593
  987.6 214.0 %reduce-scatter.27.cloned.1.call-start = ((), (), s32[]{:S(2)}) async-start(), calls=%async_computation.28 | async-start | bytes 3932160 | tf_op jit(solution)/shard_map/reduce_scatter | solution.py:644
  1004.5 69.8 %collective-permute-start.86 = (bf16[1280,1024]{1,0:T(8,128)(2,1)}, bf16[1280,1024]{1,0:T(8,128)(2,1)}, u32[]{:S(2)}, u32[]{:S(2)}) collective-permute-start(bf16[1280,1024]{1,0:T(8,128)(2,1)} %bitcast.177), channel_id=1, source_target_pairs={{0,4},{4,0},{8,12},{12,8},{1,5},{5,1},{9,13},{13,9},{2,6},{6,2},{1... | collective-permute-start | bytes 7864328 | tf_op jit(solution)/shard_map/ppermute | solution.py:508
  1025.9 48.0 %collective-permute-start.85 = (bf16[384,1536]{1,0:T(8,128)(2,1)}, bf16[384,1536]{1,0:T(8,128)(2,1)S(1)}, u32[]{:S(2)}, u32[]{:S(2)}) collective-permute-start(bf16[384,1536]{1,0:T(8,128)(2,1)} %slice.328), channel_id=1, source_target_pairs={{0,8},{4,12},{8,0},{12,4},{1,9},{5,13},{9,1},{13,5},{2,10},{6,14},... | collective-permute-start | bytes 3538952 | tf_op jit(solution)/shard_map/ppermute | solution.py:508
  1028.7 56.7 %collective-permute-start.87 = (bf16[256,2048]{1,0:T(8,128)(2,1)}, bf16[256,2048]{1,0:T(8,128)(2,1)}, u32[]{:S(2)}, u32[]{:S(2)}) collective-permute-start(bf16[256,2048]{1,0:T(8,128)(2,1)} %broadcast_select_fusion.8), channel_id=1, source_target_pairs={{0,16},{16,0},{1,17},{17,1},{2,18},{18,2},{3,19},{19,3},{4,20},{20... | collective-permute-start | bytes 3145736 | tf_op jit(solution)/shard_map/ppermute | solution.py:508
  1032.0 51.3 %collective-permute-start.88 = (bf16[256,768]{1,0:T(8,128)(2,1)}, bf16[256,768]{1,0:T(8,128)(2,1)}, u32[]{:S(2)}, u32[]{:S(2)}) collective-permute-start(bf16[256,768]{1,0:T(8,128)(2,1)} %broadcast_select_fusion.24), channel_id=1, source_target_pairs={{0,16},{16,0},{1,17},{17,1},{2,18},{18,2},{3,19},{19,3},{4,20},{20... | collective-permute-start | bytes 1179656 | tf_op jit(solution)/shard_map/ppermute | solution.py:508
  1106.6 211.7 %reduce-scatter.29.cloned.1.call-start = ((), (), s32[]{:S(2)}) async-start(), calls=%async_computation.29 | async-start | bytes 1474560 | tf_op jit(solution)/shard_map/reduce_scatter | solution.py:640
  1109.8 46.6 %collective-permute-start.106 = (bf16[640,1024]{1,0:T(8,128)(2,1)}, bf16[640,1024]{1,0:T(8,128)(2,1)}, u32[]{:S(2)}, u32[]{:S(2)}) collective-permute-start(bf16[640,1024]{1,0:T(8,128)(2,1)} %slice.341), channel_id=1, source_target_pairs={{0,8},{4,12},{8,0},{12,4},{1,9},{5,13},{9,1},{13,5},{2,10},{6,14},... | collective-permute-start | bytes 3932168 | tf_op jit(solution)/shard_map/ppermute | solution.py:508
  1141.3 47.9 %collective-permute-start.90 = (bf16[768,1536]{1,0:T(8,128)(2,1)}, bf16[768,1536]{1,0:T(8,128)(2,1)}, u32[]{:S(2)}, u32[]{:S(2)}) collective-permute-start(bf16[768,1536]{1,0:T(8,128)(2,1)} %slice.334), channel_id=1, source_target_pairs={{0,4},{4,0},{8,12},{12,8},{1,5},{5,1},{9,13},{13,9},{2,6},{6,2},{1... | collective-permute-start | bytes 7077896 | tf_op jit(solution)/shard_map/ppermute | solution.py:508
  1160.9 59.7 %collective-permute-start.107 = (bf16[640,512]{1,0:T(8,128)(2,1)}, bf16[640,512]{1,0:T(8,128)(2,1)}, u32[]{:S(2)}, u32[]{:S(2)}) collective-permute-start(bf16[640,512]{1,0:T(8,128)(2,1)} %slice.342), channel_id=1, source_target_pairs={{0,1},{1,0},{2,3},{3,2},{4,5},{5,4},{6,7},{7,6},{8,9},{9,8},{10,11... | collective-permute-start | bytes 1966088 | tf_op jit(solution)/shard_map/ppermute | solution.py:508
  1254.8 56.0 %collective-permute-start.99 = (bf16[1,32,32,384]{3,2,1,0:T(8,128)(2,1)}, bf16[1,32,32,384]{3,2,1,0:T(8,128)(2,1)}, u32[]{:S(2)}, u32[]{:S(2)}) collective-permute-start(bf16[1,32,32,384]{3,2,1,0:T(8,128)(2,1)} %select_convert_fusion), channel_id=1, source_target_pairs={{0,16},{16,0},{1,17},{17,1},{2,18},{18,2},{3,19},{19,3},{4,20},{20... | collective-permute-start | bytes 2359304 | tf_op jit(solution)/shard_map/ppermute | solution.py:508
  1265.0 49.3 %collective-permute-start.116 = (bf16[384,1536]{1,0:T(8,128)(2,1)}, bf16[384,1536]{1,0:T(8,128)(2,1)}, u32[]{:S(2)}, u32[]{:S(2)}) collective-permute-start(bf16[384,1536]{1,0:T(8,128)(2,1)} %broadcast_select_fusion.7), channel_id=1, source_target_pairs={{0,16},{16,0},{1,17},{17,1},{2,18},{18,2},{3,19},{19,3},{4,20},{20... | collective-permute-start | bytes 3538952 | tf_op jit(solution)/shard_map/ppermute | solution.py:508
  (438 other events, 5861.7 us)
Sparse Core Ops, SparseCore 0:
  10.2 31.7 all-gather.32
  44.1 29.4 all-gather.12
  75.7 62.4 all-gather.14
  157.2 58.8 reduce-scatter.10
  237.7 77.3 all-gather.18
  317.1 28.9 all-gather.16
  348.4 64.0 reduce-scatter.12
  420.0 31.9 all-gather.20
  458.5 33.5 reduce-scatter.14
  496.5 30.0 all-gather.22
  545.9 29.8 all-gather.24
  589.0 28.2 reduce-scatter.16
  647.2 27.3 reduce-scatter.18
  701.9 38.6 all-gather.26
  747.4 28.0 reduce-scatter.20
  777.5 66.8 all-gather.28
  846.6 29.1 reduce-scatter.22
  877.9 74.3 reduce-scatter.24
  987.8 61.5 all-gather.30
  1106.7 56.9 reduce-scatter.26
  1251.8 39.1 reduce-scatter.28

commit v4 on v3

--- a/solution.py
+++ b/solution.py
@@ -691,6 +691,16 @@
             if self.moves:
                 self.send()
         return self.partial
+
+
+class Sections:
+    def __init__(self, former, latter):
+        self.kept = select(former, latter)
+        self.got = traded(select(latter, former), PIPE, 1)
+
+    def total(self, *earlier):
+        got = after(self.got, *earlier) if earlier else self.got
+        return self.kept.astype(F32) + got.astype(F32)
 
 
 def over_sections(former, latter):
@@ -954,10 +964,11 @@
     vit1.normed_a = gather(normed_a1)
     vit1.project, vit1.attended, moved = vit_attention(vit1.normed_a, key_mask, w1)
     stream_mid1 = stream_in1 + moved
+    out_conv = both_images(grid1, grid2, normed_a1).reshape(1, -1, cells, own_channels)
     normed_b1, vit1.scaled_b, vit1.inverse_b = vit_norm(stream_mid1, w1, 1)
     vit1.normed_b = gather(normed_b1)
     vit1.hidden, vit1.slope, top_partial = mlp(
-        flat(vit1.normed_b), w1.fc_in, w1.fc_out
+        flat(vit1.normed_b), w1.fc_in, w1.fc_out, (out_conv,)
     )
 
     norm_sums = [None, None]
@@ -996,7 +1007,7 @@
     def row_grads(kept, grad_rows, grad_own, *earlier):
         sides = lax.axis_size(DP)
         pairs = [
-            product(by_relative(left), by_relative(after(right, *earlier), TENSOR), 0, 0)
+            product(by_relative(left), after(right, *earlier), 0, 0)
             for left, right in ((kept.pooled, grad_rows), (flat(grad_own), kept.attended))
         ]
         blocks = [pair.astype(BF16).reshape(sides, -1, model_width) for pair in pairs]
@@ -1023,14 +1034,16 @@
     )
     tap_sums[1] = jnp.concatenate([tap_sum, gate_sum[None]], 0)
 
+    squares = total_over(both_images(square0, square1, grad_mid1_own), TENSOR)
+    rms_conv = jnp.sqrt(squares)[None]
     grad_map1, scaled1 = spread_back(
-        grad_pooled1, portion(dy_conv).reshape(grid0.shape), w1.gain[1]
+        grad_pooled1, portion(dy_conv).reshape(grid0.shape), w1.gain[1], (rms_conv,)
     )
     grad_branch1 = gather(flat(scaled1))
     grad_mid0, mlp0, sums_b0 = back_to_middle(
         grad_stream, grad_stream_full, vit0, w0, lambda partial: (), scaled1
     )
-    rows1 = Reduction(row_grads(vit1, grad_rows1, grad_mid1_own, scaled1), True)
+    rows1 = Reduction(row_grads(vit1, grad_rows1, grad_mid1_own, scaled1))
     grad_mid0_own = grad_mid0.astype(BF16)
     rows1.step(grad_mid0_own)
     grad_in0, qkv0, sums_a0 = back_to_start(
@@ -1053,19 +1066,23 @@
         features_to_holders(grad_last), vit0, places, w0, (conv_in1.partial, conv_out1.partial)
     )
     tap_sums[0] = jnp.concatenate([tap_sum, gate_sum[None]], 0)
-    grad_grid1 = depthwise(grad_mixed1, w1.dw, 7, grad_map1, True)
+    ready = step_all([conv_out1, conv_in1], conv_in1.partial, conv_out1.partial)
+    grad_grid1 = depthwise(
+        grad_mixed1, w1.dw, 7, grad_map1, True, F32, ready + [rows1.partial]
+    )
     grad_next = grad_grid1.astype(BF16)
 
-    ready = step_all([mlp0, qkv], grad_grid1)
+    ready = step_all([mlp0, qkv, conv_out1], grad_grid1)
     grad_map0, scaled0 = spread_back(grad_pooled0, grad_next, w0.gain[1], ready)
     grad_branch0 = gather(flat(scaled0))
-    step_all([conv_out1, conv_in1], scaled0)
-    grad_fc = over_sections(after(mlp0.partial, scaled0), mlp1.partial)
+    fc = Sections(after(mlp0.partial, scaled0), mlp1.partial)
     half = qkv.partial.shape[1] // 2
-    grad_qkv = over_sections(after(qkv.partial[:, :half], scaled0), qkv.partial[:, half:])
-    rows0 = Reduction(row_grads(vit0, grad_rows0, grad_mid0_own), True)
+    sections_qkv = Sections(after(qkv.partial[:, :half], scaled0), qkv.partial[:, half:])
+    rows0 = Reduction(row_grads(vit0, grad_rows0, grad_mid0_own, scaled0))
+    grad_vit = both_images(grad_in0[None], grad_in1[None], scaled0)
+    grad_vit = grad_vit.reshape((1, -1) + grad_in0.shape[1:])
     taps1 = depthwise_taps(conv1.grid, grad_mixed1, 7, later_than=(scaled0,))
-    ready = step_all([conv_out1, conv_in1], taps1)
+    ready = step_all([conv_in1], taps1)
     rows0.step(*ready)
     (grad_hidden0,), parts = wide_mlp(
         0,
@@ -1074,7 +1091,7 @@
         second,
         tile,
         conv0.slope,
-        ready + [rows0.partial, grad_fc, grad_qkv],
+        ready + [rows0.partial, fc.got, sections_qkv.got, grad_vit],
     )
     grad_normed0 = scatter_parts(parts)
     rows0.step(parts)
@@ -1083,21 +1100,30 @@
     conv_out0.step(conv_in0.partial)
     conv_in0.step(conv_out0.partial)
     conv_out0.step(conv_in0.partial)
-    rows1.step(conv_in0.partial)
-    grad_normed0 = after(grad_normed0, conv_in0.partial, conv_out0.partial)
+    grad_normed0 = after(grad_normed0, conv_out0.partial)
+    row_parts = jnp.concatenate([rows0.partial, rows1.partial], 0)
+    row_parts = row_parts.reshape(row_parts.shape[0], count, -1).swapaxes(0, 1)
+    row_sums = lax.psum_scatter(
+        after(row_parts, grad_normed0), TENSOR, scatter_dimension=0, tiled=False
+    )
     grad_mixed0, gain0, shift0 = conv_norm_back(grad_normed0, conv0, w0)
-    grad_grid0 = depthwise(grad_mixed0, w0.dw, 7, grad_map0, True)
-    grad_conv_out = over_sections(conv_out0.partial, conv_out1.partial)
+    conv_in0.step(conv_out0.partial)
+    grad_grid0 = depthwise(
+        grad_mixed0, w0.dw, 7, grad_map0, True, F32, (conv_in0.partial,)
+    )
+    conv_out = Sections(conv_out0.partial, conv_out1.partial)
     grad_conv = both_images(grad_grid0, grad_grid1)
+    conv_in = Sections(conv_in0.partial, conv_in1.partial)
     taps0 = depthwise_taps(conv0.grid, grad_mixed0, 7, later_than=(grad_grid0,))
-    conv_in0.step(grad_grid0)
-    grad_conv_in = over_sections(conv_in0.partial, conv_in1.partial)
-    step_all([rows0, rows1], grad_grid0)
     stream_out1 = stream_mid1 + scatter_tokens(
-        after(top_partial, grad_normed0).reshape(stream_shape(vit1))
-    )
-    rows0.step(taps0)
-    grad_proj_attn = over_sections(rows0.partial, rows1.partial)
+        after(top_partial, row_sums).reshape(stream_shape(vit1))
+    )
+    grad_fc = fc.total(taps0)
+    grad_qkv = sections_qkv.total(taps0)
+    grad_conv_out = conv_out.total(taps0)
+    row_blocks = jnp.split(row_sums, 2, 0)
+    grad_proj_attn = over_sections(after(row_blocks[0], taps0), row_blocks[1])
+    grad_conv_in = conv_in.total(taps0)
     proj_rows = channels // lax.axis_size(DP)
     scale1 = jnp.sum(flat(grad_map1) * conv1.branch, 0)
     scale0 = jnp.sum(flat(grad_map0) * conv0.branch, 0)
@@ -1106,25 +1132,46 @@
         return total_over(select(*pair) + traded(select(*pair[::-1]), PIPE, 1), DP)
 
     token_terms = [
-        jnp.concatenate([widen(tap_sums[layer], model_width, 1), norm_sums[layer]], 0)
+        jnp.concatenate(
+            [
+                widen(after(tap_sums[layer], grad_grid0), model_width, 1),
+                after(norm_sums[layer], grad_grid0),
+            ],
+            0,
+        )
         for layer in range(2)
     ]
-    token_sums = total_over(over_images(token_terms), TENSOR)
-    column_sums = over_images(
-        [
-            jnp.concatenate([taps0, jnp.stack([gain0, scale0, shift0])], 0),
-            jnp.concatenate([taps1, jnp.stack([gain1, scale1, shift1])], 0),
-        ]
-    )
-
-    out_conv = both_images(grid1, grid2, grad_mid1_own).reshape(1, -1, cells, own_channels)
+    token_terms = total_over(jnp.concatenate(token_terms, 0), TENSOR)
+
+    def rows_of_lanes(values):
+        return values.reshape(-1, LANES)
+
+    column_terms = [
+        jnp.concatenate([taps0, jnp.stack([gain0, scale0, shift0])], 0),
+        jnp.concatenate([taps1, jnp.stack([gain1, scale1, shift1])], 0),
+    ]
+    token_rows = side + 5
+    column_sums, token_sums = jnp.split(
+        over_images(
+            [
+                jnp.concatenate(
+                    [
+                        rows_of_lanes(columns),
+                        rows_of_lanes(token_terms[layer * token_rows : (layer + 1) * token_rows]),
+                    ],
+                    0,
+                )
+                for layer, columns in enumerate(column_terms)
+            ]
+        ),
+        [column_terms[0].size // LANES],
+    )
+    column_sums = column_sums.reshape(column_terms[0].shape)
+    token_sums = token_sums.reshape(token_rows, model_width)
+
     out_vit = both_images(stream1, stream_out1.astype(BF16))[None]
-    squares = total_over(both_images(square0, square1, grad_mid1_own), TENSOR)
-    rms_conv = jnp.sqrt(squares)[None]
     mean_squares = [jnp.mean(out * out, -1) for out in (stream_out0, stream_out1)]
     rms_vit = jnp.sqrt(both_images(*mean_squares))[None]
-    grad_vit = both_images(grad_in0[None], grad_in1[None], grad_last)
-    grad_vit = grad_vit.reshape((1, -1) + grad_in0.shape[1:])
     return (
         out_vit,
         out_conv,

time: 1350 us -> 1330 us (0.985)
  Pallas kernels: 219 us -> 200 us
    ppermute x60, waiting for transfers between devices: 162 us -> 183 us  [turned(): lax.ppermute(values, TENSOR, [(i, (i + by) % count) for i in range(count)])]
    pallas_call x46 -> x42, Pallas kernels: 146 us -> 126 us  [run(): pl.pallas_call(without_extra, in_specs=list(in_specs) + [ANYWHERE] * extr...]
    ppermute x61 -> x54, waiting for transfers between devices: 207 us -> 190 us  [traded(): lax.ppermute(array, axis, [(i, i ^ bit) for i in range(lax.axis_size(axis...]
    ppermute x61 -> x54, starting transfers between devices: 51.5 us -> 47 us  [traded(): lax.ppermute(array, axis, [(i, i ^ bit) for i in range(lax.axis_size(axis...]
    unnamed x762 -> x732, local copies, waits for them, and re-layouts: 88.1 us -> 87.8 us
  transfers between devices with their start and end apart: 142 -> 136, of which waited for: 65 -> 70; matrix products, arithmetic and copies ran while one was open for 24% -> 25% of each run, Pallas kernels for 12% -> 11%
where the time goes in v4:
time: 1330 us; the launch traced here: 1320 us
  waiting for transfers between devices  537 us (40%)
  Pallas kernels  200 us (15%)
  local copies, waits for them, and re-layouts  179 us (13%)
  other arithmetic  162 us (12%)
  starting transfers between devices  132 us (10%)
  matrix products  87.9 us (7%)
  between operations  19.9 us (1%)
    ppermute x54, waiting for transfers between devices, traded(): lax.ppermute(array, axis, [(i, i ^ bit) for i in range(lax.axis_size(axis...  190 us
    ppermute x60, waiting for transfers between devices, turned(): lax.ppermute(values, TENSOR, [(i, (i + by) % count) for i in range(count)])  183 us
    pallas_call x42, Pallas kernels, run(): pl.pallas_call(without_extra, in_specs=list(in_specs) + [ANYWHERE] * extr...  126 us
    all_gather x10, waiting for transfers between devices, gather(): return lax.all_gather(values, TENSOR, axis=1, tiled=True)  88.7 us
    unnamed x732, local copies, waits for them, and re-layouts  87.8 us
    dot_general x26, matrix products, product(): lax.dot_general(left, right, (((left_axis,), (right_axis,)), ((), ())), p...  84.5 us
    ppermute x60, starting transfers between devices, turned(): lax.ppermute(values, TENSOR, [(i, (i + by) % count) for i in range(count)])  82.2 us
    pallas_call x4, Pallas kernels, wide_mlp(): pl.pallas_call(without_extra, grid_spec=pltpu.PrefetchScalarGridSpec(num_...  73.6 us
  transfers between devices with their start and end apart: 136, of which 70 were waited for; matrix products, arithmetic and copies ran while one was open for 25% of the time, Pallas kernels for 11%

profile of v4, /device:TPU:0, one launch (start us, length us, event | category | flops | bytes accessed | tf_op | source)
XLA Modules:
  0.0 1316.8 jit_solution(8523892130247075125)
XLA Ops:
  39.1 20.6 %collective-permute-done.5.refs_0_ = bf16[384,1536]{1,0:T(8,128)(2,1)} collective-permute-done((bf16[384,1536]{1,0:T(8,128)(2,1)}, bf16[384,1536]{1,0:T(8,128)(2,1)}, u32[]{:S(2)}, u32[]{:S(2)}) %collective-permute-start.5) | collective-permute-done | bytes 1179680 | tf_op jit(solution)/shard_map/ppermute | solution.py:508
  62.0 11.6 all-gather.13.cloned.1.call-done.refs_1_
  76.3 9.4 collective-permute-done.6.refs_0_
  91.8 20.5 %collective-permute-done.9.refs_0_ = bf16[384,1536]{1,0:T(8,128)(2,1)} collective-permute-done((bf16[384,1536]{1,0:T(8,128)(2,1)}, bf16[384,1536]{1,0:T(8,128)(2,1)}, u32[]{:S(2)}, u32[]{:S(2)}) %collective-permute-start.9) | collective-permute-done | bytes 1179680 | tf_op jit(solution)/shard_map/ppermute | solution.py:508
  112.3 8.5 collective-permute-done.10.refs_1_.refs_0_
  128.9 9.3 all-gather.15.cloned.1.call-done.refs_0_
  138.2 18.8 %shard_map.357 = (bf16[1024,1536]{1,0:T(8,128)(2,1)}, bf16[1024,1536]{1,0:T(8,128)(2,1)}, bf16[4,1024,384]{2,1,0:T(8,128)(2,1)}) custom-call(s32[2]{0:T(128)} %pad_add_fusion.meta_ref, bf16[1024,1536]{1,0:T(8,128)(2,1)} %all-gather.15.cloned.1.call-done.refs_0_, bf16[1536,1536]{1,0:T(8,128)(2,1)} %bitcast.562, ...), custom_call_target="tpu_custom_call" | custom-call | tf_op jit(solution)/shard_map/pallas_call | solution.py:267
  178.1 37.9 %reduce-scatter.12.cloned.1.call-done = bf16[1,1024,384]{2,1,0:T(8,128)(2,1)} async-done(((bf16[4,1024,384]{2,1,0:T(8,128)(2,1)}), bf16[1,1024,384]{2,1,0:T(8,128)(2,1)}) %reduce-scatter.12.cloned.1.call-update) | async-done | bytes 786448 | tf_op jit(solution)/shard_map/reduce_scatter | solution.py:644
  257.2 10.2 collective-permute-done.19
  295.0 22.0 %collective-permute-done.28.refs_0_ = bf16[512,1024]{1,0:T(8,128)(2,1)S(1)} collective-permute-done((bf16[512,1024]{1,0:T(8,128)(2,1)}, bf16[512,1024]{1,0:T(8,128)(2,1)S(1)}, u32[]{:S(2)}, u32[]{:S(2)}) %collective-permute-start.28) | collective-permute-done | bytes 1048608 | tf_op jit(solution)/shard_map/ppermute | solution.py:508
  318.0 19.0 %shard_map.368 = (bf16[1024,1536]{1,0:T(8,128)(2,1)}, bf16[1024,1536]{1,0:T(8,128)(2,1)}, bf16[4,1024,384]{2,1,0:T(8,128)(2,1)}) custom-call(s32[2]{0:T(128)} %pad_add_fusion.1.meta_ref, bf16[1024,1536]{1,0:T(8,128)(2,1)} %all-gather.19.cloned.1.call-done.refs_0_, bf16[1536,1536]{1,0:T(8,128)(2,1)} %bitcast.563, ...), custom_call_target="tpu_custom_call" | custom-call | tf_op jit(solution)/shard_map/pallas_call | solution.py:267
  350.8 10.0 collective-permute-done.32
  370.9 8.4 collective-permute-start.29
  389.0 13.4 %collective-permute-done.30 = bf16[1,144,256]{2,1,0:T(8,128)(2,1)S(1)} collective-permute-done((bf16[1,144,256]{2,1,0:T(8,128)(2,1)S(1)}, bf16[1,144,256]{2,1,0:T(8,128)(2,1)S(1)}, u32[]{:S(2)}, u32[]{:S(2)}) %collective-permute-start.30) | collective-permute-done | bytes 73760 | tf_op jit(solution)/shard_map/ppermute | solution.py:598
  422.1 8.5 collective-permute-done.37
  495.9 30.0 %all-gather.23.cloned.1.call-done = bf16[1,576,1024]{2,1,0:T(8,128)(2,1)} async-done(((bf16[1,144,1024]{2,1,0:T(8,128)(2,1)}), bf16[1,576,1024]{2,1,0:T(8,128)(2,1)}) %all-gather.23.cloned.1.call-update) | async-done | bytes 1179664 | tf_op jit(solution)/shard_map/all_gather | solution.py:593
  547.9 18.6 %collective-permute-done.48 = bf16[1,32,32,384]{3,2,1,0:T(8,128)(2,1)S(1)} collective-permute-done((bf16[1,32,32,384]{3,2,1,0:T(8,128)(2,1)}, bf16[1,32,32,384]{3,2,1,0:T(8,128)(2,1)S(1)}, u32[]{:S(2)}, u32[]{:S(2)}) %collective-permute-start.48) | collective-permute-done | bytes 786464 | tf_op jit(solution)/shard_map/ppermute | solution.py:508
  603.0 14.0 %reduce-scatter.18.cloned.1.call-done = bf16[1,144,1024]{2,1,0:T(8,128)(2,1)} async-done(((bf16[1,576,1024]{2,1,0:T(8,128)(2,1)}), bf16[1,144,1024]{2,1,0:T(8,128)(2,1)}) %reduce-scatter.18.cloned.1.call-update) | async-done | bytes 294928 | tf_op jit(solution)/shard_map/reduce_scatter | solution.py:640
  669.0 14.7 %collective-permute-done.53.refs_1_ = bf16[256,2048]{1,0:T(8,128)(2,1)S(1)} collective-permute-done((bf16[256,2048]{1,0:T(8,128)(2,1)}, bf16[256,2048]{1,0:T(8,128)(2,1)S(1)}, u32[]{:S(2)}, u32[]{:S(2)}) %collective-permute-start.53) | collective-permute-done | bytes 1048608 | tf_op jit(solution)/shard_map/ppermute | solution.py:508
  729.4 12.7 collective-permute-done.61
  796.6 11.3 collective-permute-done.67
  837.2 13.7 %all-gather.29.cloned.1.call-done.refs_0_ = bf16[1024,1536]{1,0:T(8,128)(2,1)} async-done(((bf16[1024,384]{1,0:T(8,128)(2,1)}), bf16[1024,1536]{1,0:T(8,128)(2,1)}) %all-gather.29.cloned.1.call-update) | async-done | bytes 3145744 | tf_op jit(solution)/shard_map/all_gather | solution.py:593
  850.9 17.9 %shard_map.402 = (bf16[1024,1536]{1,0:T(8,128)(2,1)}, bf16[4,1024,384]{2,1,0:T(8,128)(2,1)}) custom-call(s32[2]{0:T(128)} %pad_add_fusion.1.meta_ref, bf16[1024,1536]{1,0:T(8,128)(2,1)} %all-gather.29.cloned.1.call-done.refs_0_, bf16[1024,1536]{1,0:T(8,128)(2,1)} %get-tuple-element.65.refs_1_, bf16[1536,1536]{1,0:T(8,128)(2,1)} %bitcast.564, ...), custom_call_target="tpu_custom_call" | custom-call | tf_op jit(solution)/shard_map/pallas_call | solution.py:267
  869.0 9.4 convolution_convert_fusion.3.refs_2_.refs_0_
  901.1 12.2 collective-permute-done.70
  924.0 10.6 collective-permute-done.74
  934.7 8.2 collective-permute-done.75
  954.4 8.2 collective-permute-done.77
  1050.4 10.9 collective-permute-done.91.refs_1_
  1076.6 8.0 all-gather.31.cloned.1.call-done.refs_0_
  1084.6 17.9 %shard_map.424 = (bf16[1024,1536]{1,0:T(8,128)(2,1)}, bf16[4,1024,384]{2,1,0:T(8,128)(2,1)}) custom-call(s32[2]{0:T(128)} %pad_add_fusion.meta_ref, bf16[1024,1536]{1,0:T(8,128)(2,1)} %all-gather.31.cloned.1.call-done.refs_0_, bf16[1024,1536]{1,0:T(8,128)(2,1)} %get-tuple-element.71.refs_1_, bf16[1536,1536]{1,0:T(8,128)(2,1)} %bitcast.565, ...), custom_call_target="tpu_custom_call" | custom-call | tf_op jit(solution)/shard_map/pallas_call | solution.py:267
  1180.4 14.1 %collective-permute-done.103.refs_1_ = bf16[384,1536]{1,0:T(8,128)(2,1)} collective-permute-done((bf16[384,1536]{1,0:T(8,128)(2,1)}, bf16[384,1536]{1,0:T(8,128)(2,1)}, u32[]{:S(2)}, u32[]{:S(2)}) %collective-permute-start.103) | collective-permute-done | bytes 1179680 | tf_op jit(solution)/shard_map/ppermute | solution.py:508
  (1421 shorter events, 836.5 us)
Async XLA Ops:
  7.2 54.7 %all-gather.33.cloned.1.call-start = ((), (), s32[]{:S(2)}) async-start(), calls=%async_computation.32 | async-start | bytes 1310720 | tf_op jit(solution)/shard_map/all_gather | solution.py:902
  9.1 64.5 %all-gather.13.cloned.1.call-start = ((), (), s32[]{:S(2)}) async-start(), calls=%async_computation.11 | async-start | bytes 1474560 | tf_op jit(solution)/shard_map/all_gather | solution.py:593
  59.8 78.4 %all-gather.15.cloned.1.call-start = ((), (), s32[]{:S(2)}) async-start(), calls=%async_computation.12 | async-start | bytes 3932160 | tf_op jit(solution)/shard_map/all_gather | solution.py:593
  73.6 142.4 %reduce-scatter.12.cloned.1.call-start = ((), (), s32[]{:S(2)}) async-start(), calls=%async_computation.13 | async-start | bytes 3932160 | tf_op jit(solution)/shard_map/reduce_scatter | solution.py:644
  157.1 160.9 %all-gather.19.cloned.1.call-start = ((), (), s32[]{:S(2)}) async-start(), calls=%async_computation.15 | async-start | bytes 3932160 | tf_op jit(solution)/shard_map/all_gather | solution.py:593
  169.0 48.4 %collective-permute-start.13 = (bf16[512,1024]{1,0:T(8,128)(2,1)}, bf16[512,1024]{1,0:T(8,128)(2,1)S(1)}, u32[]{:S(2)}, u32[]{:S(2)}) collective-permute-start(bf16[512,1024]{1,0:T(8,128)(2,1)} %shard_map.359), channel_id=1, source_target_pairs={{0,16},{16,0},{1,17},{17,1},{2,18},{18,2},{3,19},{19,3},{4,20},{20... | collective-permute-start | bytes 3145736 | tf_op jit(solution)/shard_map/ppermute | solution.py:508
  171.4 46.1 %collective-permute-start.12 = (bf16[512,768]{1,0:T(8,128)(2,1)}, bf16[512,768]{1,0:T(8,128)(2,1)}, u32[]{:S(2)}, u32[]{:S(2)}) collective-permute-start(bf16[512,768]{1,0:T(8,128)(2,1)} %shard_map.358), channel_id=1, source_target_pairs={{0,16},{16,0},{1,17},{17,1},{2,18},{18,2},{3,19},{19,3},{4,20},{20... | collective-permute-start | bytes 2359304 | tf_op jit(solution)/shard_map/ppermute | solution.py:508
  238.8 124.7 %all-gather.17.cloned.1.call-start = ((), (), s32[]{:S(2)}) async-start(), calls=%async_computation.14 | async-start | bytes 1474560 | tf_op jit(solution)/shard_map/all_gather | solution.py:593
  292.1 119.7 %reduce-scatter.14.cloned.1.call-start = ((), (), s32[]{:S(2)}) async-start(), calls=%async_computation.17 | async-start | bytes 3932160 | tf_op jit(solution)/shard_map/reduce_scatter | solution.py:644
  337.1 114.3 %all-gather.21.cloned.1.call-start = ((), (), s32[]{:S(2)}) async-start(), calls=%async_computation.16 | async-start | bytes 1474560 | tf_op jit(solution)/shard_map/all_gather | solution.py:593
  419.2 72.4 %reduce-scatter.16.cloned.1.call-start = ((), (), s32[]{:S(2)}) async-start(), calls=%async_computation.18 | async-start | bytes 1474560 | tf_op jit(solution)/shard_map/reduce_scatter | solution.py:640
  457.8 68.1 %all-gather.23.cloned.1.call-start = ((), (), s32[]{:S(2)}) async-start(), calls=%async_computation.19 | async-start | bytes 1474560 | tf_op jit(solution)/shard_map/all_gather | solution.py:593
  495.9 79.5 %all-gather.25.cloned.1.call-start = ((), (), s32[]{:S(2)}) async-start(), calls=%async_computation.20 | async-start | bytes 1474560 | tf_op jit(solution)/shard_map/all_gather | solution.py:593
  545.1 71.8 %reduce-scatter.18.cloned.1.call-start = ((), (), s32[]{:S(2)}) async-start(), calls=%async_computation.21 | async-start | bytes 1474560 | tf_op jit(solution)/shard_map/reduce_scatter | solution.py:640
  588.5 96.4 %reduce-scatter.20.cloned.1.call-start = ((), (), s32[]{:S(2)}) async-start(), calls=%async_computation.22 | async-start | bytes 1474560 | tf_op jit(solution)/shard_map/reduce_scatter | solution.py:640
  647.6 99.5 %all-gather.27.cloned.1.call-start = ((), (), s32[]{:S(2)}) async-start(), calls=%async_computation.23 | async-start | bytes 1474560 | tf_op jit(solution)/shard_map/all_gather | solution.py:593
  706.3 75.7 %reduce-scatter.22.cloned.1.call-start = ((), (), s32[]{:S(2)}) async-start(), calls=%async_computation.24 | async-start | bytes 1474560 | tf_op jit(solution)/shard_map/reduce_scatter | solution.py:640
  753.8 97.1 %all-gather.29.cloned.1.call-start = ((), (), s32[]{:S(2)}) async-start(), calls=%async_computation.26 | async-start | bytes 3932160 | tf_op jit(solution)/shard_map/all_gather | solution.py:593
  756.4 126.5 %reduce-scatter.24.cloned.1.call-start = ((), (), s32[]{:S(2)}) async-start(), calls=%async_computation.25 | async-start | bytes 1474560 | tf_op jit(solution)/shard_map/reduce_scatter | solution.py:640
  816.4 157.9 %reduce-scatter.26.cloned.1.call-start = ((), (), s32[]{:S(2)}) async-start(), calls=%async_computation.27 | async-start | bytes 3932160 | tf_op jit(solution)/shard_map/reduce_scatter | solution.py:644
  827.1 121.2 %collective-permute-start.85 = (bf16[512,2048]{1,0:T(8,128)(2,1)}, bf16[512,2048]{1,0:T(8,128)(2,1)}, u32[]{:S(2)}, u32[]{:S(2)}) collective-permute-start(bf16[512,2048]{1,0:T(8,128)(2,1)} %fusion.16), channel_id=1, source_target_pairs={{0,4},{4,0},{8,12},{12,8},{1,5},{5,1},{9,13},{13,9},{2,6},{6,2},{1... | collective-permute-start | bytes 6291464 | tf_op jit(solution)/shard_map/ppermute | solution.py:508
  836.7 107.6 %collective-permute-start.87 = (bf16[512,1536]{1,0:T(8,128)(2,1)}, bf16[512,1536]{1,0:T(8,128)(2,1)}, u32[]{:S(2)}, u32[]{:S(2)}) collective-permute-start(bf16[512,1536]{1,0:T(8,128)(2,1)} %fusion.18), channel_id=1, source_target_pairs={{0,4},{4,0},{8,12},{12,8},{1,5},{5,1},{9,13},{13,9},{2,6},{6,2},{1... | collective-permute-start | bytes 4718600 | tf_op jit(solution)/shard_map/ppermute | solution.py:508
  868.9 215.7 %all-gather.31.cloned.1.call-start = ((), (), s32[]{:S(2)}) async-start(), calls=%async_computation.28 | async-start | bytes 3932160 | tf_op jit(solution)/shard_map/all_gather | solution.py:593
  923.1 46.3 %collective-permute-start.82 = (bf16[768,1536]{1,0:T(8,128)(2,1)S(1)}, bf16[768,1536]{1,0:T(8,128)(2,1)S(1)}, u32[]{:S(2)}, u32[]{:S(2)}) collective-permute-start(bf16[768,1536]{1,0:T(8,128)(2,1)S(1)} %slice.333), channel_id=1, source_target_pairs={{0,4},{4,0},{8,12},{12,8},{1,5},{5,1},{9,13},{13,9},{2,6},{6,2},{1... | collective-permute-start | bytes 7077896 | tf_op jit(solution)/shard_map/ppermute | solution.py:508
  948.7 58.7 %collective-permute-start.88 = (bf16[256,1536]{1,0:T(8,128)(2,1)}, bf16[256,1536]{1,0:T(8,128)(2,1)}, u32[]{:S(2)}, u32[]{:S(2)}) collective-permute-start(bf16[256,1536]{1,0:T(8,128)(2,1)} %slice.341), channel_id=1, source_target_pairs={{0,8},{4,12},{8,0},{12,4},{1,9},{5,13},{9,1},{13,5},{2,10},{6,14},... | collective-permute-start | bytes 2359304 | tf_op jit(solution)/shard_map/ppermute | solution.py:508
  953.9 50.2 %collective-permute-start.86 = (bf16[256,2048]{1,0:T(8,128)(2,1)}, bf16[256,2048]{1,0:T(8,128)(2,1)S(1)}, u32[]{:S(2)}, u32[]{:S(2)}) collective-permute-start(bf16[256,2048]{1,0:T(8,128)(2,1)} %slice.338), channel_id=1, source_target_pairs={{0,8},{4,12},{8,0},{12,4},{1,9},{5,13},{9,1},{13,5},{2,10},{6,14},... | collective-permute-start | bytes 3145736 | tf_op jit(solution)/shard_map/ppermute | solution.py:508
  972.8 44.1 %collective-permute-start.89 = (bf16[384,1536]{1,0:T(8,128)(2,1)}, bf16[384,1536]{1,0:T(8,128)(2,1)}, u32[]{:S(2)}, u32[]{:S(2)}) collective-permute-start(bf16[384,1536]{1,0:T(8,128)(2,1)} %slice.342), channel_id=1, source_target_pairs={{0,8},{4,12},{8,0},{12,4},{1,9},{5,13},{9,1},{13,5},{2,10},{6,14},... | collective-permute-start | bytes 3538952 | tf_op jit(solution)/shard_map/ppermute | solution.py:508
  1022.4 151.8 %reduce-scatter.28.cloned.1.call-start = ((), (), s32[]{:S(2)}) async-start(), calls=%async_computation.29 | async-start | bytes 3932160 | tf_op jit(solution)/shard_map/reduce_scatter | solution.py:644
  1102.5 162.5 %reduce-scatter.30.cloned.1.call-start = ((), (), s32[]{:S(2)}) async-start(), calls=%async_computation.30 | async-start | bytes 3276800 | tf_op jit(solution)/shard_map/reduce_scatter | solution.py:1106
  1176.6 119.8 %reduce-scatter.32.cloned.1.call-start = ((), (), s32[]{:S(2)}) async-start(), calls=%async_computation.31 | async-start | bytes 1474560 | tf_op jit(solution)/shard_map/reduce_scatter | solution.py:640
  1201.8 54.3 %collective-permute-start.112 = (bf16[384,1536]{1,0:T(8,128)(2,1)}, bf16[384,1536]{1,0:T(8,128)(2,1)}, u32[]{:S(2)}, u32[]{:S(2)}) collective-permute-start(bf16[384,1536]{1,0:T(8,128)(2,1)} %broadcast_select_fusion.7), channel_id=1, source_target_pairs={{0,16},{16,0},{1,17},{17,1},{2,18},{18,2},{3,19},{19,3},{4,20},{20... | collective-permute-start | bytes 3538952 | tf_op jit(solution)/shard_map/ppermute | solution.py:508
  1203.3 58.4 %collective-permute-start.113 = (bf16[384,1536]{1,0:T(8,128)(2,1)}, bf16[384,1536]{1,0:T(8,128)(2,1)}, u32[]{:S(2)}, u32[]{:S(2)}) collective-permute-start(bf16[384,1536]{1,0:T(8,128)(2,1)} %broadcast_select_fusion.6), channel_id=1, source_target_pairs={{0,16},{16,0},{1,17},{17,1},{2,18},{18,2},{3,19},{19,3},{4,20},{20... | collective-permute-start | bytes 3538952 | tf_op jit(solution)/shard_map/ppermute | solution.py:508
  (417 other events, 5581.7 us)
Sparse Core Ops, SparseCore 0:
  10.2 31.7 all-gather.32
  44.1 29.4 all-gather.12
  75.7 62.4 all-gather.14
  157.2 58.8 reduce-scatter.11
  238.9 75.4 all-gather.18
  316.4 29.0 all-gather.16
  347.8 64.0 reduce-scatter.13
  419.4 31.9 all-gather.20
  457.9 33.6 reduce-scatter.15
  496.0 29.8 all-gather.22
  545.3 30.1 all-gather.24
  588.6 28.2 reduce-scatter.17
  647.7 27.7 reduce-scatter.19
  706.4 40.6 all-gather.26
  753.9 28.0 reduce-scatter.21
  784.0 66.8 all-gather.28
  853.7 29.1 reduce-scatter.23
  885.1 70.2 reduce-scatter.25
  1022.5 62.0 all-gather.30
  1102.6 58.8 reduce-scatter.27
  1176.7 52.6 reduce-scatter.29
  1265.2 31.2 reduce-scatter.31

commit v5 on v4

--- a/solution.py
+++ b/solution.py
@@ -1134,8 +1134,8 @@
     token_terms = [
         jnp.concatenate(
             [
-                widen(after(tap_sums[layer], grad_grid0), model_width, 1),
-                after(norm_sums[layer], grad_grid0),
+                widen(after(tap_sums[layer], scaled0), model_width, 1),
+                after(norm_sums[layer], scaled0),
             ],
             0,
         )

time: 1330 us -> 1340 us (level)
    unnamed x732 -> x734, local copies, waits for them, and re-layouts: 87.8 us -> 94.9 us
  transfers between devices with their start and end apart: 136 -> 136, of which waited for: 70 -> 66; matrix products, arithmetic and copies ran while one was open for 25% -> 25% of each run, Pallas kernels for 11% -> 11%
where the time goes in v5:
time: 1340 us; the launch traced here: 1330 us
  waiting for transfers between devices  538 us (40%)
  Pallas kernels  203 us (15%)
  local copies, waits for them, and re-layouts  185 us (14%)
  other arithmetic  164 us (12%)
  starting transfers between devices  125 us (9%)
  matrix products  91.5 us (7%)
  between operations  19.9 us (1%)
    ppermute x54, waiting for transfers between devices, traded(): lax.ppermute(array, axis, [(i, i ^ bit) for i in range(lax.axis_size(axis...  203 us
    ppermute x60, waiting for transfers between devices, turned(): lax.ppermute(values, TENSOR, [(i, (i + by) % count) for i in range(count)])  184 us
    pallas_call x42, Pallas kernels, run(): pl.pallas_call(without_extra, in_specs=list(in_specs) + [ANYWHERE] * extr...  129 us
    unnamed x734, local copies, waits for them, and re-layouts  94.9 us
    dot_general x26, matrix products, product(): lax.dot_general(left, right, (((left_axis,), (right_axis,)), ((), ())), p...  87.3 us
    ppermute x60, starting transfers between devices, turned(): lax.ppermute(values, TENSOR, [(i, (i + by) % count) for i in range(count)])  82.5 us
    all_gather x10, waiting for transfers between devices, gather(): return lax.all_gather(values, TENSOR, axis=1, tiled=True)  78.8 us
    pallas_call x4, Pallas kernels, wide_mlp(): pl.pallas_call(without_extra, grid_spec=pltpu.PrefetchScalarGridSpec(num_...  73.9 us
  transfers between devices with their start and end apart: 136, of which 66 were waited for; matrix products, arithmetic and copies ran while one was open for 25% of the time, Pallas kernels for 11%

profile of v5, /device:TPU:0, one launch (start us, length us, event | category | flops | bytes accessed | tf_op | source)
XLA Modules:
  0.0 1327.7 jit_solution(15401625717139218988)
XLA Ops:
  39.1 20.6 %collective-permute-done.5.refs_0_ = bf16[384,1536]{1,0:T(8,128)(2,1)} collective-permute-done((bf16[384,1536]{1,0:T(8,128)(2,1)}, bf16[384,1536]{1,0:T(8,128)(2,1)}, u32[]{:S(2)}, u32[]{:S(2)}) %collective-permute-start.5) | collective-permute-done | bytes 1179680 | tf_op jit(solution)/shard_map/ppermute | solution.py:508
  62.0 11.6 all-gather.13.cloned.1.call-done.refs_1_
  76.3 9.4 collective-permute-done.6.refs_0_
  91.8 20.5 %collective-permute-done.9.refs_0_ = bf16[384,1536]{1,0:T(8,128)(2,1)} collective-permute-done((bf16[384,1536]{1,0:T(8,128)(2,1)}, bf16[384,1536]{1,0:T(8,128)(2,1)}, u32[]{:S(2)}, u32[]{:S(2)}) %collective-permute-start.9) | collective-permute-done | bytes 1179680 | tf_op jit(solution)/shard_map/ppermute | solution.py:508
  112.3 8.5 collective-permute-done.10.refs_1_.refs_0_
  128.9 9.3 all-gather.15.cloned.1.call-done.refs_0_
  138.2 18.8 %shard_map.357 = (bf16[1024,1536]{1,0:T(8,128)(2,1)}, bf16[1024,1536]{1,0:T(8,128)(2,1)}, bf16[4,1024,384]{2,1,0:T(8,128)(2,1)}) custom-call(s32[2]{0:T(128)} %pad_add_fusion.meta_ref, bf16[1024,1536]{1,0:T(8,128)(2,1)} %all-gather.15.cloned.1.call-done.refs_0_, bf16[1536,1536]{1,0:T(8,128)(2,1)} %bitcast.562, ...), custom_call_target="tpu_custom_call" | custom-call | tf_op jit(solution)/shard_map/pallas_call | solution.py:267
  178.0 38.0 %reduce-scatter.12.cloned.1.call-done = bf16[1,1024,384]{2,1,0:T(8,128)(2,1)} async-done(((bf16[4,1024,384]{2,1,0:T(8,128)(2,1)}), bf16[1,1024,384]{2,1,0:T(8,128)(2,1)}) %reduce-scatter.12.cloned.1.call-update) | async-done | bytes 786448 | tf_op jit(solution)/shard_map/reduce_scatter | solution.py:644
  257.2 10.2 collective-permute-done.19
  295.0 22.0 %collective-permute-done.28.refs_0_ = bf16[512,1024]{1,0:T(8,128)(2,1)S(1)} collective-permute-done((bf16[512,1024]{1,0:T(8,128)(2,1)}, bf16[512,1024]{1,0:T(8,128)(2,1)S(1)}, u32[]{:S(2)}, u32[]{:S(2)}) %collective-permute-start.28) | collective-permute-done | bytes 1048608 | tf_op jit(solution)/shard_map/ppermute | solution.py:508
  318.0 19.2 %shard_map.368 = (bf16[1024,1536]{1,0:T(8,128)(2,1)}, bf16[1024,1536]{1,0:T(8,128)(2,1)}, bf16[4,1024,384]{2,1,0:T(8,128)(2,1)}) custom-call(s32[2]{0:T(128)} %pad_add_fusion.1.meta_ref, bf16[1024,1536]{1,0:T(8,128)(2,1)} %all-gather.19.cloned.1.call-done.refs_0_, bf16[1536,1536]{1,0:T(8,128)(2,1)} %bitcast.563, ...), custom_call_target="tpu_custom_call" | custom-call | tf_op jit(solution)/shard_map/pallas_call | solution.py:267
  351.0 10.0 collective-permute-done.32
  371.1 8.4 collective-permute-start.29
  389.2 13.3 %collective-permute-done.30 = bf16[1,144,256]{2,1,0:T(8,128)(2,1)S(1)} collective-permute-done((bf16[1,144,256]{2,1,0:T(8,128)(2,1)S(1)}, bf16[1,144,256]{2,1,0:T(8,128)(2,1)S(1)}, u32[]{:S(2)}, u32[]{:S(2)}) %collective-permute-start.30) | collective-permute-done | bytes 73760 | tf_op jit(solution)/shard_map/ppermute | solution.py:598
  422.1 8.5 collective-permute-done.37
  495.8 30.0 %all-gather.23.cloned.1.call-done = bf16[1,576,1024]{2,1,0:T(8,128)(2,1)} async-done(((bf16[1,144,1024]{2,1,0:T(8,128)(2,1)}), bf16[1,576,1024]{2,1,0:T(8,128)(2,1)}) %all-gather.23.cloned.1.call-update) | async-done | bytes 1179664 | tf_op jit(solution)/shard_map/all_gather | solution.py:593
  547.7 18.3 %collective-permute-done.48 = bf16[1,32,32,384]{3,2,1,0:T(8,128)(2,1)S(1)} collective-permute-done((bf16[1,32,32,384]{3,2,1,0:T(8,128)(2,1)}, bf16[1,32,32,384]{3,2,1,0:T(8,128)(2,1)S(1)}, u32[]{:S(2)}, u32[]{:S(2)}) %collective-permute-start.48) | collective-permute-done | bytes 786464 | tf_op jit(solution)/shard_map/ppermute | solution.py:508
  602.8 14.0 %reduce-scatter.18.cloned.1.call-done = bf16[1,144,1024]{2,1,0:T(8,128)(2,1)} async-done(((bf16[1,576,1024]{2,1,0:T(8,128)(2,1)}), bf16[1,144,1024]{2,1,0:T(8,128)(2,1)}) %reduce-scatter.18.cloned.1.call-update) | async-done | bytes 294928 | tf_op jit(solution)/shard_map/reduce_scatter | solution.py:640
  668.9 14.7 %collective-permute-done.53.refs_1_ = bf16[256,2048]{1,0:T(8,128)(2,1)S(1)} collective-permute-done((bf16[256,2048]{1,0:T(8,128)(2,1)}, bf16[256,2048]{1,0:T(8,128)(2,1)S(1)}, u32[]{:S(2)}, u32[]{:S(2)}) %collective-permute-start.53) | collective-permute-done | bytes 1048608 | tf_op jit(solution)/shard_map/ppermute | solution.py:508
  729.2 12.8 collective-permute-done.61
  799.2 10.2 collective-permute-done.67
  838.9 12.8 all-gather.29.cloned.1.call-done.refs_0_
  851.7 18.0 %shard_map.402 = (bf16[1024,1536]{1,0:T(8,128)(2,1)}, bf16[4,1024,384]{2,1,0:T(8,128)(2,1)}) custom-call(s32[2]{0:T(128)} %pad_add_fusion.1.meta_ref, bf16[1024,1536]{1,0:T(8,128)(2,1)} %all-gather.29.cloned.1.call-done.refs_0_, bf16[1024,1536]{1,0:T(8,128)(2,1)} %get-tuple-element.65.refs_1_, bf16[1536,1536]{1,0:T(8,128)(2,1)} %bitcast.564, ...), custom_call_target="tpu_custom_call" | custom-call | tf_op jit(solution)/shard_map/pallas_call | solution.py:267
  869.8 9.4 convolution_convert_fusion.3.refs_2_.refs_0_
  901.5 12.2 collective-permute-done.70
  924.8 12.7 collective-permute-done.74
  937.5 8.3 collective-permute-done.75
  955.7 8.1 collective-permute-done.77
  1051.5 11.1 collective-permute-done.91.refs_1_
  1086.2 17.9 %shard_map.424 = (bf16[1024,1536]{1,0:T(8,128)(2,1)}, bf16[4,1024,384]{2,1,0:T(8,128)(2,1)}) custom-call(s32[2]{0:T(128)} %pad_add_fusion.meta_ref, bf16[1024,1536]{1,0:T(8,128)(2,1)} %all-gather.31.cloned.1.call-done.refs_0_, bf16[1024,1536]{1,0:T(8,128)(2,1)} %get-tuple-element.71.refs_1_, bf16[1536,1536]{1,0:T(8,128)(2,1)} %bitcast.565, ...), custom_call_target="tpu_custom_call" | custom-call | tf_op jit(solution)/shard_map/pallas_call | solution.py:267
  1188.7 13.0 collective-permute-done.103.refs_1_
  1253.8 17.7 %collective-permute-done.109 = f32[268,128]{1,0:T(8,128)} collective-permute-done((f32[268,128]{1,0:T(8,128)}, f32[268,128]{1,0:T(8,128)}, u32[]{:S(2)}, u32[]{:S(2)}) %collective-permute-start.109) | collective-permute-done | bytes 137248 | tf_op jit(solution)/shard_map/ppermute | solution.py:508
  (1423 shorter events, 838.1 us)
Async XLA Ops:
  7.2 54.7 %all-gather.33.cloned.1.call-start = ((), (), s32[]{:S(2)}) async-start(), calls=%async_computation.32 | async-start | bytes 1310720 | tf_op jit(solution)/shard_map/all_gather | solution.py:902
  9.1 64.5 %all-gather.13.cloned.1.call-start = ((), (), s32[]{:S(2)}) async-start(), calls=%async_computation.11 | async-start | bytes 1474560 | tf_op jit(solution)/shard_map/all_gather | solution.py:593
  59.8 78.4 %all-gather.15.cloned.1.call-start = ((), (), s32[]{:S(2)}) async-start(), calls=%async_computation.12 | async-start | bytes 3932160 | tf_op jit(solution)/shard_map/all_gather | solution.py:593
  73.6 142.4 %reduce-scatter.12.cloned.1.call-start = ((), (), s32[]{:S(2)}) async-start(), calls=%async_computation.13 | async-start | bytes 3932160 | tf_op jit(solution)/shard_map/reduce_scatter | solution.py:644
  157.0 160.9 %all-gather.19.cloned.1.call-start = ((), (), s32[]{:S(2)}) async-start(), calls=%async_computation.15 | async-start | bytes 3932160 | tf_op jit(solution)/shard_map/all_gather | solution.py:593
  169.0 48.4 %collective-permute-start.13 = (bf16[512,1024]{1,0:T(8,128)(2,1)}, bf16[512,1024]{1,0:T(8,128)(2,1)S(1)}, u32[]{:S(2)}, u32[]{:S(2)}) collective-permute-start(bf16[512,1024]{1,0:T(8,128)(2,1)} %shard_map.359), channel_id=1, source_target_pairs={{0,16},{16,0},{1,17},{17,1},{2,18},{18,2},{3,19},{19,3},{4,20},{20... | collective-permute-start | bytes 3145736 | tf_op jit(solution)/shard_map/ppermute | solution.py:508
  171.3 46.1 %collective-permute-start.12 = (bf16[512,768]{1,0:T(8,128)(2,1)}, bf16[512,768]{1,0:T(8,128)(2,1)}, u32[]{:S(2)}, u32[]{:S(2)}) collective-permute-start(bf16[512,768]{1,0:T(8,128)(2,1)} %shard_map.358), channel_id=1, source_target_pairs={{0,16},{16,0},{1,17},{17,1},{2,18},{18,2},{3,19},{19,3},{4,20},{20... | collective-permute-start | bytes 2359304 | tf_op jit(solution)/shard_map/ppermute | solution.py:508
  238.8 124.9 %all-gather.17.cloned.1.call-start = ((), (), s32[]{:S(2)}) async-start(), calls=%async_computation.14 | async-start | bytes 1474560 | tf_op jit(solution)/shard_map/all_gather | solution.py:593
  292.1 119.7 %reduce-scatter.14.cloned.1.call-start = ((), (), s32[]{:S(2)}) async-start(), calls=%async_computation.17 | async-start | bytes 3932160 | tf_op jit(solution)/shard_map/reduce_scatter | solution.py:644
  337.2 114.0 %all-gather.21.cloned.1.call-start = ((), (), s32[]{:S(2)}) async-start(), calls=%async_computation.16 | async-start | bytes 1474560 | tf_op jit(solution)/shard_map/all_gather | solution.py:593
  419.2 72.4 %reduce-scatter.16.cloned.1.call-start = ((), (), s32[]{:S(2)}) async-start(), calls=%async_computation.18 | async-start | bytes 1474560 | tf_op jit(solution)/shard_map/reduce_scatter | solution.py:640
  457.7 68.1 %all-gather.23.cloned.1.call-start = ((), (), s32[]{:S(2)}) async-start(), calls=%async_computation.19 | async-start | bytes 1474560 | tf_op jit(solution)/shard_map/all_gather | solution.py:593
  495.8 79.5 %all-gather.25.cloned.1.call-start = ((), (), s32[]{:S(2)}) async-start(), calls=%async_computation.20 | async-start | bytes 1474560 | tf_op jit(solution)/shard_map/all_gather | solution.py:593
  545.0 71.8 %reduce-scatter.18.cloned.1.call-start = ((), (), s32[]{:S(2)}) async-start(), calls=%async_computation.21 | async-start | bytes 1474560 | tf_op jit(solution)/shard_map/reduce_scatter | solution.py:640
  588.4 96.4 %reduce-scatter.20.cloned.1.call-start = ((), (), s32[]{:S(2)}) async-start(), calls=%async_computation.22 | async-start | bytes 1474560 | tf_op jit(solution)/shard_map/reduce_scatter | solution.py:640
  647.4 99.6 %all-gather.27.cloned.1.call-start = ((), (), s32[]{:S(2)}) async-start(), calls=%async_computation.23 | async-start | bytes 1474560 | tf_op jit(solution)/shard_map/all_gather | solution.py:593
  706.3 76.1 %reduce-scatter.22.cloned.1.call-start = ((), (), s32[]{:S(2)}) async-start(), calls=%async_computation.24 | async-start | bytes 1474560 | tf_op jit(solution)/shard_map/reduce_scatter | solution.py:640
  753.8 98.0 %all-gather.29.cloned.1.call-start = ((), (), s32[]{:S(2)}) async-start(), calls=%async_computation.26 | async-start | bytes 3932160 | tf_op jit(solution)/shard_map/all_gather | solution.py:593
  756.4 126.9 %reduce-scatter.24.cloned.1.call-start = ((), (), s32[]{:S(2)}) async-start(), calls=%async_computation.25 | async-start | bytes 1474560 | tf_op jit(solution)/shard_map/reduce_scatter | solution.py:640
  818.0 157.4 %reduce-scatter.26.cloned.1.call-start = ((), (), s32[]{:S(2)}) async-start(), calls=%async_computation.27 | async-start | bytes 3932160 | tf_op jit(solution)/shard_map/reduce_scatter | solution.py:644
  828.8 120.8 %collective-permute-start.85 = (bf16[512,2048]{1,0:T(8,128)(2,1)}, bf16[512,2048]{1,0:T(8,128)(2,1)}, u32[]{:S(2)}, u32[]{:S(2)}) collective-permute-start(bf16[512,2048]{1,0:T(8,128)(2,1)} %fusion.16), channel_id=1, source_target_pairs={{0,4},{4,0},{8,12},{12,8},{1,5},{5,1},{9,13},{13,9},{2,6},{6,2},{1... | collective-permute-start | bytes 6291464 | tf_op jit(solution)/shard_map/ppermute | solution.py:508
  838.5 108.9 %collective-permute-start.87 = (bf16[512,1536]{1,0:T(8,128)(2,1)}, bf16[512,1536]{1,0:T(8,128)(2,1)S(1)}, u32[]{:S(2)}, u32[]{:S(2)}) collective-permute-start(bf16[512,1536]{1,0:T(8,128)(2,1)} %fusion.18), channel_id=1, source_target_pairs={{0,4},{4,0},{8,12},{12,8},{1,5},{5,1},{9,13},{13,9},{2,6},{6,2},{1... | collective-permute-start | bytes 4718600 | tf_op jit(solution)/shard_map/ppermute | solution.py:508
  869.7 215.8 %all-gather.31.cloned.1.call-start = ((), (), s32[]{:S(2)}) async-start(), calls=%async_computation.28 | async-start | bytes 3932160 | tf_op jit(solution)/shard_map/all_gather | solution.py:593
  924.8 45.7 %collective-permute-start.82 = (bf16[768,1536]{1,0:T(8,128)(2,1)}, bf16[768,1536]{1,0:T(8,128)(2,1)S(1)}, u32[]{:S(2)}, u32[]{:S(2)}) collective-permute-start(bf16[768,1536]{1,0:T(8,128)(2,1)} %slice.333), channel_id=1, source_target_pairs={{0,4},{4,0},{8,12},{12,8},{1,5},{5,1},{9,13},{13,9},{2,6},{6,2},{1... | collective-permute-start | bytes 7077896 | tf_op jit(solution)/shard_map/ppermute | solution.py:508
  950.1 58.5 %collective-permute-start.88 = (bf16[256,1536]{1,0:T(8,128)(2,1)}, bf16[256,1536]{1,0:T(8,128)(2,1)}, u32[]{:S(2)}, u32[]{:S(2)}) collective-permute-start(bf16[256,1536]{1,0:T(8,128)(2,1)} %slice.341), channel_id=1, source_target_pairs={{0,8},{4,12},{8,0},{12,4},{1,9},{5,13},{9,1},{13,5},{2,10},{6,14},... | collective-permute-start | bytes 2359304 | tf_op jit(solution)/shard_map/ppermute | solution.py:508
  954.4 50.9 %collective-permute-start.86 = (bf16[256,2048]{1,0:T(8,128)(2,1)}, bf16[256,2048]{1,0:T(8,128)(2,1)S(1)}, u32[]{:S(2)}, u32[]{:S(2)}) collective-permute-start(bf16[256,2048]{1,0:T(8,128)(2,1)} %slice.338), channel_id=1, source_target_pairs={{0,8},{4,12},{8,0},{12,4},{1,9},{5,13},{9,1},{13,5},{2,10},{6,14},... | collective-permute-start | bytes 3145736 | tf_op jit(solution)/shard_map/ppermute | solution.py:508
  973.9 44.2 %collective-permute-start.89 = (bf16[384,1536]{1,0:T(8,128)(2,1)}, bf16[384,1536]{1,0:T(8,128)(2,1)}, u32[]{:S(2)}, u32[]{:S(2)}) collective-permute-start(bf16[384,1536]{1,0:T(8,128)(2,1)} %slice.342), channel_id=1, source_target_pairs={{0,8},{4,12},{8,0},{12,4},{1,9},{5,13},{9,1},{13,5},{2,10},{6,14},... | collective-permute-start | bytes 3538952 | tf_op jit(solution)/shard_map/ppermute | solution.py:508
  1023.7 159.8 %reduce-scatter.28.cloned.1.call-start = ((), (), s32[]{:S(2)}) async-start(), calls=%async_computation.29 | async-start | bytes 3932160 | tf_op jit(solution)/shard_map/reduce_scatter | solution.py:644
  1036.1 49.4 %collective-permute-start.93 = (bf16[256,2048]{1,0:T(8,128)(2,1)}, bf16[256,2048]{1,0:T(8,128)(2,1)}, u32[]{:S(2)}, u32[]{:S(2)}) collective-permute-start(bf16[256,2048]{1,0:T(8,128)(2,1)} %broadcast_select_fusion.8), channel_id=1, source_target_pairs={{0,16},{16,0},{1,17},{17,1},{2,18},{18,2},{3,19},{19,3},{4,20},{20... | collective-permute-start | bytes 3145736 | tf_op jit(solution)/shard_map/ppermute | solution.py:508
  1104.2 173.5 %reduce-scatter.30.cloned.1.call-start = ((), (), s32[]{:S(2)}) async-start(), calls=%async_computation.30 | async-start | bytes 3276800 | tf_op jit(solution)/shard_map/reduce_scatter | solution.py:1106
  1185.9 121.4 %reduce-scatter.32.cloned.1.call-start = ((), (), s32[]{:S(2)}) async-start(), calls=%async_computation.31 | async-start | bytes 1474560 | tf_op jit(solution)/shard_map/reduce_scatter | solution.py:640
  1215.7 60.3 %collective-permute-start.113 = (bf16[384,1536]{1,0:T(8,128)(2,1)}, bf16[384,1536]{1,0:T(8,128)(2,1)}, u32[]{:S(2)}, u32[]{:S(2)}) collective-permute-start(bf16[384,1536]{1,0:T(8,128)(2,1)} %broadcast_select_fusion.6), channel_id=1, source_target_pairs={{0,16},{16,0},{1,17},{17,1},{2,18},{18,2},{3,19},{19,3},{4,20},{20... | collective-permute-start | bytes 3538952 | tf_op jit(solution)/shard_map/ppermute | solution.py:508
  (418 other events, 5760.6 us)
Sparse Core Ops, SparseCore 0:
  10.2 31.7 all-gather.32
  44.1 29.4 all-gather.12
  75.7 62.4 all-gather.14
  157.1 58.8 reduce-scatter.11
  238.9 75.4 all-gather.18
  316.4 29.0 all-gather.16
  347.8 64.0 reduce-scatter.13
  419.3 31.9 all-gather.20
  457.9 33.6 reduce-scatter.15
  495.9 29.8 all-gather.22
  545.1 30.1 all-gather.24
  588.5 28.2 reduce-scatter.17
  647.5 27.8 reduce-scatter.19
  706.4 40.6 all-gather.26
  753.9 28.4 reduce-scatter.21
  784.4 67.2 all-gather.28
  854.5 28.7 reduce-scatter.23
  885.4 69.8 reduce-scatter.25
  1023.8 61.2 all-gather.30
  1104.3 61.3 reduce-scatter.27
  1186.0 51.3 reduce-scatter.29
  1277.9 29.3 reduce-scatter.31
